TPU v7x, 256 devices: a whole 4x4x8 slice. The times are simulated.
256 devices in a mesh: aux: 8 (over z), pair: 32 (over x, y, core).
Axes of the slice: x: 4, y: 4, z: 8, core: 2. Of those that a mesh axis runs over, the one named last changes fastest.
Arguments:
- b_three: bfloat16 [16384, 4096], P('pair', 'aux'), may hold values from -0.09375 to 0.09375
- metric: bfloat16 [4096, 4096], P(None, 'aux'), may hold values from -1 to 2
- aux_map: int32 [256, 64], P('pair', 'aux'), may hold values 0 or 1
- domains: int32 [320, 4], replicated, may hold values from 0 to 255, as said below
- counts: int32 [320], P('pair'), may hold values from 1 to 4, as said below
Outputs:
- pair_integrals: float32 [320, 256, 256], P('pair', 'aux')
Inputs may be any that keep to these rules, and one draw needn't show every extreme that they name: `domains`: of the 40 slots of the pairs of one index of pair (pairs q * 10 to (q + 1) * 10 - 1), at most 2 name blocks held by one index of pair (blocks o * 8 to (o + 1) * 8 - 1), and exactly 2 for some such index in every draw. `counts`: slots at or past a pair's count are padding.
All inputs are finite; a program needn't handle non-finite values. No bound on the sum of `aux_map` on one device may be relied on, other than what follows from the above.
Results may differ from a plain program's by a relative error of at most 0.00079.
Values may be sent and summed in bfloat16 or wider, within the bound.
No kernel may reach another device: no remote copies, remote signals or barrier semaphores. Data moves between devices by JAX's collectives and lax.ppermute only.
A program may use at most 64 MiB of HBM per device.

v0:
```python
import jax
import jax.numpy as jnp
from jax import lax
from jax.sharding import PartitionSpec as P


def per_device(b_three, metric, aux_map, domains, counts):
    rows_dev, aux_dev = b_three.shape
    blocks_dev, aux_blocks = aux_map.shape
    width_cw = rows_dev // blocks_dev
    aux_width = aux_dev // aux_blocks
    keep_mask = aux_map.astype(jnp.bfloat16)
    masked = (
        b_three.reshape(blocks_dev, width_cw, aux_blocks, aux_width) * keep_mask[:, None, :, None]
    ).reshape(rows_dev, aux_dev)
    fitted = jnp.dot(
        lax.all_gather(masked, "aux", axis=1, tiled=True),
        metric,
        preferred_element_type=jnp.float32,
    ).astype(jnp.bfloat16)
    block_table = fitted.reshape(blocks_dev, width_cw * aux_dev)
    peer_count = lax.axis_size("pair")
    own_index = lax.axis_index("pair")
    pairs_dev = counts.shape[0]
    domain_max = domains.shape[1]
    slot_count = pairs_dev * domain_max
    all_domains = domains.reshape(peer_count, slot_count)
    own_domains = lax.dynamic_slice_in_dim(all_domains, own_index, 1, 0)[0]
    shard_piece = lax.all_gather(block_table, "pair", axis=0, tiled=True)
    block_ids = jnp.arange(shard_piece.shape[0], dtype=jnp.int32)
    onehot = (own_domains[:, None] == block_ids[None, :]).astype(jnp.bfloat16)
    chosen = jnp.dot(onehot, shard_piece, preferred_element_type=jnp.float32).astype(jnp.bfloat16)
    stacks = chosen.reshape(pairs_dev, domain_max * width_cw, aux_dev)
    partial_value = jnp.einsum("pax,pbx->pab", stacks, stacks, preferred_element_type=jnp.float32)
    slot_of = jnp.arange(domain_max * width_cw, dtype=jnp.int32) // width_cw
    live_rows = slot_of[None, :] < counts[:, None]
    partial_value = jnp.where(
        live_rows[:, :, None] & live_rows[:, None, :], partial_value, jnp.zeros_like(partial_value)
    )
    summed = lax.psum(partial_value, "aux")
    share_rows = summed.shape[1] // lax.axis_size("aux")
    return lax.dynamic_slice_in_dim(summed, lax.axis_index("aux") * share_rows, share_rows, 1)


def solution(mesh):
    return jax.shard_map(
        per_device,
        mesh=mesh,
        in_specs=(P("pair", "aux"), P(None, "aux"), P("pair", "aux"), P(), P("pair")),
        out_specs=P("pair", "aux", None),
        check_vma=False,
    )
```

profile of v0, /device:TPU:2, one launch (start us, length us, event | category | flops | bytes accessed | tf_op | source)
XLA Modules:
  0.0 261.1 jit_solution(16600572603146968970)
XLA Ops:
  6.5 0.0 all-gather.3.cloned.1.call-start
  6.5 0.7 convert_element_type.10
  7.3 0.2 mul.14
  7.5 0.6 mul.15
  8.1 0.9 mul.16
  9.1 0.0 all-gather.3.cloned.1.call-update
  9.1 0.0 copy-start.1
  9.1 0.0 copy-start.2
  9.1 0.0 all-gather.5.cloned.1.call-start
  9.2 57.9 %all-gather.3.cloned.1.call-done = bf16[512,4096]{1,0:T(8,128)(2,1)} async-done(((bf16[512,512]{1,0:T(8,128)(2,1)}), bf16[512,4096]{1,0:T(8,128)(2,1)}) %all-gather.3.cloned.1.call-update) | async-done | bytes 4194320 | tf_op jit(solution)/shard_map/all_gather | solution.py:17
  67.0 5.8 %convolution_convert_fusion.1 = bf16[512,512]{1,0:T(8,128)(2,1)S(1)} fusion(bf16[512,4096]{1,0:T(8,128)(2,1)} %all-gather.3.cloned.1.call-done, bf16[4096,512]{1,0:T(8,128)(2,1)} %param.6), kind=kOutput, calls=%fused_computation.2 | convolution fusion | flops 2147745792 | bytes 8912896 | tf_op jit(solution)/shard_map/dot_general | solution.py:16
  72.8 1.0 reshape.77
  73.9 0.0 all-gather.5.cloned.1.call-update
  73.9 0.0 all-reduce.2.cloned.1.call-start
  74.0 0.1 copy.6
  74.1 0.1 reshape.76
  74.3 0.1 broadcast_compare_fusion
  74.3 75.8 %all-gather.5.cloned.1.call-done = bf16[256,32768]{1,0:T(8,128)(2,1)} async-done(((bf16[8,32768]{1,0:T(8,128)(2,1)}), bf16[256,32768]{1,0:T(8,128)(2,1)}) %all-gather.5.cloned.1.call-update) | async-done | bytes 16777232 | tf_op jit(solution)/shard_map/all_gather | solution.py:29
  150.1 8.7 %convolution_convert_fusion = bf16[40,32768]{1,0:T(8,128)(2,1)S(1)} fusion(bf16[256,32768]{1,0:T(8,128)(2,1)} %all-gather.5.cloned.1.call-done, s32[40]{0:T(128)S(1)} %dynamic-slice_bitcast_fusion), kind=kOutput, calls=%fused_computation | convolution fusion | flops 672409600 | bytes 19398816 | tf_op jit(solution)/shard_map/dot_general | solution.py:32
  158.9 3.1 %reshape.78 = bf16[10,256,512]{2,1,0:T(8,128)(2,1)} reshape(bf16[40,32768]{1,0:T(8,128)(2,1)S(1)} %convolution_convert_fusion) | data formatting | bytes 5242880 | tf_op jit(solution)/shard_map/reshape | solution.py:33
  162.0 5.0 %and_select_fusion = f32[10,256,256]{2,1,0:T(8,128)} fusion(bf16[10,256,512]{2,1,0:T(8,128)(2,1)} %reshape.78, pred[10,256]{1,0:T(8,128)(4,1)S(1)} %broadcast_compare_fusion), kind=kOutput, calls=%fused_computation.1 | convolution fusion | flops 672399360 | bytes 5245440 | tf_op jit(solution)/shard_map/pax,pbx->pab/dot_general | solution.py:34
  167.0 0.0 all-reduce.2.cloned.1.call-update
  167.0 85.9 %all-reduce.2.cloned.1.call-done = f32[10,256,256]{2,1,0:T(8,128)} async-done(((f32[10,256,256]{2,1,0:T(8,128)}), f32[10,256,256]{2,1,0:T(8,128)}) %all-reduce.2.cloned.1.call-update) | async-done | bytes 2621456 | tf_op jit(solution)/shard_map/psum | solution.py:40
  252.9 1.7 constant_dynamic-slice_fusion
  (6 shorter events, 0.0 us)
Async XLA Ops:
  6.5 1.6 copy-start
  6.5 60.5 %all-gather.3.cloned.1.call-start = ((), (), s32[]{:S(2)}) async-start(), calls=%async_computation | async-start | bytes 4718592 | tf_op jit(solution)/shard_map/all_gather | solution.py:17
  9.1 64.9 %copy-start.1 = (s32[320,4]{0,1:T(4,128)S(1)}, s32[320,4]{0,1:T(4,128)}, u32[]{:S(2)}) copy-start(s32[320,4]{0,1:T(4,128)} %param.8) | copy-start | bytes 15364
  9.1 65.1 %copy-start.2 = (s32[10]{0:T(128)S(1)}, s32[10]{0:T(128)}, u32[]{:S(2)}) copy-start(s32[10]{0:T(128)} %param.9) | copy-start | bytes 124
  9.1 141.0 %all-gather.5.cloned.1.call-start = ((), (), s32[]{:S(2)}) async-start(), calls=%async_computation.1 | async-start | bytes 17301504 | tf_op jit(solution)/shard_map/all_gather | solution.py:29
  73.9 179.0 %all-reduce.2.cloned.1.call-start = ((), (), s32[]{:S(2)}) async-start(), calls=%async_computation.2 | async-start | bytes 5242880 | tf_op jit(solution)/shard_map/psum | solution.py:40
Sparse Core Ops, SparseCore 0:
  9.2 57.7 all-gather.2
  74.0 76.0 all-gather.4
  167.1 85.6 all-reduce.1
where the time goes:
time: 261 us
  waiting for transfers between devices  220 us (84%)
  matrix products  19.5 us (7%)
  between operations  13.2 us (5%)
  local copies, waits for them, and re-layouts  6.99 us (3%)
    psum x1, waiting for transfers between devices, per_device(): summed = lax.psum(partial_value, 'aux')  85.9 us
    all_gather x1, waiting for transfers between devices, per_device(): shard_piece = lax.all_gather(block_table, 'pair', axis=0, tiled=True)  75.8 us
    all_gather x1, waiting for transfers between devices, per_device(): lax.all_gather(masked, 'aux', axis=1, tiled=True)  57.9 us
    dot_general x1, matrix products, per_device(): jnp.dot(onehot, shard_piece, preferred_element_type=jnp.float32)  8.73 us
    dot_general x1, matrix products, per_device(): jnp.dot(lax.all_gather(masked, 'aux', axis=1, tiled=True), metric, prefer...  5.79 us
  transfers between devices with their start and end apart: 3, of which 3 were waited for; matrix products, arithmetic and copies ran while one was open for 0% of the time, Pallas kernels for 0%

commit v1 on v0

v1 whole, which is shorter than its diff:
```python
import functools

import jax
import jax.numpy as jnp
from jax import lax
from jax.experimental import pallas as pl
from jax.experimental.pallas import tpu as pltpu
from jax.sharding import PartitionSpec as P

VMEM_LIMIT = 48 * 1024 * 1024


def mask_kernel(map_ref, b_ref, out_ref):
    blocks_dev, aux_blocks = map_ref.shape
    rows_dev, aux_dev = b_ref.shape
    width = rows_dev // blocks_dev
    aux_width = aux_dev // aux_blocks
    spread = (
        lax.broadcasted_iota(jnp.int32, (aux_blocks, aux_dev), 1) // aux_width
        == lax.broadcasted_iota(jnp.int32, (aux_blocks, aux_dev), 0)
    ).astype(jnp.float32)
    keep = jnp.dot(map_ref[...].astype(jnp.float32), spread, preferred_element_type=jnp.float32)
    keep = keep.astype(jnp.bfloat16)
    for block in range(blocks_dev):
        rows = slice(block * width, (block + 1) * width)
        out_ref[rows, :] = b_ref[rows, :] * keep[block : block + 1, :]


def fit_kernel(blocks_dev, send_ref, m_ref, w_ref, out_ref, total, fitted, sems):
    step = pl.program_id(0)
    steps = pl.num_programs(0)
    slots = out_ref.shape[0]
    part = jnp.dot(m_ref[0], w_ref[...], preferred_element_type=jnp.float32)

    @pl.when(step == 0)
    def _():
        total[...] = part

    @pl.when(step > 0)
    def _():
        total[...] += part

    @pl.when(step == steps - 1)
    def _():
        fitted[...] = total[...].astype(jnp.bfloat16).reshape(fitted.shape)
        copies = [
            pltpu.make_async_copy(fitted.at[send_ref[slot]], out_ref.at[slot], sems.at[slot])
            for slot in range(slots)
        ]
        for copy in copies:
            copy.start()
        for copy in copies:
            copy.wait()


def gram_kernel(where_ref, counts_ref, s0, s1, s2, s3, out_ref):
    pair = pl.program_id(0)
    width = s0.shape[1]
    stack = jnp.concatenate([s0[0], s1[0], s2[0], s3[0]], axis=0)
    size = stack.shape[0]
    value = lax.dot_general(
        stack, stack, (((1,), (1,)), ((), ())), preferred_element_type=jnp.float32
    )
    live = counts_ref[pair] * width
    row = lax.broadcasted_iota(jnp.int32, (size, size), 0)
    column = lax.broadcasted_iota(jnp.int32, (size, size), 1)
    value = jnp.where(jnp.maximum(row, column) < live, value, 0.0)
    out_ref[...] = value.reshape(out_ref.shape)


def per_device(b_three, metric, aux_map, domains, counts):
    rows_dev, aux_dev = b_three.shape
    blocks_dev, _ = aux_map.shape
    width = rows_dev // blocks_dev
    n_pair = lax.axis_size("pair")
    n_aux = lax.axis_size("aux")
    own = lax.axis_index("pair")
    pairs_dev = counts.shape[0]
    domain_max = domains.shape[1]
    slots_dev = pairs_dev * domain_max
    cap = 2

    masked = pl.pallas_call(
        mask_kernel,
        out_shape=jax.ShapeDtypeStruct(b_three.shape, jnp.bfloat16),
        compiler_params=pltpu.CompilerParams(vmem_limit_bytes=VMEM_LIMIT),
        name="mask",
    )(aux_map, b_three)
    gathered = lax.all_gather(masked, "aux", axis=0)

    table = domains.reshape(n_pair, slots_dev)
    owner = table // blocks_dev
    same = owner[:, :, None] == owner[:, None, :]
    earlier = jnp.tril(jnp.ones((slots_dev, slots_dev), jnp.bool_), -1)
    rank = jnp.sum((same & earlier[None]).astype(jnp.int32), axis=2)
    local = table % blocks_dev
    hit = (owner == own)[:, None, :] & (rank[:, None, :] == jnp.arange(cap, dtype=jnp.int32)[None, :, None])
    send = jnp.sum(jnp.where(hit, local[:, None, :], 0), axis=2).reshape(n_pair * cap)
    here = jnp.arange(n_pair, dtype=jnp.int32)[:, None] == own
    where = jnp.sum(jnp.where(here, owner * cap + rank, 0), axis=0)

    slots = n_pair * cap
    picked = pl.pallas_call(
        functools.partial(fit_kernel, blocks_dev),
        grid_spec=pltpu.PrefetchScalarGridSpec(
            num_scalar_prefetch=1,
            grid=(n_aux,),
            in_specs=[
                pl.BlockSpec((1, rows_dev, aux_dev), lambda k, send: (k, 0, 0)),
                pl.BlockSpec((aux_dev, aux_dev), lambda k, send: (k, 0)),
            ],
            out_specs=pl.BlockSpec(memory_space=pl.ANY),
            scratch_shapes=[
                pltpu.VMEM((rows_dev, aux_dev), jnp.float32),
                pltpu.VMEM((blocks_dev, width, aux_dev), jnp.bfloat16),
                pltpu.SemaphoreType.DMA((slots,)),
            ],
        ),
        out_shape=jax.ShapeDtypeStruct((slots, width, aux_dev), jnp.bfloat16),
        compiler_params=pltpu.CompilerParams(vmem_limit_bytes=VMEM_LIMIT),
        name="fit",
    )(send, gathered, metric)

    arrived = lax.all_to_all(
        picked.reshape(n_pair, cap * width, aux_dev), "pair", split_axis=0, concat_axis=0, tiled=True
    ).reshape(slots, width, aux_dev)

    size = domain_max * width
    share = size // n_aux

    def slot_spec(index):
        return pl.BlockSpec(
            (1, width, aux_dev), lambda p, where, live: (where[p * domain_max + index], 0, 0)
        )

    partial_value = pl.pallas_call(
        gram_kernel,
        grid_spec=pltpu.PrefetchScalarGridSpec(
            num_scalar_prefetch=2,
            grid=(pairs_dev,),
            in_specs=[slot_spec(index) for index in range(domain_max)],
            out_specs=pl.BlockSpec((n_aux, 1, share, size), lambda p, where, live: (0, p, 0, 0)),
        ),
        out_shape=jax.ShapeDtypeStruct((n_aux, pairs_dev, share, size), jnp.float32),
        compiler_params=pltpu.CompilerParams(vmem_limit_bytes=VMEM_LIMIT),
        name="gram",
    )(where, counts, arrived, arrived, arrived, arrived)
    return lax.psum_scatter(partial_value, "aux", scatter_dimension=0, tiled=False)


def solution(mesh):
    return jax.shard_map(
        per_device,
        mesh=mesh,
        in_specs=(P("pair", "aux"), P(None, "aux"), P("pair", "aux"), P(), P("pair")),
        out_specs=P("pair", "aux", None),
        check_vma=False,
    )
```

time: 261 us -> 202 us (0.77)
  waiting for transfers between devices: 220 us -> 150 us
  Pallas kernels: 0 us -> 24 us
  matrix products: 19.5 us -> 0 us
  starting transfers between devices: 0.09 us -> 7.65 us
    psum x1 -> x0, waiting for transfers between devices: 85.9 us -> none  [per_device(): summed = lax.psum(partial_value, 'aux')]
    all_gather x2 -> x1, waiting for transfers between devices: 134 us -> 55.7 us  [per_device(): gathered = lax.all_gather(masked, 'aux', axis=0)]
    all_to_all x0 -> x1, waiting for transfers between devices: none -> 50.1 us  [per_device(): lax.all_to_all(picked.reshape(n_pair, cap * width, aux_dev), 'pair', spli...]
    reduce_scatter x0 -> x1, waiting for transfers between devices: none -> 44.5 us  [per_device(): lax.psum_scatter(partial_value, 'aux', scatter_dimension=0, tiled=False)]
    pallas_call x0 -> x3, Pallas kernels: none -> 24 us  [the longest x1 14.6 us: per_device(): pl.pallas_call(functools.partial(fit_kernel, blocks_dev), grid_spec=pltpu...]
    dot_general x3 -> x0, matrix products: 19.5 us -> none  [the longest x1 8.73 us: per_device(): jnp.dot(onehot, shard_piece, preferred_element_type=jnp.float32)]
    all_to_all x0 -> x1, starting transfers between devices: none -> 7.61 us  [per_device(): lax.all_to_all(picked.reshape(n_pair, cap * width, aux_dev), 'pair', spli...]
    unnamed x7 -> x9, local copies, waits for them, and re-layouts: 0.15 us -> 4.51 us
  transfers between devices with their start and end apart: 3 -> 3, of which waited for: 3 -> 3; matrix products, arithmetic and copies ran while one was open for 0% -> 1% of each run, Pallas kernels for 0% -> 0%
where the time goes in v1:
time: 202 us; the launch traced here: 201 us
  waiting for transfers between devices  150 us (74%)
  Pallas kernels  24 us (12%)
  between operations  13.5 us (7%)
  starting transfers between devices  7.65 us (4%)
  local copies, waits for them, and re-layouts  4.81 us (2%)
    all_gather x1, waiting for transfers between devices, per_device(): gathered = lax.all_gather(masked, 'aux', axis=0)  55.7 us
    all_to_all x1, waiting for transfers between devices, per_device(): lax.all_to_all(picked.reshape(n_pair, cap * width, aux_dev), 'pair', spli...  50.1 us
    reduce_scatter x1, waiting for transfers between devices, per_device(): lax.psum_scatter(partial_value, 'aux', scatter_dimension=0, tiled=False)  44.5 us
    pallas_call x1, Pallas kernels, per_device(): pl.pallas_call(functools.partial(fit_kernel, blocks_dev), grid_spec=pltpu...  14.6 us
    pallas_call x1, Pallas kernels, per_device(): pl.pallas_call(gram_kernel, grid_spec=pltpu.PrefetchScalarGridSpec(num_sc...  8.42 us
    all_to_all x1, starting transfers between devices, per_device(): lax.all_to_all(picked.reshape(n_pair, cap * width, aux_dev), 'pair', spli...  7.61 us
    unnamed x9, local copies, waits for them, and re-layouts  4.51 us
  transfers between devices with their start and end apart: 3, of which 3 were waited for; matrix products, arithmetic and copies ran while one was open for 1% of the time, Pallas kernels for 0%

profile of v1, /device:TPU:2, one launch (start us, length us, event | category | flops | bytes accessed | tf_op | source)
XLA Modules:
  0.0 201.4 jit_solution(3174168768630441595)
XLA Ops:
  6.5 0.0 all-gather.3.cloned.1.call-start
  6.5 1.0 copy-done.1
  7.6 0.7 copy-done.2
  8.3 1.0 mask.1
  9.2 0.0 all-gather.3.cloned.1.call-update
  9.3 0.8 copy.7
  10.1 0.1 reshape.118
  10.2 0.1 iota_compare_fusion.1
  10.3 0.8 convert_reduce_fusion
  11.1 0.1 select_reduce_fusion
  11.3 0.1 copy.8
  11.3 0.1 reshape.119.send_ref
  11.5 55.7 %all-gather.3.cloned.1.call-done = bf16[4096,512]{1,0:T(8,128)(2,1)} async-done(((bf16[512,512]{1,0:T(8,128)(2,1)}), bf16[4096,512]{1,0:T(8,128)(2,1)}) %all-gather.3.cloned.1.call-update) | async-done | bytes 4194320 | tf_op jit(solution)/shard_map/all_gather | solution.py:89
  67.2 14.6 %fit.1 = bf16[64,64,512]{2,1,0:T(8,128)(2,1)S(1)} custom-call(s32[64]{0:T(128)S(1)} %reshape.119.send_ref, bf16[8,512,512]{2,1,0:T(8,128)(2,1)} %bitcast.5, bf16[4096,512]{1,0:T(8,128)(2,1)} %w_ref.1), custom_call_target="tpu_custom_call" | custom-call | tf_op jit(solution)/shard_map/fit/pallas_call | solution.py:103
  81.8 0.0 copy-start
  81.8 2.0 copy-done
  83.7 7.6 %all-to-all-start = ((bf16[32,128,512]{2,1,0:T(8,128)(2,1)}), bf16[32,128,512]{2,1,0:T(8,128)(2,1)}, u32[]{:S(2)}, u32[]{:S(2)}) async-start(bf16[32,128,512]{2,1,0:T(8,128)(2,1)} %bitcast.4), calls=%async_computation | async-start | bytes 8388608 | tf_op jit(solution)/shard_map/all_to_all | solution.py:124
  91.3 0.0 reduce-scatter.2.cloned.1.call-start
  91.4 0.1 select_reduce_fusion.1.where_ref
  91.5 50.1 %all-to-all-done = bf16[32,128,512]{2,1,0:T(8,128)(2,1)} async-done(((bf16[32,128,512]{2,1,0:T(8,128)(2,1)}), bf16[32,128,512]{2,1,0:T(8,128)(2,1)}, u32[]{:S(2)}, u32[]{:S(2)}) %all-to-all-start) | async-done | bytes 4194336 | tf_op jit(solution)/shard_map/all_to_all | solution.py:124
  141.6 0.0 copy-done.3
  141.6 8.4 %gram.1 = f32[8,10,32,256]{3,2,1,0:T(8,128)} custom-call(s32[40]{0:T(128)S(1)} %select_reduce_fusion.1.where_ref, s32[10]{0:T(128)S(1)} %copy-done.3, bf16[64,64,512]{2,1,0:T(8,128)(2,1)} %bitcast.2.s0.s1.s2.s3, bf16[64,64,512]{2,1,0:T(8,128)(2,1)} %bitcast.2.s0.s1.s2.s3, bf16[64,64,512]{2,1,0:T(8,128)(2,1)} %bitcast.2.s0.s1.s2.s3, ...), custom_call_target="tpu_custom_call" | custom-call | tf_op jit(solution)/shard_map/gram/pallas_call | solution.py:136
  150.0 0.0 reduce-scatter.2.cloned.1.call-update
  150.0 44.5 %reduce-scatter.2.cloned.1.call-done = f32[1,10,32,256]{3,2,1,0:T(8,128)} async-done(((f32[8,10,32,256]{3,2,1,0:T(8,128)}), f32[1,10,32,256]{3,2,1,0:T(8,128)}) %reduce-scatter.2.cloned.1.call-update) | async-done | bytes 327696 | tf_op jit(solution)/shard_map/reduce_scatter | solution.py:148
  (7 shorter events, 0.0 us)
Async XLA Ops:
  6.5 60.6 %all-gather.3.cloned.1.call-start = ((), (), s32[]{:S(2)}) async-start(), calls=%async_computation.3 | async-start | bytes 4718592 | tf_op jit(solution)/shard_map/all_gather | solution.py:89
  6.5 1.0 copy-start.1
  7.6 0.7 copy-start.2
  81.8 2.0 copy-start
  83.7 57.9 %copy-start.3 = (s32[10]{0:T(128)S(1)}, s32[10]{0:T(128)}, u32[]{:S(2)}) copy-start(s32[10]{0:T(128)} %counts_ref.1) | copy-start | bytes 124
  83.7 57.9 %all-to-all-start = ((bf16[32,128,512]{2,1,0:T(8,128)(2,1)}), bf16[32,128,512]{2,1,0:T(8,128)(2,1)}, u32[]{:S(2)}, u32[]{:S(2)}) async-start(bf16[32,128,512]{2,1,0:T(8,128)(2,1)} %bitcast.4), calls=%async_computation | async-start | bytes 8388608 | tf_op jit(solution)/shard_map/all_to_all | solution.py:124
  91.3 103.2 %reduce-scatter.2.cloned.1.call-start = ((), (), s32[]{:S(2)}) async-start(), calls=%async_computation.2 | async-start | bytes 2949120 | tf_op jit(solution)/shard_map/reduce_scatter | solution.py:148
Sparse Core Ops, SparseCore 0:
  9.4 57.7 all-gather.2
  150.2 44.3 reduce-scatter.1

commit v2 on v1

v2 whole, which is shorter than its diff:
```python
import functools

import jax
import jax.numpy as jnp
from jax import lax
from jax.experimental import pallas as pl
from jax.experimental.pallas import tpu as pltpu
from jax.sharding import PartitionSpec as P

VMEM_LIMIT = 48 * 1024 * 1024
SIDE = 4
CAP = 2


def mask_kernel(map_ref, b_ref, out_ref):
    blocks_dev, aux_blocks = map_ref.shape
    rows_dev, aux_dev = b_ref.shape
    width = rows_dev // blocks_dev
    aux_width = aux_dev // aux_blocks
    spread = (
        lax.broadcasted_iota(jnp.int32, (aux_blocks, aux_dev), 1) // aux_width
        == lax.broadcasted_iota(jnp.int32, (aux_blocks, aux_dev), 0)
    ).astype(jnp.float32)
    keep = jnp.dot(map_ref[...].astype(jnp.float32), spread, preferred_element_type=jnp.float32)
    keep = keep.astype(jnp.bfloat16)
    for block in range(blocks_dev):
        rows = slice(block * width, (block + 1) * width)
        out_ref[rows, :] = b_ref[rows, :] * keep[block : block + 1, :]


def fit_kernel(m_ref, w_ref, out_ref, total):
    step = pl.program_id(0)
    part = jnp.dot(m_ref[0], w_ref[...], preferred_element_type=jnp.float32)

    @pl.when(step == 0)
    def _():
        total[...] = part

    @pl.when(step > 0)
    def _():
        total[...] += part

    @pl.when(step == pl.num_programs(0) - 1)
    def _():
        out_ref[...] = total[...].astype(jnp.bfloat16).reshape(out_ref.shape)


def pick_kernel(send_ref, *refs):
    sources, outs = refs[:SIDE], refs[SIDE : SIDE + 2 * SIDE]
    held, load_sems, store_sems = refs[SIDE + 2 * SIDE :]
    blocks_dev = sources[0].shape[0]
    slots = outs[0].shape[0]
    loads = [
        pltpu.make_async_copy(source, held.at[pl.ds(index * blocks_dev, blocks_dev)], load_sems.at[index])
        for index, source in enumerate(sources)
    ]
    for load in loads:
        load.start()
    for load in loads:
        load.wait()
    stores = [
        pltpu.make_async_copy(
            held.at[send_ref[message * slots + slot]], out.at[slot], store_sems.at[message * slots + slot]
        )
        for message, out in enumerate(outs)
        for slot in range(slots)
    ]
    for store in stores:
        store.start()
    for store in stores:
        store.wait()


def gram_kernel(domain_max, where_ref, counts_ref, *refs):
    messages = 2 * SIDE
    arrived, out_ref = refs[:messages], refs[messages]
    held, values, load_sems, store_sems = refs[messages + 1 :]
    slots = arrived[0].shape[0]
    pairs_dev, n_aux, share, size = values.shape
    width = held.shape[1]
    loads = [
        pltpu.make_async_copy(source, held.at[pl.ds(index * slots, slots)], load_sems.at[index])
        for index, source in enumerate(arrived)
    ]
    for load in loads:
        load.start()
    for load in loads:
        load.wait()
    row = lax.broadcasted_iota(jnp.int32, (size, size), 0)
    column = lax.broadcasted_iota(jnp.int32, (size, size), 1)
    furthest = jnp.maximum(row, column)
    stores = []
    for pair in range(pairs_dev):
        stack = jnp.concatenate(
            [held[where_ref[pair * domain_max + index]] for index in range(domain_max)], axis=0
        )
        value = lax.dot_general(
            stack, stack, (((1,), (1,)), ((), ())), preferred_element_type=jnp.float32
        )
        value = jnp.where(furthest < counts_ref[pair] * width, value, 0.0)
        values[pair] = value.reshape(n_aux, share, size)
        store = pltpu.make_async_copy(values.at[pair], out_ref.at[:, pair], store_sems.at[pair])
        store.start()
        stores.append(store)
    for store in stores:
        store.wait()


def device_of(x, y, core):
    return (x % SIDE) * 2 * SIDE + (y % SIDE) * 2 + core % 2


def gather_perm(hop):
    return [
        (device_of(x, y, core), device_of(x + hop, y, 0) if core == 0 else device_of(x, y + hop, 1))
        for x in range(SIDE)
        for y in range(SIDE)
        for core in range(2)
    ]


def spread_perm(hop, flip):
    return [
        (
            device_of(x, y, core),
            device_of(x, y + hop, flip) if core == 0 else device_of(x + hop, y, 1 - flip),
        )
        for x in range(SIDE)
        for y in range(SIDE)
        for core in range(2)
    ]


def plan(domains, own, pairs_dev, blocks_dev, n_pair):
    table = domains.reshape(n_pair, pairs_dev * domains.shape[1])
    slots_dev = table.shape[1]
    x, y, core = own // (2 * SIDE), (own // 2) % SIDE, own % 2
    first = core == 0
    hops = jnp.arange(SIDE, dtype=jnp.int32)
    flips = jnp.arange(2, dtype=jnp.int32)
    source = jnp.where(first, device_of(x - hops, y, 0), device_of(x, y - hops, 1))
    target = jnp.where(
        first,
        device_of(x, y + hops[:, None], flips[None, :]),
        device_of(x + hops[:, None], y, 1 - flips[None, :]),
    ).reshape(2 * SIDE)

    owner, local = table // blocks_dev, table % blocks_dev
    earlier = jnp.tril(jnp.ones((slots_dev, slots_dev), jnp.bool_), -1)
    rank = jnp.sum(((owner[:, :, None] == owner[:, None, :]) & earlier[None]).astype(jnp.int32), axis=2)

    packed = (owner * CAP + rank) * blocks_dev + local
    chosen = jnp.concatenate([target, own[None]])[:, None] == jnp.arange(n_pair, dtype=jnp.int32)[None, :]
    rows = jnp.sum(jnp.where(chosen[:, :, None], packed[None], 0), axis=1)
    key = rows // blocks_dev
    wanted = (source[:, None] * CAP + jnp.arange(CAP, dtype=jnp.int32)[None, :]).reshape(SIDE * CAP)
    from_hop = (jnp.arange(SIDE * CAP, dtype=jnp.int32) // CAP) * blocks_dev
    hit = key[:-1, None, :] == wanted[None, :, None]
    send = from_hop[None, :] + jnp.sum(jnp.where(hit, rows[:-1, None, :] % blocks_dev, 0), axis=2)

    named, place = key[-1] // CAP, key[-1] % CAP
    back_x, back_y = (x - named // (2 * SIDE)) % SIDE, (y - (named // 2) % SIDE) % SIDE
    sent_first = named % 2 == 0
    gathered = jnp.where(sent_first, back_x, back_y)
    spread = jnp.where(sent_first, back_y, back_x)
    flip = jnp.where(sent_first, core, 1 - core)
    where = ((spread * 2 + flip) * SIDE + gathered) * CAP + place
    return send.reshape(-1), where


def per_device(b_three, metric, aux_map, domains, counts):
    rows_dev, aux_dev = b_three.shape
    blocks_dev, _ = aux_map.shape
    width = rows_dev // blocks_dev
    n_pair = lax.axis_size("pair")
    n_aux = lax.axis_size("aux")
    own = lax.axis_index("pair")
    pairs_dev = counts.shape[0]
    domain_max = domains.shape[1]
    params = pltpu.CompilerParams(vmem_limit_bytes=VMEM_LIMIT)
    anywhere = pl.BlockSpec(memory_space=pl.ANY)

    masked = pl.pallas_call(
        mask_kernel,
        out_shape=jax.ShapeDtypeStruct(b_three.shape, jnp.bfloat16),
        compiler_params=params,
        name="mask",
    )(aux_map, b_three)
    gathered = lax.all_gather(masked, "aux", axis=0)
    send, where = plan(domains, own, pairs_dev, blocks_dev, n_pair)

    block_shape = (width, aux_dev)
    fitted = pl.pallas_call(
        fit_kernel,
        grid=(n_aux,),
        in_specs=[
            pl.BlockSpec((1, rows_dev, aux_dev), lambda k: (k, 0, 0)),
            pl.BlockSpec((aux_dev, aux_dev), lambda k: (k, 0)),
        ],
        out_specs=pl.BlockSpec((blocks_dev, *block_shape), lambda k: (0, 0, 0)),
        scratch_shapes=[pltpu.VMEM((rows_dev, aux_dev), jnp.float32)],
        out_shape=jax.ShapeDtypeStruct((blocks_dev, *block_shape), jnp.bfloat16),
        compiler_params=params,
        name="fit",
    )(gathered, metric)

    sources = {0: fitted}
    for hop in (1, 3, 2):
        sources[hop] = lax.ppermute(fitted, "pair", gather_perm(hop))

    messages, slots = 2 * SIDE, SIDE * CAP
    picked = pl.pallas_call(
        pick_kernel,
        grid_spec=pltpu.PrefetchScalarGridSpec(
            num_scalar_prefetch=1,
            grid=(),
            in_specs=[anywhere] * SIDE,
            out_specs=[anywhere] * messages,
            scratch_shapes=[
                pltpu.VMEM((SIDE * blocks_dev, *block_shape), jnp.bfloat16),
                pltpu.SemaphoreType.DMA((SIDE,)),
                pltpu.SemaphoreType.DMA((messages * slots,)),
            ],
        ),
        out_shape=[jax.ShapeDtypeStruct((slots, *block_shape), jnp.bfloat16)] * messages,
        compiler_params=params,
        name="pick",
    )(send, *[sources[hop] for hop in range(SIDE)])

    arrived = {0: picked[0]}
    for hop, flip in ((1, 0), (3, 0), (1, 1), (3, 1), (2, 0), (2, 1), (0, 1)):
        message = hop * 2 + flip
        arrived[message] = lax.ppermute(picked[message], "pair", spread_perm(hop, flip))

    size = domain_max * width
    share = size // n_aux
    partial_value = pl.pallas_call(
        functools.partial(gram_kernel, domain_max),
        grid_spec=pltpu.PrefetchScalarGridSpec(
            num_scalar_prefetch=2,
            grid=(),
            in_specs=[anywhere] * messages,
            out_specs=anywhere,
            scratch_shapes=[
                pltpu.VMEM((messages * slots, *block_shape), jnp.bfloat16),
                pltpu.VMEM((pairs_dev, n_aux, share, size), jnp.float32),
                pltpu.SemaphoreType.DMA((messages,)),
                pltpu.SemaphoreType.DMA((pairs_dev,)),
            ],
        ),
        out_shape=jax.ShapeDtypeStruct((n_aux, pairs_dev, share, size), jnp.float32),
        compiler_params=params,
        name="gram",
    )(where, counts, *[arrived[message] for message in range(messages)])
    return lax.psum_scatter(partial_value, "aux", scatter_dimension=0, tiled=False)


def solution(mesh):
    return jax.shard_map(
        per_device,
        mesh=mesh,
        in_specs=(P("pair", "aux"), P(None, "aux"), P("pair", "aux"), P(), P("pair")),
        out_specs=P("pair", "aux", None),
        check_vma=False,
    )
```

time: 202 us -> 184 us (0.911)
  waiting for transfers between devices: 150 us -> 129 us
  starting transfers between devices: 7.65 us -> 15.9 us
  Pallas kernels: 24 us -> 17.9 us
    all_to_all x1 -> x0, waiting for transfers between devices: 50.1 us -> none  [per_device(): lax.all_to_all(picked.reshape(n_pair, cap * width, aux_dev), 'pair', spli...]
    ppermute x0 -> x10, waiting for transfers between devices: none -> 30.8 us  [the longest x7 19 us: per_device(): lax.ppermute(picked[message], 'pair', spread_perm(hop, flip))]
    ppermute x0 -> x10, starting transfers between devices: none -> 15.9 us  [the longest x7 11.1 us: per_device(): lax.ppermute(picked[message], 'pair', spread_perm(hop, flip))]
    all_to_all x1 -> x0, starting transfers between devices: 7.61 us -> none  [per_device(): lax.all_to_all(picked.reshape(n_pair, cap * width, aux_dev), 'pair', spli...]
    pallas_call x2 -> x3, Pallas kernels: 23 us -> 17 us  [the longest x1 7.03 us: per_device(): pl.pallas_call(fit_kernel, grid=(n_aux,), in_specs=[pl.BlockSpec((1, rows...]
    unnamed x9 -> x11, local copies, waits for them, and re-layouts: 4.51 us -> 4.75 us
  transfers between devices with their start and end apart: 3 -> 12, of which waited for: 3 -> 10; matrix products, arithmetic and copies ran while one was open for 1% -> 2% of each run, Pallas kernels for 0% -> 0%
where the time goes in v2:
time: 184 us; the launch traced here: 183 us
  waiting for transfers between devices  129 us (70%)
  Pallas kernels  17.9 us (10%)
  starting transfers between devices  15.9 us (9%)
  between operations  13.6 us (7%)
  local copies, waits for them, and re-layouts  5.11 us (3%)
    all_gather x1, waiting for transfers between devices, per_device(): gathered = lax.all_gather(masked, 'aux', axis=0)  55.2 us
    reduce_scatter x1, waiting for transfers between devices, per_device(): lax.psum_scatter(partial_value, 'aux', scatter_dimension=0, tiled=False)  43 us
    ppermute x7, waiting for transfers between devices, per_device(): lax.ppermute(picked[message], 'pair', spread_perm(hop, flip))  19 us
    ppermute x3, waiting for transfers between devices, per_device(): sources[hop] = lax.ppermute(fitted, 'pair', gather_perm(hop))  11.8 us
    ppermute x7, starting transfers between devices, per_device(): lax.ppermute(picked[message], 'pair', spread_perm(hop, flip))  11.1 us
    pallas_call x1, Pallas kernels, per_device(): pl.pallas_call(fit_kernel, grid=(n_aux,), in_specs=[pl.BlockSpec((1, rows...  7.03 us
    pallas_call x1, Pallas kernels, per_device(): pl.pallas_call(pick_kernel, grid_spec=pltpu.PrefetchScalarGridSpec(num_sc...  5.97 us
    ppermute x3, starting transfers between devices, per_device(): sources[hop] = lax.ppermute(fitted, 'pair', gather_perm(hop))  4.79 us
  transfers between devices with their start and end apart: 12, of which 10 were waited for; matrix products, arithmetic and copies ran while one was open for 2% of the time, Pallas kernels for 0%

profile of v2, /device:TPU:2, one launch (start us, length us, event | category | flops | bytes accessed | tf_op | source)
XLA Modules:
  0.0 183.4 jit_solution(6833474644458808611)
XLA Ops:
  6.5 1.0 copy-done.1
  8.3 1.0 mask.1
  12.0 55.2 %all-gather.3.cloned.1.call-done = bf16[4096,512]{1,0:T(8,128)(2,1)} async-done(((bf16[512,512]{1,0:T(8,128)(2,1)}), bf16[4096,512]{1,0:T(8,128)(2,1)}) %all-gather.3.cloned.1.call-update) | async-done | bytes 4194320 | tf_op jit(solution)/shard_map/all_gather | solution.py:189
  67.2 2.2 %copy-done = bf16[4096,512]{1,0:T(8,128)(2,1)S(1)} copy-done((bf16[4096,512]{1,0:T(8,128)(2,1)S(1)}, bf16[4096,512]{1,0:T(8,128)(2,1)}, u32[]{:S(2)}) %copy-start) | copy-done | bytes 4194328
  69.4 7.0 %fit.1.refs_0_ = bf16[8,64,512]{2,1,0:T(8,128)(2,1)S(1)} custom-call(bf16[8,512,512]{2,1,0:T(8,128)(2,1)S(1)} %bitcast.7, bf16[4096,512]{1,0:T(8,128)(2,1)} %w_ref.1), custom_call_target="tpu_custom_call" | custom-call | tf_op jit(solution)/shard_map/fit/pallas_call | solution.py:193
  77.0 2.4 %collective-permute-start.1 = (bf16[8,64,512]{2,1,0:T(8,128)(2,1)S(1)}, bf16[8,64,512]{2,1,0:T(8,128)(2,1)S(1)}, u32[]{:S(2)}, u32[]{:S(2)}) collective-permute-start(bf16[8,64,512]{2,1,0:T(8,128)(2,1)S(1)} %fit.1.refs_0_), channel_id=1, source_target_pairs={{0,16},{1,5},{2,18},{3,7},{4,20},{5,1},{6,22},{7,3},{8,24},{9,13},... | collective-permute-start | bytes 1572872 | tf_op jit(solution)/shard_map/ppermute | solution.py:209
  79.4 1.8 collective-permute-start
  81.6 4.1 %collective-permute-done.2.refs_3_ = bf16[8,64,512]{2,1,0:T(8,128)(2,1)S(1)} collective-permute-done((bf16[8,64,512]{2,1,0:T(8,128)(2,1)S(1)}, bf16[8,64,512]{2,1,0:T(8,128)(2,1)S(1)}, u32[]{:S(2)}, u32[]{:S(2)}) %collective-permute-start.2) | collective-permute-done | bytes 524320 | tf_op jit(solution)/shard_map/ppermute | solution.py:209
  85.7 6.5 %collective-permute-done.1.refs_2_ = bf16[8,64,512]{2,1,0:T(8,128)(2,1)S(1)} collective-permute-done((bf16[8,64,512]{2,1,0:T(8,128)(2,1)S(1)}, bf16[8,64,512]{2,1,0:T(8,128)(2,1)S(1)}, u32[]{:S(2)}, u32[]{:S(2)}) %collective-permute-start.1) | collective-permute-done | bytes 524320 | tf_op jit(solution)/shard_map/ppermute | solution.py:209
  92.2 1.2 collective-permute-done.refs_1_
  93.4 6.0 %pick.1 = (bf16[8,64,512]{2,1,0:T(8,128)(2,1)S(1)}, bf16[8,64,512]{2,1,0:T(8,128)(2,1)S(1)}, bf16[8,64,512]{2,1,0:T(8,128)(2,1)S(1)}, bf16[8,64,512]{2,1,0:T(8,1...) custom-call(s32[64]{0:T(128)S(1)} %add.346.send_ref, ...), custom_call_target="tpu_custom_call" | custom-call | tf_op jit(solution)/shard_map/pick/pallas_call | solution.py:212
  100.0 1.0 collective-permute-start.4
  101.0 1.2 collective-permute-start.5
  102.2 2.7 %collective-permute-start.6 = (bf16[8,64,512]{2,1,0:T(8,128)(2,1)}, bf16[8,64,512]{2,1,0:T(8,128)(2,1)S(1)}, u32[]{:S(2)}, u32[]{:S(2)}) collective-permute-start(bf16[8,64,512]{2,1,0:T(8,128)(2,1)} %get-tuple-element.17), channel_id=1, source_target_pairs={{0,4},{1,17},{2,6},{3,19},{4,0},{5,21},{6,2},{7,23},{8,12},{9,25},... | collective-permute-start | bytes 1572872 | tf_op jit(solution)/shard_map/ppermute | solution.py:233
  104.9 3.0 %collective-permute-start.7 = (bf16[8,64,512]{2,1,0:T(8,128)(2,1)}, bf16[8,64,512]{2,1,0:T(8,128)(2,1)S(1)}, u32[]{:S(2)}, u32[]{:S(2)}) collective-permute-start(bf16[8,64,512]{2,1,0:T(8,128)(2,1)} %get-tuple-element.18), channel_id=1, source_target_pairs={{0,5},{1,16},{2,7},{3,18},{4,1},{5,20},{6,3},{7,22},{8,13},{9,24},... | collective-permute-start | bytes 1572872 | tf_op jit(solution)/shard_map/ppermute | solution.py:233
  107.9 1.4 collective-permute-start.8
  109.3 1.0 collective-permute-done.4.refs_2_
  110.4 1.1 collective-permute-start.9
  111.6 3.1 %collective-permute-done.5.refs_3_ = bf16[8,64,512]{2,1,0:T(8,128)(2,1)S(1)} collective-permute-done((bf16[8,64,512]{2,1,0:T(8,128)(2,1)}, bf16[8,64,512]{2,1,0:T(8,128)(2,1)S(1)}, u32[]{:S(2)}, u32[]{:S(2)}) %collective-permute-start.5) | collective-permute-done | bytes 524320 | tf_op jit(solution)/shard_map/ppermute | solution.py:233
  114.7 7.4 %collective-permute-done.6.refs_4_ = bf16[8,64,512]{2,1,0:T(8,128)(2,1)S(1)} collective-permute-done((bf16[8,64,512]{2,1,0:T(8,128)(2,1)}, bf16[8,64,512]{2,1,0:T(8,128)(2,1)S(1)}, u32[]{:S(2)}, u32[]{:S(2)}) %collective-permute-start.6) | collective-permute-done | bytes 524320 | tf_op jit(solution)/shard_map/ppermute | solution.py:233
  122.1 2.5 %collective-permute-done.7.refs_5_ = bf16[8,64,512]{2,1,0:T(8,128)(2,1)S(1)} collective-permute-done((bf16[8,64,512]{2,1,0:T(8,128)(2,1)}, bf16[8,64,512]{2,1,0:T(8,128)(2,1)S(1)}, u32[]{:S(2)}, u32[]{:S(2)}) %collective-permute-start.7) | collective-permute-done | bytes 524320 | tf_op jit(solution)/shard_map/ppermute | solution.py:233
  124.7 4.8 %collective-permute-done.9.refs_7_ = bf16[8,64,512]{2,1,0:T(8,128)(2,1)} collective-permute-done((bf16[8,64,512]{2,1,0:T(8,128)(2,1)}, bf16[8,64,512]{2,1,0:T(8,128)(2,1)}, u32[]{:S(2)}, u32[]{:S(2)}) %collective-permute-start.9) | collective-permute-done | bytes 524320 | tf_op jit(solution)/shard_map/ppermute | solution.py:233
  129.5 4.0 %gram.1 = f32[8,10,32,256]{3,2,1,0:T(8,128)} custom-call(s32[40]{0:T(128)S(1)} %fusion.6.where_ref, s32[10]{0:T(128)S(1)} %copy-done.3, bf16[8,64,512]{2,1,0:T(8,128)(2,1)S(1)} %get-tuple-element.13.refs_0_, bf16[8,64,512]{2,1,0:T(8,128)(2,1)S(1)} %collective-permute-done.3.refs_1_, bf16[8,64,512]{2,1,0:T(8,128)(2,1)S(1)} %collective-permute-done.4.refs_2_, ...), custom_call_target="tpu_custom_call" | custom-call | tf_op jit(solution)/shard_map/gram/pallas_call | solution.py:237
  133.5 43.0 %reduce-scatter.2.cloned.1.call-done = f32[1,10,32,256]{3,2,1,0:T(8,128)} async-done(((f32[8,10,32,256]{3,2,1,0:T(8,128)}), f32[1,10,32,256]{3,2,1,0:T(8,128)}) %reduce-scatter.2.cloned.1.call-update) | async-done | bytes 327696 | tf_op jit(solution)/shard_map/reduce_scatter | solution.py:255
  (41 shorter events, 4.9 us)
Async XLA Ops:
  6.5 60.6 %all-gather.3.cloned.1.call-start = ((), (), s32[]{:S(2)}) async-start(), calls=%async_computation.2 | async-start | bytes 4718592 | tf_op jit(solution)/shard_map/all_gather | solution.py:189
  6.5 1.0 copy-start.1
  7.6 0.7 copy-start.2
  9.2 167.3 %reduce-scatter.2.cloned.1.call-start = ((), (), s32[]{:S(2)}) async-start(), calls=%async_computation.1 | async-start | bytes 2949120 | tf_op jit(solution)/shard_map/reduce_scatter | solution.py:255
  67.2 2.2 %copy-start = (bf16[4096,512]{1,0:T(8,128)(2,1)S(1)}, bf16[4096,512]{1,0:T(8,128)(2,1)}, u32[]{:S(2)}) copy-start(bf16[4096,512]{1,0:T(8,128)(2,1)} %all-gather.3.cloned.1.call-done) | copy-start | bytes 12582916
  69.4 60.1 %copy-start.3 = (s32[10]{0:T(128)S(1)}, s32[10]{0:T(128)}, u32[]{:S(2)}) copy-start(s32[10]{0:T(128)} %counts_ref.1) | copy-start | bytes 124
  76.4 9.3 %collective-permute-start.2 = (bf16[8,64,512]{2,1,0:T(8,128)(2,1)S(1)}, bf16[8,64,512]{2,1,0:T(8,128)(2,1)S(1)}, u32[]{:S(2)}, u32[]{:S(2)}) collective-permute-start(bf16[8,64,512]{2,1,0:T(8,128)(2,1)S(1)} %fit.1.refs_0_), channel_id=1, source_target_pairs={{0,24},{1,7},{2,26},{3,1},{4,28},{5,3},{6,30},{7,5},{8,0},{9,15},{... | collective-permute-start | bytes 1572872 | tf_op jit(solution)/shard_map/ppermute | solution.py:209
  77.0 15.1 %collective-permute-start.1 = (bf16[8,64,512]{2,1,0:T(8,128)(2,1)S(1)}, bf16[8,64,512]{2,1,0:T(8,128)(2,1)S(1)}, u32[]{:S(2)}, u32[]{:S(2)}) collective-permute-start(bf16[8,64,512]{2,1,0:T(8,128)(2,1)S(1)} %fit.1.refs_0_), channel_id=1, source_target_pairs={{0,16},{1,5},{2,18},{3,7},{4,20},{5,1},{6,22},{7,3},{8,24},{9,13},... | collective-permute-start | bytes 1572872 | tf_op jit(solution)/shard_map/ppermute | solution.py:209
  79.4 14.0 %collective-permute-start = (bf16[8,64,512]{2,1,0:T(8,128)(2,1)S(1)}, bf16[8,64,512]{2,1,0:T(8,128)(2,1)S(1)}, u32[]{:S(2)}, u32[]{:S(2)}) collective-permute-start(bf16[8,64,512]{2,1,0:T(8,128)(2,1)S(1)} %fit.1.refs_0_), channel_id=1, source_target_pairs={{0,8},{1,3},{2,10},{3,5},{4,12},{5,7},{6,14},{7,1},{8,16},{9,11},{... | collective-permute-start | bytes 1572872 | tf_op jit(solution)/shard_map/ppermute | solution.py:209
  85.7 7.7 %copy-start.4 = (bf16[8,64,512]{2,1,0:T(8,128)(2,1)}, bf16[8,64,512]{2,1,0:T(8,128)(2,1)S(1)}, u32[]{:S(2)}) copy-start(bf16[8,64,512]{2,1,0:T(8,128)(2,1)S(1)} %collective-permute-done.2.refs_3_) | copy-start | bytes 1572868
  99.4 8.5 %collective-permute-start.3 = (bf16[8,64,512]{2,1,0:T(8,128)(2,1)S(1)}, bf16[8,64,512]{2,1,0:T(8,128)(2,1)S(1)}, u32[]{:S(2)}, u32[]{:S(2)}) collective-permute-start(bf16[8,64,512]{2,1,0:T(8,128)(2,1)S(1)} %get-tuple-element.14), channel_id=1, source_target_pairs={{0,1},{1,0},{2,3},{3,2},{4,5},{5,4},{6,7},{7,6},{8,9},{9,8},{10,11... | collective-permute-start | bytes 1572872 | tf_op jit(solution)/shard_map/ppermute | solution.py:233
  100.0 10.4 %collective-permute-start.4 = (bf16[8,64,512]{2,1,0:T(8,128)(2,1)S(1)}, bf16[8,64,512]{2,1,0:T(8,128)(2,1)S(1)}, u32[]{:S(2)}, u32[]{:S(2)}) collective-permute-start(bf16[8,64,512]{2,1,0:T(8,128)(2,1)S(1)} %get-tuple-element.15), channel_id=1, source_target_pairs={{0,2},{1,9},{2,4},{3,11},{4,6},{5,13},{6,0},{7,15},{8,10},{9,17},{... | collective-permute-start | bytes 1572872 | tf_op jit(solution)/shard_map/ppermute | solution.py:233
  101.0 13.7 %collective-permute-start.5 = (bf16[8,64,512]{2,1,0:T(8,128)(2,1)}, bf16[8,64,512]{2,1,0:T(8,128)(2,1)S(1)}, u32[]{:S(2)}, u32[]{:S(2)}) collective-permute-start(bf16[8,64,512]{2,1,0:T(8,128)(2,1)} %get-tuple-element.16), channel_id=1, source_target_pairs={{0,3},{1,8},{2,5},{3,10},{4,7},{5,12},{6,1},{7,14},{8,11},{9,16},{... | collective-permute-start | bytes 1572872 | tf_op jit(solution)/shard_map/ppermute | solution.py:233
  102.2 19.9 %collective-permute-start.6 = (bf16[8,64,512]{2,1,0:T(8,128)(2,1)}, bf16[8,64,512]{2,1,0:T(8,128)(2,1)S(1)}, u32[]{:S(2)}, u32[]{:S(2)}) collective-permute-start(bf16[8,64,512]{2,1,0:T(8,128)(2,1)} %get-tuple-element.17), channel_id=1, source_target_pairs={{0,4},{1,17},{2,6},{3,19},{4,0},{5,21},{6,2},{7,23},{8,12},{9,25},... | collective-permute-start | bytes 1572872 | tf_op jit(solution)/shard_map/ppermute | solution.py:233
  104.9 19.8 %collective-permute-start.7 = (bf16[8,64,512]{2,1,0:T(8,128)(2,1)}, bf16[8,64,512]{2,1,0:T(8,128)(2,1)S(1)}, u32[]{:S(2)}, u32[]{:S(2)}) collective-permute-start(bf16[8,64,512]{2,1,0:T(8,128)(2,1)} %get-tuple-element.18), channel_id=1, source_target_pairs={{0,5},{1,16},{2,7},{3,18},{4,1},{5,20},{6,3},{7,22},{8,13},{9,24},... | collective-permute-start | bytes 1572872 | tf_op jit(solution)/shard_map/ppermute | solution.py:233
  107.9 16.8 %collective-permute-start.8 = (bf16[8,64,512]{2,1,0:T(8,128)(2,1)}, bf16[8,64,512]{2,1,0:T(8,128)(2,1)}, u32[]{:S(2)}, u32[]{:S(2)}) collective-permute-start(bf16[8,64,512]{2,1,0:T(8,128)(2,1)} %get-tuple-element.19), channel_id=1, source_target_pairs={{0,6},{1,25},{2,0},{3,27},{4,2},{5,29},{6,4},{7,31},{8,14},{9,1},{... | collective-permute-start | bytes 1572872 | tf_op jit(solution)/shard_map/ppermute | solution.py:233
  110.4 19.1 %collective-permute-start.9 = (bf16[8,64,512]{2,1,0:T(8,128)(2,1)}, bf16[8,64,512]{2,1,0:T(8,128)(2,1)}, u32[]{:S(2)}, u32[]{:S(2)}) collective-permute-start(bf16[8,64,512]{2,1,0:T(8,128)(2,1)} %get-tuple-element.20), channel_id=1, source_target_pairs={{0,7},{1,24},{2,1},{3,26},{4,3},{5,28},{6,5},{7,30},{8,15},{9,0},{... | collective-permute-start | bytes 1572872 | tf_op jit(solution)/shard_map/ppermute | solution.py:233
Sparse Core Ops, SparseCore 0:
  9.4 57.7 all-gather.2
  133.6 42.8 reduce-scatter.1

commit v3 on v2

--- a/solution.py
+++ b/solution.py
@@ -8,11 +8,12 @@
 from jax.sharding import PartitionSpec as P
 
 VMEM_LIMIT = 48 * 1024 * 1024
+CHUNKS = (5, 3)
 SIDE = 4
 CAP = 2
 
 
-def mask_kernel(map_ref, b_ref, out_ref):
+def mask_kernel(map_ref, b_ref, *out_refs):
     blocks_dev, aux_blocks = map_ref.shape
     rows_dev, aux_dev = b_ref.shape
     width = rows_dev // blocks_dev
@@ -23,37 +24,55 @@
     ).astype(jnp.float32)
     keep = jnp.dot(map_ref[...].astype(jnp.float32), spread, preferred_element_type=jnp.float32)
     keep = keep.astype(jnp.bfloat16)
-    for block in range(blocks_dev):
-        rows = slice(block * width, (block + 1) * width)
-        out_ref[rows, :] = b_ref[rows, :] * keep[block : block + 1, :]
-
-
-def fit_kernel(m_ref, w_ref, out_ref, total):
-    step = pl.program_id(0)
-    part = jnp.dot(m_ref[0], w_ref[...], preferred_element_type=jnp.float32)
-
-    @pl.when(step == 0)
-    def _():
-        total[...] = part
-
-    @pl.when(step > 0)
-    def _():
-        total[...] += part
-
-    @pl.when(step == pl.num_programs(0) - 1)
-    def _():
-        out_ref[...] = total[...].astype(jnp.bfloat16).reshape(out_ref.shape)
+    block = 0
+    for out_ref in out_refs:
+        for start in range(0, out_ref.shape[0], width):
+            out_ref[start : start + width, :] = (
+                b_ref[block * width : (block + 1) * width, :] * keep[block : block + 1, :]
+            )
+            block += 1
+
+
+def fit_kernel(hops, own_ref, *refs):
+    steps = len(hops)
+    pieces, w_ref, out_ref = refs[:steps], refs[steps], refs[steps + 1]
+    left, right, total, left_sems, right_sems = refs[steps + 2 :]
+    depth = right.shape[1]
+    loads = []
+    for step, hop in enumerate(hops):
+        row = pl.multiple_of(((own_ref[0] + steps - hop) % steps) * depth, depth)
+        loads.append(
+            (
+                pltpu.make_async_copy(pieces[step], left.at[step], left_sems.at[step]),
+                pltpu.make_async_copy(w_ref.at[pl.ds(row, depth)], right.at[step], right_sems.at[step]),
+            )
+        )
+    for pair in loads:
+        for load in pair:
+            load.start()
+
+    total[...] = jnp.zeros_like(total)
+
+    @pl.loop(0, steps)
+    def _(step):
+        pltpu.make_async_copy(pieces[0], left.at[step], left_sems.at[step]).wait()
+        pltpu.make_async_copy(w_ref.at[pl.ds(0, depth)], right.at[step], right_sems.at[step]).wait()
+        total[...] += jnp.dot(left[step], right[step], preferred_element_type=jnp.float32)
+
+    out_ref[...] = total[...].astype(jnp.bfloat16).reshape(out_ref.shape)
 
 
 def pick_kernel(send_ref, *refs):
-    sources, outs = refs[:SIDE], refs[SIDE : SIDE + 2 * SIDE]
-    held, load_sems, store_sems = refs[SIDE + 2 * SIDE :]
-    blocks_dev = sources[0].shape[0]
+    count = SIDE * len(CHUNKS)
+    sources, outs = refs[:count], refs[count : count + 2 * SIDE]
+    held, load_sems, store_sems = refs[count + 2 * SIDE :]
     slots = outs[0].shape[0]
-    loads = [
-        pltpu.make_async_copy(source, held.at[pl.ds(index * blocks_dev, blocks_dev)], load_sems.at[index])
-        for index, source in enumerate(sources)
-    ]
+    loads, block = [], 0
+    for index, source in enumerate(sources):
+        loads.append(
+            pltpu.make_async_copy(source, held.at[pl.ds(block, source.shape[0])], load_sems.at[index])
+        )
+        block += source.shape[0]
     for load in loads:
         load.start()
     for load in loads:
@@ -71,13 +90,14 @@
         store.wait()
 
 
-def gram_kernel(domain_max, where_ref, counts_ref, *refs):
+def gram_kernel(domain_max, where_ref, counts_ref, own_ref, *refs):
     messages = 2 * SIDE
-    arrived, out_ref = refs[:messages], refs[messages]
-    held, values, load_sems, store_sems = refs[messages + 1 :]
+    arrived, out_refs = refs[:messages], refs[messages : messages + 2]
+    held, values, load_sems, store_sems = refs[messages + 2 :]
     slots = arrived[0].shape[0]
-    pairs_dev, n_aux, share, size = values.shape
+    n_aux, pairs_dev, share, size = values.shape
     width = held.shape[1]
+    half = out_refs[0].shape[1]
     loads = [
         pltpu.make_async_copy(source, held.at[pl.ds(index * slots, slots)], load_sems.at[index])
         for index, source in enumerate(arrived)
@@ -90,20 +110,66 @@
     column = lax.broadcasted_iota(jnp.int32, (size, size), 1)
     furthest = jnp.maximum(row, column)
     stores = []
-    for pair in range(pairs_dev):
-        stack = jnp.concatenate(
-            [held[where_ref[pair * domain_max + index]] for index in range(domain_max)], axis=0
-        )
-        value = lax.dot_general(
-            stack, stack, (((1,), (1,)), ((), ())), preferred_element_type=jnp.float32
-        )
-        value = jnp.where(furthest < counts_ref[pair] * width, value, 0.0)
-        values[pair] = value.reshape(n_aux, share, size)
-        store = pltpu.make_async_copy(values.at[pair], out_ref.at[:, pair], store_sems.at[pair])
+    for index, out in enumerate(out_refs):
+
+        @pl.loop(index * half, (index + 1) * half)
+        def _(pair):
+            stack = jnp.concatenate(
+                [held[where_ref[pair * domain_max + index]] for index in range(domain_max)], axis=0
+            )
+            value = lax.dot_general(
+                stack, stack, (((1,), (1,)), ((), ())), preferred_element_type=jnp.float32
+            )
+            value = jnp.where(furthest < counts_ref[pair] * width, value, 0.0)
+            value = value.reshape(n_aux, share, size)
+            for index in range(n_aux):
+                values[(index + n_aux - own_ref[0]) % n_aux, pair] = value[index]
+
+        store = pltpu.make_async_copy(
+            values.at[:, pl.ds(index * half, half)], out, store_sems.at[index]
+        )
         store.start()
         stores.append(store)
     for store in stores:
         store.wait()
+
+
+def ring_gather(chunks):
+    n_aux = lax.axis_size("aux")
+    rings = []
+    for index, chunk in enumerate(chunks):
+        far = n_aux // 2 if index % 2 == 0 else n_aux // 2 - 1
+        rings.append((far, n_aux - 1 - far, {0: chunk}, [chunk, chunk]))
+    for step in range(1, n_aux // 2 + 1):
+        for far_right, far_left, found, moving in rings:
+            if step <= far_right:
+                moving[0] = shift(moving[0], 1)
+                found[step] = moving[0]
+            if step <= far_left:
+                moving[1] = shift(moving[1], -1)
+                found[n_aux - step] = moving[1]
+    return [found for _, _, found, _ in rings]
+
+
+def ring_sum(parts):
+    n_aux = lax.axis_size("aux")
+    rings = []
+    for index, part in enumerate(parts):
+        far = n_aux // 2 if index % 2 == 0 else n_aux // 2 - 1
+        rings.append([part, far, n_aux - 1 - far, None, None])
+    for step in range(n_aux // 2, 0, -1):
+        for ring in rings:
+            part, far_right, far_left, right, left = ring
+            if step <= far_right:
+                ring[3] = shift(part[step] if right is None else right + part[step], 1)
+            if step <= far_left:
+                ring[4] = shift(part[n_aux - step] if left is None else left + part[n_aux - step], -1)
+    return [part[0] + right + left for part, _, _, right, left in rings]
+
+
+def shift(value, by):
+    n_aux = lax.axis_size("aux")
+    return lax.ppermute(value, "aux", [(index, (index + by) % n_aux) for index in range(n_aux)])
 
 
 def device_of(x, y, core):
@@ -180,33 +246,43 @@
     params = pltpu.CompilerParams(vmem_limit_bytes=VMEM_LIMIT)
     anywhere = pl.BlockSpec(memory_space=pl.ANY)
 
+    place = lax.axis_index("aux").astype(jnp.int32).reshape(1)
+
     masked = pl.pallas_call(
         mask_kernel,
-        out_shape=jax.ShapeDtypeStruct(b_three.shape, jnp.bfloat16),
+        out_shape=[jax.ShapeDtypeStruct((blocks * width, aux_dev), jnp.bfloat16) for blocks in CHUNKS],
         compiler_params=params,
         name="mask",
     )(aux_map, b_three)
-    gathered = lax.all_gather(masked, "aux", axis=0)
+    rings = ring_gather(masked)
     send, where = plan(domains, own, pairs_dev, blocks_dev, n_pair)
 
     block_shape = (width, aux_dev)
-    fitted = pl.pallas_call(
-        fit_kernel,
-        grid=(n_aux,),
-        in_specs=[
-            pl.BlockSpec((1, rows_dev, aux_dev), lambda k: (k, 0, 0)),
-            pl.BlockSpec((aux_dev, aux_dev), lambda k: (k, 0)),
-        ],
-        out_specs=pl.BlockSpec((blocks_dev, *block_shape), lambda k: (0, 0, 0)),
-        scratch_shapes=[pltpu.VMEM((rows_dev, aux_dev), jnp.float32)],
-        out_shape=jax.ShapeDtypeStruct((blocks_dev, *block_shape), jnp.bfloat16),
-        compiler_params=params,
-        name="fit",
-    )(gathered, metric)
-
-    sources = {0: fitted}
-    for hop in (1, 3, 2):
-        sources[hop] = lax.ppermute(fitted, "pair", gather_perm(hop))
+    sources = {}
+    for index, (blocks, ring) in enumerate(zip(CHUNKS, rings)):
+        hops = tuple(ring)
+        fitted = pl.pallas_call(
+            functools.partial(fit_kernel, hops),
+            grid_spec=pltpu.PrefetchScalarGridSpec(
+                num_scalar_prefetch=1,
+                grid=(),
+                in_specs=[anywhere] * (n_aux + 1),
+                out_specs=pl.BlockSpec(memory_space=pltpu.VMEM),
+                scratch_shapes=[
+                    pltpu.VMEM((n_aux, blocks * width, aux_dev), jnp.bfloat16),
+                    pltpu.VMEM((n_aux, aux_dev, aux_dev), jnp.bfloat16),
+                    pltpu.VMEM((blocks * width, aux_dev), jnp.float32),
+                    pltpu.SemaphoreType.DMA((n_aux,)),
+                    pltpu.SemaphoreType.DMA((n_aux,)),
+                ],
+            ),
+            out_shape=jax.ShapeDtypeStruct((blocks, *block_shape), jnp.bfloat16),
+            compiler_params=params,
+            name="fit",
+        )(place, *[ring[hop] for hop in hops], metric)
+        sources[0, index] = fitted
+        for hop in (1, 3, 2):
+            sources[hop, index] = lax.ppermute(fitted, "pair", gather_perm(hop))
 
     messages, slots = 2 * SIDE, SIDE * CAP
     picked = pl.pallas_call(
@@ -214,18 +290,18 @@
         grid_spec=pltpu.PrefetchScalarGridSpec(
             num_scalar_prefetch=1,
             grid=(),
-            in_specs=[anywhere] * SIDE,
+            in_specs=[anywhere] * (SIDE * len(CHUNKS)),
             out_specs=[anywhere] * messages,
             scratch_shapes=[
                 pltpu.VMEM((SIDE * blocks_dev, *block_shape), jnp.bfloat16),
-                pltpu.SemaphoreType.DMA((SIDE,)),
+                pltpu.SemaphoreType.DMA((SIDE * len(CHUNKS),)),
                 pltpu.SemaphoreType.DMA((messages * slots,)),
             ],
         ),
         out_shape=[jax.ShapeDtypeStruct((slots, *block_shape), jnp.bfloat16)] * messages,
         compiler_params=params,
         name="pick",
-    )(send, *[sources[hop] for hop in range(SIDE)])
+    )(send, *[sources[hop, index] for hop in range(SIDE) for index in range(len(CHUNKS))])
 
     arrived = {0: picked[0]}
     for hop, flip in ((1, 0), (3, 0), (1, 1), (3, 1), (2, 0), (2, 1), (0, 1)):
@@ -234,25 +310,26 @@
 
     size = domain_max * width
     share = size // n_aux
-    partial_value = pl.pallas_call(
+    half = pairs_dev // 2
+    partial_values = pl.pallas_call(
         functools.partial(gram_kernel, domain_max),
         grid_spec=pltpu.PrefetchScalarGridSpec(
-            num_scalar_prefetch=2,
+            num_scalar_prefetch=3,
             grid=(),
             in_specs=[anywhere] * messages,
-            out_specs=anywhere,
+            out_specs=[anywhere] * 2,
             scratch_shapes=[
                 pltpu.VMEM((messages * slots, *block_shape), jnp.bfloat16),
-                pltpu.VMEM((pairs_dev, n_aux, share, size), jnp.float32),
+                pltpu.VMEM((n_aux, pairs_dev, share, size), jnp.float32),
                 pltpu.SemaphoreType.DMA((messages,)),
-                pltpu.SemaphoreType.DMA((pairs_dev,)),
+                pltpu.SemaphoreType.DMA((2,)),
             ],
         ),
-        out_shape=jax.ShapeDtypeStruct((n_aux, pairs_dev, share, size), jnp.float32),
+        out_shape=[jax.ShapeDtypeStruct((n_aux, half, share, size), jnp.float32)] * 2,
         compiler_params=params,
         name="gram",
-    )(where, counts, *[arrived[message] for message in range(messages)])
-    return lax.psum_scatter(partial_value, "aux", scatter_dimension=0, tiled=False)
+    )(where, counts, place, *[arrived[message] for message in range(messages)])
+    return jnp.concatenate(ring_sum(partial_values), axis=0)
 
 
 def solution(mesh):

time: 184 us -> 161 us (0.88)
  waiting for transfers between devices: 129 us -> 63.4 us
  starting transfers between devices: 15.9 us -> 66 us
  between operations: 13.6 us -> 0.32 us
  Pallas kernels: 17.9 us -> 21.2 us
    all_gather x1 -> x0, waiting for transfers between devices: 55.2 us -> none  [per_device(): gathered = lax.all_gather(masked, 'aux', axis=0)]
    ppermute x3 -> x34, starting transfers between devices: 4.79 us -> 53.4 us  [the longest x28 45.7 us: shift(): lax.ppermute(value, 'aux', [(index, (index + by) % n_aux) for index in ra...]
    reduce_scatter x1 -> x0, waiting for transfers between devices: 43 us -> none  [per_device(): lax.psum_scatter(partial_value, 'aux', scatter_dimension=0, tiled=False)]
    ppermute x3 -> x34, waiting for transfers between devices: 11.8 us -> 45.5 us  [the longest x28 35.6 us: shift(): lax.ppermute(value, 'aux', [(index, (index + by) % n_aux) for index in ra...]
    pallas_call x1, Pallas kernels: 3.96 us -> 5.91 us  [per_device(): pl.pallas_call(functools.partial(gram_kernel, domain_max), grid_spec=pltp...]
    pallas_call x2 -> x3, Pallas kernels: 7.99 us -> 8.84 us  [the longest x2 8.68 us: per_device(): pl.pallas_call(functools.partial(fit_kernel, hops), grid_spec=pltpu.Prefe...]
  transfers between devices with their start and end apart: 12 -> 41, of which waited for: 10 -> 18; matrix products, arithmetic and copies ran while one was open for 2% -> 3% of each run, Pallas kernels for 0% -> 5%
where the time goes in v3:
time: 161 us; the launch traced here: 160 us
  starting transfers between devices  66 us (41%)
  waiting for transfers between devices  63.4 us (39%)
  Pallas kernels  21.2 us (13%)
  local copies, waits for them, and re-layouts  6.16 us (4%)
  other arithmetic  2.79 us (2%)
    ppermute x28, starting transfers between devices, shift(): lax.ppermute(value, 'aux', [(index, (index + by) % n_aux) for index in ra...  45.7 us
    ppermute x28, waiting for transfers between devices, shift(): lax.ppermute(value, 'aux', [(index, (index + by) % n_aux) for index in ra...  35.6 us
    ppermute x7, waiting for transfers between devices, per_device(): lax.ppermute(picked[message], 'pair', spread_perm(hop, flip))  17.9 us
    ppermute x7, starting transfers between devices, per_device(): lax.ppermute(picked[message], 'pair', spread_perm(hop, flip))  12.6 us
    ppermute x6, waiting for transfers between devices, per_device(): sources[hop, index] = lax.ppermute(fitted, 'pair', gather_perm(hop))  9.93 us
    pallas_call x2, Pallas kernels, per_device(): pl.pallas_call(functools.partial(fit_kernel, hops), grid_spec=pltpu.Prefe...  8.68 us
    ppermute x6, starting transfers between devices, per_device(): sources[hop, index] = lax.ppermute(fitted, 'pair', gather_perm(hop))  7.62 us
    pallas_call x1, Pallas kernels, per_device(): pl.pallas_call(pick_kernel, grid_spec=pltpu.PrefetchScalarGridSpec(num_sc...  6.49 us
  transfers between devices with their start and end apart: 41, of which 18 were waited for; matrix products, arithmetic and copies ran while one was open for 3% of the time, Pallas kernels for 5%

profile of v3, /device:TPU:2, one launch (start us, length us, event | category | flops | bytes accessed | tf_op | source)
XLA Modules:
  0.0 159.8 jit_solution(13249519225889475991)
XLA Ops:
  1.9 5.9 %collective-permute-start.8 = (bf16[192,512]{1,0:T(8,128)(2,1)S(1)}, bf16[192,512]{1,0:T(8,128)(2,1)S(1)}, u32[]{:S(2)}, u32[]{:S(2)}) collective-permute-start(bf16[192,512]{1,0:T(8,128)(2,1)S(1)} %get-tuple-element.18.refs_0_), channel_id=1, source_target_pairs={{0,224},{32,0},{64,32},{96,64},{128,96},{160,128},{192,160},{224,1... | collective-permute-start | bytes 589832 | tf_op jit(solution)/shard_map/ppermute | solution.py:172
  7.8 3.2 %collective-permute-start.1 = (bf16[320,512]{1,0:T(8,128)(2,1)S(1)}, bf16[320,512]{1,0:T(8,128)(2,1)S(1)}, u32[]{:S(2)}, u32[]{:S(2)}) collective-permute-start(bf16[320,512]{1,0:T(8,128)(2,1)S(1)} %get-tuple-element.17.refs_0_), channel_id=1, source_target_pairs={{0,224},{32,0},{64,32},{96,64},{128,96},{160,128},{192,160},{224,1... | collective-permute-start | bytes 983048 | tf_op jit(solution)/shard_map/ppermute | solution.py:172
  13.3 9.1 %collective-permute-done.refs_1_ = bf16[320,512]{1,0:T(8,128)(2,1)S(1)} collective-permute-done((bf16[320,512]{1,0:T(8,128)(2,1)S(1)}, bf16[320,512]{1,0:T(8,128)(2,1)S(1)}, u32[]{:S(2)}, u32[]{:S(2)}) %collective-permute-start) | collective-permute-done | bytes 327712 | tf_op jit(solution)/shard_map/ppermute | solution.py:172
  22.5 3.3 %collective-permute-start.10 = (bf16[192,512]{1,0:T(8,128)(2,1)S(1)}, bf16[192,512]{1,0:T(8,128)(2,1)S(1)}, u32[]{:S(2)}, u32[]{:S(2)}) collective-permute-start(bf16[192,512]{1,0:T(8,128)(2,1)S(1)} %collective-permute-done.8.refs_2_), channel_id=1, source_target_pairs={{0,224},{32,0},{64,32},{96,64},{128,96},{160,128},{192,160},{224,1... | collective-permute-start | bytes 589832 | tf_op jit(solution)/shard_map/ppermute | solution.py:172
  26.0 5.9 %collective-permute-done.2.refs_3_ = bf16[320,512]{1,0:T(8,128)(2,1)S(1)} collective-permute-done((bf16[320,512]{1,0:T(8,128)(2,1)S(1)}, bf16[320,512]{1,0:T(8,128)(2,1)S(1)}, u32[]{:S(2)}, u32[]{:S(2)}) %collective-permute-start.2) | collective-permute-done | bytes 327712 | tf_op jit(solution)/shard_map/ppermute | solution.py:172
  32.1 3.3 %collective-permute-start.12 = (bf16[192,512]{1,0:T(8,128)(2,1)S(1)}, bf16[192,512]{1,0:T(8,128)(2,1)S(1)}, u32[]{:S(2)}, u32[]{:S(2)}) collective-permute-start(bf16[192,512]{1,0:T(8,128)(2,1)S(1)} %collective-permute-done.10.refs_4_), channel_id=1, source_target_pairs={{0,224},{32,0},{64,32},{96,64},{128,96},{160,128},{192,160},{224,1... | collective-permute-start | bytes 589832 | tf_op jit(solution)/shard_map/ppermute | solution.py:172
  35.5 9.2 %collective-permute-done.9.refs_3_ = bf16[192,512]{1,0:T(8,128)(2,1)S(1)} collective-permute-done((bf16[192,512]{1,0:T(8,128)(2,1)S(1)}, bf16[192,512]{1,0:T(8,128)(2,1)S(1)}, u32[]{:S(2)}, u32[]{:S(2)}) %collective-permute-start.9) | collective-permute-done | bytes 196640 | tf_op jit(solution)/shard_map/ppermute | solution.py:172
  44.7 3.2 %collective-permute-start.13 = (bf16[192,512]{1,0:T(8,128)(2,1)S(1)}, bf16[192,512]{1,0:T(8,128)(2,1)S(1)}, u32[]{:S(2)}, u32[]{:S(2)}) collective-permute-start(bf16[192,512]{1,0:T(8,128)(2,1)S(1)} %collective-permute-done.12.refs_6_), channel_id=1, source_target_pairs={{0,224},{32,0},{64,32},{96,64},{128,96},{160,128},{192,160},{224,1... | collective-permute-start | bytes 589832 | tf_op jit(solution)/shard_map/ppermute | solution.py:172
  49.9 3.7 %collective-permute-done.11.refs_5_ = bf16[192,512]{1,0:T(8,128)(2,1)S(1)} collective-permute-done((bf16[192,512]{1,0:T(8,128)(2,1)S(1)}, bf16[192,512]{1,0:T(8,128)(2,1)S(1)}, u32[]{:S(2)}, u32[]{:S(2)}) %collective-permute-start.11) | collective-permute-done | bytes 196640 | tf_op jit(solution)/shard_map/ppermute | solution.py:172
  55.9 4.6 %fit.3.refs_1_ = bf16[3,64,512]{2,1,0:T(8,128)(2,1)S(1)} custom-call(s32[1]{0:T(128)} %bitcast.2.own_ref, bf16[192,512]{1,0:T(8,128)(2,1)S(1)} %get-tuple-element.18.refs_0_, bf16[192,512]{1,0:T(8,128)(2,1)S(1)} %collective-permute-done.7.refs_1_, bf16[192,512]{1,0:T(8,128)(2,1)S(1)} %collective-permute-done.8.refs_2_, ...), custom_call_target="tpu_custom_call" | custom-call | tf_op jit(solution)/shard_map/fit/pallas_call | solution.py:264
  61.4 4.0 %fit.2.refs_0_ = bf16[5,64,512]{2,1,0:T(8,128)(2,1)S(1)} custom-call(s32[1]{0:T(128)} %bitcast.2.own_ref, bf16[320,512]{1,0:T(8,128)(2,1)S(1)} %get-tuple-element.17.refs_0_, bf16[320,512]{1,0:T(8,128)(2,1)S(1)} %collective-permute-done.refs_1_, bf16[320,512]{1,0:T(8,128)(2,1)S(1)} %collective-permute-done.1.refs_2_, ...), custom_call_target="tpu_custom_call" | custom-call | tf_op jit(solution)/shard_map/fit/pallas_call | solution.py:264
  72.6 6.6 %collective-permute-done.17.refs_5_ = bf16[3,64,512]{2,1,0:T(8,128)(2,1)S(1)} collective-permute-done((bf16[3,64,512]{2,1,0:T(8,128)(2,1)S(1)}, bf16[3,64,512]{2,1,0:T(8,128)(2,1)S(1)}, u32[]{:S(2)}, u32[]{:S(2)}) %collective-permute-start.17) | collective-permute-done | bytes 196640 | tf_op jit(solution)/shard_map/ppermute | solution.py:285
  79.2 3.3 %collective-permute-done.15.refs_3_ = bf16[3,64,512]{2,1,0:T(8,128)(2,1)S(1)} collective-permute-done((bf16[3,64,512]{2,1,0:T(8,128)(2,1)S(1)}, bf16[3,64,512]{2,1,0:T(8,128)(2,1)S(1)}, u32[]{:S(2)}, u32[]{:S(2)}) %collective-permute-start.15) | collective-permute-done | bytes 196640 | tf_op jit(solution)/shard_map/ppermute | solution.py:285
  82.5 6.5 %pick.1 = (bf16[8,64,512]{2,1,0:T(8,128)(2,1)S(1)}, bf16[8,64,512]{2,1,0:T(8,128)(2,1)S(1)}, bf16[8,64,512]{2,1,0:T(8,128)(2,1)S(1)}, bf16[8,64,512]{2,1,0:T(8,1...) custom-call(s32[64]{0:T(128)S(1)} %add.386.send_ref, ...), custom_call_target="tpu_custom_call" | custom-call | tf_op jit(solution)/shard_map/pick/pallas_call | solution.py:288
  94.8 3.3 %collective-permute-start.24 = (bf16[8,64,512]{2,1,0:T(8,128)(2,1)}, bf16[8,64,512]{2,1,0:T(8,128)(2,1)S(1)}, u32[]{:S(2)}, u32[]{:S(2)}) collective-permute-start(bf16[8,64,512]{2,1,0:T(8,128)(2,1)} %get-tuple-element.24), channel_id=1, source_target_pairs={{0,5},{1,16},{2,7},{3,18},{4,1},{5,20},{6,3},{7,22},{8,13},{9,24},... | collective-permute-start | bytes 1572872 | tf_op jit(solution)/shard_map/ppermute | solution.py:309
  104.6 7.4 %collective-permute-done.23.refs_4_ = bf16[8,64,512]{2,1,0:T(8,128)(2,1)S(1)} collective-permute-done((bf16[8,64,512]{2,1,0:T(8,128)(2,1)}, bf16[8,64,512]{2,1,0:T(8,128)(2,1)S(1)}, u32[]{:S(2)}, u32[]{:S(2)}) %collective-permute-start.23) | collective-permute-done | bytes 524320 | tf_op jit(solution)/shard_map/ppermute | solution.py:309
  114.5 5.0 %collective-permute-done.26.refs_7_ = bf16[8,64,512]{2,1,0:T(8,128)(2,1)} collective-permute-done((bf16[8,64,512]{2,1,0:T(8,128)(2,1)}, bf16[8,64,512]{2,1,0:T(8,128)(2,1)}, u32[]{:S(2)}, u32[]{:S(2)}) %collective-permute-start.26) | collective-permute-done | bytes 524320 | tf_op jit(solution)/shard_map/ppermute | solution.py:309
  119.5 5.9 %gram.1 = (f32[8,5,32,256]{3,2,1,0:T(8,128)S(1)}, f32[8,5,32,256]{3,2,1,0:T(8,128)}) custom-call(s32[40]{0:T(128)S(1)} %fusion.8.where_ref, s32[10]{0:T(128)S(1)} %copy-done.3, s32[1]{0:T(128)} %bitcast.2.own_ref, bf16[8,64,512]{2,1,0:T(8,128)(2,1)S(1)} %get-tuple-element.19.refs_0_, bf16[8,64,512]{2,1,0:T(8,128)(2,1)S(1)} %collective-permute-done.20.refs_1_, ...), custom_call_target="tpu_custom_call" | custom-call | tf_op jit(solution)/shard_map/gram/pallas_call | solution.py:314
  125.6 3.2 %collective-permute-start.31 = (f32[5,32,256]{2,1,0:T(8,128)S(1)}, f32[5,32,256]{2,1,0:T(8,128)S(1)}, u32[]{:S(2)}, u32[]{:S(2)}) collective-permute-start(f32[5,32,256]{2,1,0:T(8,128)S(1)} %get-tuple-element.34), channel_id=1, source_target_pairs={{0,224},{32,0},{64,32},{96,64},{128,96},{160,128},{192,160},{224,1... | collective-permute-start | bytes 491528 | tf_op jit(solution)/shard_map/ppermute | solution.py:172
  129.9 3.2 %collective-permute-start.37 = (f32[5,32,256]{2,1,0:T(8,128)S(1)}, f32[5,32,256]{2,1,0:T(8,128)S(1)}, u32[]{:S(2)}, u32[]{:S(2)}) collective-permute-start(f32[5,32,256]{2,1,0:T(8,128)S(1)} %get-tuple-element.40), channel_id=1, source_target_pairs={{0,224},{32,0},{64,32},{96,64},{128,96},{160,128},{192,160},{224,1... | collective-permute-start | bytes 491528 | tf_op jit(solution)/shard_map/ppermute | solution.py:172
  136.0 3.8 %collective-permute-start.38 = (f32[5,32,256]{2,1,0:T(8,128)S(1)}, f32[5,32,256]{2,1,0:T(8,128)S(1)}, u32[]{:S(2)}, u32[]{:S(2)}) collective-permute-start(f32[5,32,256]{2,1,0:T(8,128)S(1)} %bitcast_add_fusion.2), channel_id=1, source_target_pairs={{0,224},{32,0},{64,32},{96,64},{128,96},{160,128},{192,160},{224,1... | collective-permute-start | bytes 491528 | tf_op jit(solution)/shard_map/ppermute | solution.py:172
  140.1 3.2 %collective-permute-start.32 = (f32[5,32,256]{2,1,0:T(8,128)S(1)}, f32[5,32,256]{2,1,0:T(8,128)S(1)}, u32[]{:S(2)}, u32[]{:S(2)}) collective-permute-start(f32[5,32,256]{2,1,0:T(8,128)S(1)} %get-tuple-element.32), channel_id=1, source_target_pairs={{0,224},{32,0},{64,32},{96,64},{128,96},{160,128},{192,160},{224,1... | collective-permute-start | bytes 491528 | tf_op jit(solution)/shard_map/ppermute | solution.py:172
  143.8 3.8 %collective-permute-start.39 = (f32[5,32,256]{2,1,0:T(8,128)S(1)}, f32[5,32,256]{2,1,0:T(8,128)S(1)}, u32[]{:S(2)}, u32[]{:S(2)}) collective-permute-start(f32[5,32,256]{2,1,0:T(8,128)S(1)} %get-tuple-element.38), channel_id=1, source_target_pairs={{0,224},{32,0},{64,32},{96,64},{128,96},{160,128},{192,160},{224,1... | collective-permute-start | bytes 491528 | tf_op jit(solution)/shard_map/ppermute | solution.py:172
  148.2 3.6 %collective-permute-start.33 = (f32[5,32,256]{2,1,0:T(8,128)S(1)}, f32[5,32,256]{2,1,0:T(8,128)S(1)}, u32[]{:S(2)}, u32[]{:S(2)}) collective-permute-start(f32[5,32,256]{2,1,0:T(8,128)S(1)} %get-tuple-element.30), channel_id=1, source_target_pairs={{0,224},{32,0},{64,32},{96,64},{128,96},{160,128},{192,160},{224,1... | collective-permute-start | bytes 491528 | tf_op jit(solution)/shard_map/ppermute | solution.py:172
  (109 shorter events, 44.9 us)
Async XLA Ops:
  1.9 20.6 %collective-permute-start.8 = (bf16[192,512]{1,0:T(8,128)(2,1)S(1)}, bf16[192,512]{1,0:T(8,128)(2,1)S(1)}, u32[]{:S(2)}, u32[]{:S(2)}) collective-permute-start(bf16[192,512]{1,0:T(8,128)(2,1)S(1)} %get-tuple-element.18.refs_0_), channel_id=1, source_target_pairs={{0,224},{32,0},{64,32},{96,64},{128,96},{160,128},{192,160},{224,1... | collective-permute-start | bytes 589832 | tf_op jit(solution)/shard_map/ppermute | solution.py:172
  7.8 24.2 %collective-permute-start.7 = (bf16[192,512]{1,0:T(8,128)(2,1)S(1)}, bf16[192,512]{1,0:T(8,128)(2,1)S(1)}, u32[]{:S(2)}, u32[]{:S(2)}) collective-permute-start(bf16[192,512]{1,0:T(8,128)(2,1)S(1)} %get-tuple-element.18.refs_0_), channel_id=1, source_target_pairs={{0,32},{32,64},{64,96},{96,128},{128,160},{160,192},{192,224},{224... | collective-permute-start | bytes 589832 | tf_op jit(solution)/shard_map/ppermute | solution.py:172
  7.8 18.1 %collective-permute-start.1 = (bf16[320,512]{1,0:T(8,128)(2,1)S(1)}, bf16[320,512]{1,0:T(8,128)(2,1)S(1)}, u32[]{:S(2)}, u32[]{:S(2)}) collective-permute-start(bf16[320,512]{1,0:T(8,128)(2,1)S(1)} %get-tuple-element.17.refs_0_), channel_id=1, source_target_pairs={{0,224},{32,0},{64,32},{96,64},{128,96},{160,128},{192,160},{224,1... | collective-permute-start | bytes 983048 | tf_op jit(solution)/shard_map/ppermute | solution.py:172
  11.1 11.4 %collective-permute-start = (bf16[320,512]{1,0:T(8,128)(2,1)S(1)}, bf16[320,512]{1,0:T(8,128)(2,1)S(1)}, u32[]{:S(2)}, u32[]{:S(2)}) collective-permute-start(bf16[320,512]{1,0:T(8,128)(2,1)S(1)} %get-tuple-element.17.refs_0_), channel_id=1, source_target_pairs={{0,32},{32,64},{64,96},{96,128},{128,160},{160,192},{192,224},{224... | collective-permute-start | bytes 983048 | tf_op jit(solution)/shard_map/ppermute | solution.py:172
  22.5 9.6 %collective-permute-start.10 = (bf16[192,512]{1,0:T(8,128)(2,1)S(1)}, bf16[192,512]{1,0:T(8,128)(2,1)S(1)}, u32[]{:S(2)}, u32[]{:S(2)}) collective-permute-start(bf16[192,512]{1,0:T(8,128)(2,1)S(1)} %collective-permute-done.8.refs_2_), channel_id=1, source_target_pairs={{0,224},{32,0},{64,32},{96,64},{128,96},{160,128},{192,160},{224,1... | collective-permute-start | bytes 589832 | tf_op jit(solution)/shard_map/ppermute | solution.py:172
  25.9 22.0 %collective-permute-start.3 = (bf16[320,512]{1,0:T(8,128)(2,1)S(1)}, bf16[320,512]{1,0:T(8,128)(2,1)S(1)}, u32[]{:S(2)}, u32[]{:S(2)}) collective-permute-start(bf16[320,512]{1,0:T(8,128)(2,1)S(1)} %collective-permute-done.1.refs_2_), channel_id=1, source_target_pairs={{0,224},{32,0},{64,32},{96,64},{128,96},{160,128},{192,160},{224,1... | collective-permute-start | bytes 983048 | tf_op jit(solution)/shard_map/ppermute | solution.py:172
  31.9 16.1 %collective-permute-start.4 = (bf16[320,512]{1,0:T(8,128)(2,1)S(1)}, bf16[320,512]{1,0:T(8,128)(2,1)S(1)}, u32[]{:S(2)}, u32[]{:S(2)}) collective-permute-start(bf16[320,512]{1,0:T(8,128)(2,1)S(1)} %collective-permute-done.2.refs_3_), channel_id=1, source_target_pairs={{0,32},{32,64},{64,96},{96,128},{128,160},{160,192},{192,224},{224... | collective-permute-start | bytes 983048 | tf_op jit(solution)/shard_map/ppermute | solution.py:172
  32.0 12.6 %collective-permute-start.9 = (bf16[192,512]{1,0:T(8,128)(2,1)S(1)}, bf16[192,512]{1,0:T(8,128)(2,1)S(1)}, u32[]{:S(2)}, u32[]{:S(2)}) collective-permute-start(bf16[192,512]{1,0:T(8,128)(2,1)S(1)} %collective-permute-done.7.refs_1_), channel_id=1, source_target_pairs={{0,32},{32,64},{64,96},{96,128},{128,160},{160,192},{192,224},{224... | collective-permute-start | bytes 589832 | tf_op jit(solution)/shard_map/ppermute | solution.py:172
  32.1 12.5 %collective-permute-start.12 = (bf16[192,512]{1,0:T(8,128)(2,1)S(1)}, bf16[192,512]{1,0:T(8,128)(2,1)S(1)}, u32[]{:S(2)}, u32[]{:S(2)}) collective-permute-start(bf16[192,512]{1,0:T(8,128)(2,1)S(1)} %collective-permute-done.10.refs_4_), channel_id=1, source_target_pairs={{0,224},{32,0},{64,32},{96,64},{128,96},{160,128},{192,160},{224,1... | collective-permute-start | bytes 589832 | tf_op jit(solution)/shard_map/ppermute | solution.py:172
  47.9 13.5 %collective-permute-start.5 = (bf16[320,512]{1,0:T(8,128)(2,1)S(1)}, bf16[320,512]{1,0:T(8,128)(2,1)S(1)}, u32[]{:S(2)}, u32[]{:S(2)}) collective-permute-start(bf16[320,512]{1,0:T(8,128)(2,1)S(1)} %collective-permute-done.3.refs_4_), channel_id=1, source_target_pairs={{0,224},{32,0},{64,32},{96,64},{128,96},{160,128},{192,160},{224,1... | collective-permute-start | bytes 983048 | tf_op jit(solution)/shard_map/ppermute | solution.py:172
  48.0 13.4 %collective-permute-start.6 = (bf16[320,512]{1,0:T(8,128)(2,1)S(1)}, bf16[320,512]{1,0:T(8,128)(2,1)S(1)}, u32[]{:S(2)}, u32[]{:S(2)}) collective-permute-start(bf16[320,512]{1,0:T(8,128)(2,1)S(1)} %collective-permute-done.4.refs_5_), channel_id=1, source_target_pairs={{0,32},{32,64},{64,96},{96,128},{128,160},{160,192},{192,224},{224... | collective-permute-start | bytes 983048 | tf_op jit(solution)/shard_map/ppermute | solution.py:172
  60.5 11.4 %collective-permute-start.19 = (bf16[3,64,512]{2,1,0:T(8,128)(2,1)S(1)}, bf16[3,64,512]{2,1,0:T(8,128)(2,1)S(1)}, u32[]{:S(2)}, u32[]{:S(2)}) collective-permute-start(bf16[3,64,512]{2,1,0:T(8,128)(2,1)S(1)} %fit.3.refs_1_), channel_id=1, source_target_pairs={{0,24},{1,7},{2,26},{3,1},{4,28},{5,3},{6,30},{7,5},{8,0},{9,15},{... | collective-permute-start | bytes 589832 | tf_op jit(solution)/shard_map/ppermute | solution.py:285
  65.5 17.0 %collective-permute-start.18 = (bf16[5,64,512]{2,1,0:T(8,128)(2,1)S(1)}, bf16[5,64,512]{2,1,0:T(8,128)(2,1)S(1)}, u32[]{:S(2)}, u32[]{:S(2)}) collective-permute-start(bf16[5,64,512]{2,1,0:T(8,128)(2,1)S(1)} %fit.2.refs_0_), channel_id=1, source_target_pairs={{0,24},{1,7},{2,26},{3,1},{4,28},{5,3},{6,30},{7,5},{8,0},{9,15},{... | collective-permute-start | bytes 983048 | tf_op jit(solution)/shard_map/ppermute | solution.py:285
  68.3 14.2 %collective-permute-start.16 = (bf16[5,64,512]{2,1,0:T(8,128)(2,1)S(1)}, bf16[5,64,512]{2,1,0:T(8,128)(2,1)S(1)}, u32[]{:S(2)}, u32[]{:S(2)}) collective-permute-start(bf16[5,64,512]{2,1,0:T(8,128)(2,1)S(1)} %fit.2.refs_0_), channel_id=1, source_target_pairs={{0,16},{1,5},{2,18},{3,7},{4,20},{5,1},{6,22},{7,3},{8,24},{9,13},... | collective-permute-start | bytes 983048 | tf_op jit(solution)/shard_map/ppermute | solution.py:285
  68.5 14.0 %collective-permute-start.14 = (bf16[5,64,512]{2,1,0:T(8,128)(2,1)S(1)}, bf16[5,64,512]{2,1,0:T(8,128)(2,1)S(1)}, u32[]{:S(2)}, u32[]{:S(2)}) collective-permute-start(bf16[5,64,512]{2,1,0:T(8,128)(2,1)S(1)} %fit.2.refs_0_), channel_id=1, source_target_pairs={{0,8},{1,3},{2,10},{3,5},{4,12},{5,7},{6,14},{7,1},{8,16},{9,11},{... | collective-permute-start | bytes 983048 | tf_op jit(solution)/shard_map/ppermute | solution.py:285
  71.9 10.7 %collective-permute-start.15 = (bf16[3,64,512]{2,1,0:T(8,128)(2,1)S(1)}, bf16[3,64,512]{2,1,0:T(8,128)(2,1)S(1)}, u32[]{:S(2)}, u32[]{:S(2)}) collective-permute-start(bf16[3,64,512]{2,1,0:T(8,128)(2,1)S(1)} %fit.3.refs_1_), channel_id=1, source_target_pairs={{0,8},{1,3},{2,10},{3,5},{4,12},{5,7},{6,14},{7,1},{8,16},{9,11},{... | collective-permute-start | bytes 589832 | tf_op jit(solution)/shard_map/ppermute | solution.py:285
  89.1 10.5 %collective-permute-start.21 = (bf16[8,64,512]{2,1,0:T(8,128)(2,1)S(1)}, bf16[8,64,512]{2,1,0:T(8,128)(2,1)S(1)}, u32[]{:S(2)}, u32[]{:S(2)}) collective-permute-start(bf16[8,64,512]{2,1,0:T(8,128)(2,1)S(1)} %get-tuple-element.21), channel_id=1, source_target_pairs={{0,2},{1,9},{2,4},{3,11},{4,6},{5,13},{6,0},{7,15},{8,10},{9,17},{... | collective-permute-start | bytes 1572872 | tf_op jit(solution)/shard_map/ppermute | solution.py:309
  90.8 13.9 %collective-permute-start.22 = (bf16[8,64,512]{2,1,0:T(8,128)(2,1)}, bf16[8,64,512]{2,1,0:T(8,128)(2,1)S(1)}, u32[]{:S(2)}, u32[]{:S(2)}) collective-permute-start(bf16[8,64,512]{2,1,0:T(8,128)(2,1)} %get-tuple-element.22), channel_id=1, source_target_pairs={{0,3},{1,8},{2,5},{3,10},{4,7},{5,12},{6,1},{7,14},{8,11},{9,16},{... | collective-permute-start | bytes 1572872 | tf_op jit(solution)/shard_map/ppermute | solution.py:309
  91.9 20.2 %collective-permute-start.23 = (bf16[8,64,512]{2,1,0:T(8,128)(2,1)}, bf16[8,64,512]{2,1,0:T(8,128)(2,1)S(1)}, u32[]{:S(2)}, u32[]{:S(2)}) collective-permute-start(bf16[8,64,512]{2,1,0:T(8,128)(2,1)} %get-tuple-element.23), channel_id=1, source_target_pairs={{0,4},{1,17},{2,6},{3,19},{4,0},{5,21},{6,2},{7,23},{8,12},{9,25},... | collective-permute-start | bytes 1572872 | tf_op jit(solution)/shard_map/ppermute | solution.py:309
  94.8 19.7 %collective-permute-start.24 = (bf16[8,64,512]{2,1,0:T(8,128)(2,1)}, bf16[8,64,512]{2,1,0:T(8,128)(2,1)S(1)}, u32[]{:S(2)}, u32[]{:S(2)}) collective-permute-start(bf16[8,64,512]{2,1,0:T(8,128)(2,1)} %get-tuple-element.24), channel_id=1, source_target_pairs={{0,5},{1,16},{2,7},{3,18},{4,1},{5,20},{6,3},{7,22},{8,13},{9,24},... | collective-permute-start | bytes 1572872 | tf_op jit(solution)/shard_map/ppermute | solution.py:309
  98.1 16.4 %collective-permute-start.25 = (bf16[8,64,512]{2,1,0:T(8,128)(2,1)}, bf16[8,64,512]{2,1,0:T(8,128)(2,1)}, u32[]{:S(2)}, u32[]{:S(2)}) collective-permute-start(bf16[8,64,512]{2,1,0:T(8,128)(2,1)} %get-tuple-element.25), channel_id=1, source_target_pairs={{0,6},{1,25},{2,0},{3,27},{4,2},{5,29},{6,4},{7,31},{8,14},{9,1},{... | collective-permute-start | bytes 1572872 | tf_op jit(solution)/shard_map/ppermute | solution.py:309
  99.6 19.9 %collective-permute-start.26 = (bf16[8,64,512]{2,1,0:T(8,128)(2,1)}, bf16[8,64,512]{2,1,0:T(8,128)(2,1)}, u32[]{:S(2)}, u32[]{:S(2)}) collective-permute-start(bf16[8,64,512]{2,1,0:T(8,128)(2,1)} %get-tuple-element.26), channel_id=1, source_target_pairs={{0,7},{1,24},{2,1},{3,26},{4,3},{5,28},{6,5},{7,30},{8,15},{9,0},{... | collective-permute-start | bytes 1572872 | tf_op jit(solution)/shard_map/ppermute | solution.py:309
  125.6 14.2 %collective-permute-start.31 = (f32[5,32,256]{2,1,0:T(8,128)S(1)}, f32[5,32,256]{2,1,0:T(8,128)S(1)}, u32[]{:S(2)}, u32[]{:S(2)}) collective-permute-start(f32[5,32,256]{2,1,0:T(8,128)S(1)} %get-tuple-element.34), channel_id=1, source_target_pairs={{0,224},{32,0},{64,32},{96,64},{128,96},{160,128},{192,160},{224,1... | collective-permute-start | bytes 491528 | tf_op jit(solution)/shard_map/ppermute | solution.py:172
  129.8 13.5 %collective-permute-start.34 = (f32[5,32,256]{2,1,0:T(8,128)S(1)}, f32[5,32,256]{2,1,0:T(8,128)S(1)}, u32[]{:S(2)}, u32[]{:S(2)}) collective-permute-start(f32[5,32,256]{2,1,0:T(8,128)S(1)} %get-tuple-element.39), channel_id=1, source_target_pairs={{0,32},{32,64},{64,96},{96,128},{128,160},{160,192},{192,224},{224... | collective-permute-start | bytes 491528 | tf_op jit(solution)/shard_map/ppermute | solution.py:172
  (22 other events, 203.9 us)

commit v4 on v3

v4 whole, which is shorter than its diff:
```python
import functools

import jax
import jax.numpy as jnp
from jax import lax
from jax.experimental import pallas as pl
from jax.experimental.pallas import tpu as pltpu
from jax.sharding import PartitionSpec as P

VMEM_LIMIT = 16 * 1024 * 1024
CHUNKS = (5, 3)
SIDE = 4
CAP = 2


def mask_kernel(map_ref, b_ref, *out_refs):
    blocks_dev, aux_blocks = map_ref.shape
    rows_dev, aux_dev = b_ref.shape
    width = rows_dev // blocks_dev
    aux_width = aux_dev // aux_blocks
    spread = (
        lax.broadcasted_iota(jnp.int32, (aux_blocks, aux_dev), 1) // aux_width
        == lax.broadcasted_iota(jnp.int32, (aux_blocks, aux_dev), 0)
    ).astype(jnp.float32)
    keep = jnp.dot(map_ref[...].astype(jnp.float32), spread, preferred_element_type=jnp.float32)
    keep = keep.astype(jnp.bfloat16)
    block = 0
    for out_ref in out_refs:
        for start in range(0, out_ref.shape[0], width):
            out_ref[start : start + width, :] = (
                b_ref[block * width : (block + 1) * width, :] * keep[block : block + 1, :]
            )
            block += 1


def metric_kernel(hops, own_ref, w_ref, out_ref, sems):
    steps = len(hops)
    depth = out_ref.shape[1]
    loads = []
    for step, hop in enumerate(hops):
        row = pl.multiple_of(((own_ref[0] + steps - hop) % steps) * depth, depth)
        loads.append(pltpu.make_async_copy(w_ref.at[pl.ds(row, depth)], out_ref.at[step], sems.at[step]))
    for load in loads:
        load.start()
    for load in loads:
        load.wait()


def fit_kernel(*refs):
    pieces, w_ref, out_ref, total = refs[:-3], refs[-3], refs[-2], refs[-1]
    for step, piece in enumerate(pieces):
        part = jnp.dot(piece[...], w_ref[step], preferred_element_type=jnp.float32)
        if step == 0:
            total[...] = part
        elif step < len(pieces) - 1:
            total[...] += part
        else:
            out_ref[...] = (total[...] + part).astype(jnp.bfloat16).reshape(out_ref.shape)


def pick_kernel(send_ref, *refs):
    count = SIDE * len(CHUNKS)
    sources, outs = refs[:count], refs[count:]
    slots = outs[0].shape[0]
    for message, out in enumerate(outs):
        for slot in range(slots):
            block = send_ref[message * slots + slot]
            start = 0
            for chunk, blocks in enumerate(CHUNKS):
                source = sources[(slot // CAP) * len(CHUNKS) + chunk]

                @pl.when((block >= start) & (block < start + blocks))
                def _(out=out, slot=slot, source=source, index=block - start):
                    out[slot] = source[index]

                start += blocks


def gram_kernel(first_pair, domain_max, goes_ref, counts_ref, own_ref, *refs):
    arrived, out_ref, stacks = refs[:-2], refs[-2], refs[-1]
    slots = arrived[0].shape[0]
    n_aux, pairs, share, size = out_ref.shape
    places, width, depth = stacks.shape
    for message, source in enumerate(arrived):
        for slot in range(slots):
            goes = goes_ref[message * slots + slot] - first_pair * domain_max

            @pl.when((goes >= 0) & (goes < places))
            def _(source=source, slot=slot, goes=goes):
                stacks[goes] = source[slot]

    row = lax.broadcasted_iota(jnp.int32, (size, size), 0)
    column = lax.broadcasted_iota(jnp.int32, (size, size), 1)
    furthest = jnp.maximum(row, column)
    for pair in range(pairs):
        stack = stacks[pair * domain_max : (pair + 1) * domain_max].reshape(size, depth)
        value = lax.dot_general(
            stack, stack, (((1,), (1,)), ((), ())), preferred_element_type=jnp.float32
        )
        value = jnp.where(furthest < counts_ref[first_pair + pair] * width, value, 0.0)
        value = value.reshape(n_aux, share, size)
        for index in range(n_aux):
            out_ref[(index + n_aux - own_ref[0]) % n_aux, pair] = value[index]


def ring_gather(chunks):
    n_aux = lax.axis_size("aux")
    rings = []
    for index, chunk in enumerate(chunks):
        far = n_aux // 2 if index % 2 == 0 else n_aux // 2 - 1
        rings.append((far, n_aux - 1 - far, {0: chunk}, [chunk, chunk]))
    for step in range(1, n_aux // 2 + 1):
        for far_right, far_left, found, moving in rings:
            if step <= far_right:
                moving[0] = shift(moving[0], 1)
                found[step] = moving[0]
            if step <= far_left:
                moving[1] = shift(moving[1], -1)
                found[n_aux - step] = moving[1]
    return [found for _, _, found, _ in rings]


def ring_sum(parts):
    n_aux = lax.axis_size("aux")
    rings = []
    for index, part in enumerate(parts):
        far = n_aux // 2 if index % 2 == 0 else n_aux // 2 - 1
        rings.append([part, far, n_aux - 1 - far, None, None])
    for step in range(n_aux // 2, 0, -1):
        for ring in rings:
            part, far_right, far_left, right, left = ring
            if step <= far_right:
                ring[3] = shift(part[step] if right is None else right + part[step], 1)
            if step <= far_left:
                ring[4] = shift(part[n_aux - step] if left is None else left + part[n_aux - step], -1)
    return [part[0] + right + left for part, _, _, right, left in rings]


def shift(value, by):
    n_aux = lax.axis_size("aux")
    return lax.ppermute(value, "aux", [(index, (index + by) % n_aux) for index in range(n_aux)])


def device_of(x, y, core):
    return (x % SIDE) * 2 * SIDE + (y % SIDE) * 2 + core % 2


def gather_perm(hop):
    return [
        (device_of(x, y, core), device_of(x + hop, y, 0) if core == 0 else device_of(x, y + hop, 1))
        for x in range(SIDE)
        for y in range(SIDE)
        for core in range(2)
    ]


def spread_perm(hop, flip):
    return [
        (
            device_of(x, y, core),
            device_of(x, y + hop, flip) if core == 0 else device_of(x + hop, y, 1 - flip),
        )
        for x in range(SIDE)
        for y in range(SIDE)
        for core in range(2)
    ]


def plan(domains, own, pairs_dev, blocks_dev, n_pair):
    table = domains.reshape(n_pair, pairs_dev * domains.shape[1])
    slots_dev = table.shape[1]
    x, y, core = own // (2 * SIDE), (own // 2) % SIDE, own % 2
    first = core == 0
    hops = jnp.arange(SIDE, dtype=jnp.int32)
    flips = jnp.arange(2, dtype=jnp.int32)
    source = jnp.where(first, device_of(x - hops, y, 0), device_of(x, y - hops, 1))
    target = jnp.where(
        first,
        device_of(x, y + hops[:, None], flips[None, :]),
        device_of(x + hops[:, None], y, 1 - flips[None, :]),
    ).reshape(2 * SIDE)

    owner, local = table // blocks_dev, table % blocks_dev
    earlier = jnp.tril(jnp.ones((slots_dev, slots_dev), jnp.bool_), -1)
    rank = jnp.sum(((owner[:, :, None] == owner[:, None, :]) & earlier[None]).astype(jnp.int32), axis=2)

    packed = (owner * CAP + rank) * blocks_dev + local
    chosen = jnp.concatenate([target, own[None]])[:, None] == jnp.arange(n_pair, dtype=jnp.int32)[None, :]
    rows = jnp.sum(jnp.where(chosen[:, :, None], packed[None], 0), axis=1)
    key = rows // blocks_dev
    wanted = (source[:, None] * CAP + jnp.arange(CAP, dtype=jnp.int32)[None, :]).reshape(SIDE * CAP)
    hit = key[:-1, None, :] == wanted[None, :, None]
    send = jnp.sum(jnp.where(hit, rows[:-1, None, :] % blocks_dev, 0), axis=2)

    named, place = key[-1] // CAP, key[-1] % CAP
    back_x, back_y = (x - named // (2 * SIDE)) % SIDE, (y - (named // 2) % SIDE) % SIDE
    sent_first = named % 2 == 0
    gathered = jnp.where(sent_first, back_x, back_y)
    spread = jnp.where(sent_first, back_y, back_x)
    flip = jnp.where(sent_first, core, 1 - core)
    where = ((spread * 2 + flip) * SIDE + gathered) * CAP + place
    arrives = where[None, :] == jnp.arange(2 * SIDE * SIDE * CAP, dtype=jnp.int32)[:, None]
    goes = jnp.sum(jnp.where(arrives, 1 + jnp.arange(slots_dev, dtype=jnp.int32)[None, :], 0), axis=1) - 1
    return send.reshape(-1), goes


def per_device(b_three, metric, aux_map, domains, counts):
    rows_dev, aux_dev = b_three.shape
    blocks_dev, _ = aux_map.shape
    width = rows_dev // blocks_dev
    n_pair = lax.axis_size("pair")
    n_aux = lax.axis_size("aux")
    own = lax.axis_index("pair")
    pairs_dev = counts.shape[0]
    domain_max = domains.shape[1]
    params = pltpu.CompilerParams(vmem_limit_bytes=VMEM_LIMIT)
    anywhere = pl.BlockSpec(memory_space=pl.ANY)

    place = lax.axis_index("aux").astype(jnp.int32).reshape(1)

    masked = pl.pallas_call(
        mask_kernel,
        out_shape=[jax.ShapeDtypeStruct((blocks * width, aux_dev), jnp.bfloat16) for blocks in CHUNKS],
        compiler_params=params,
        name="mask",
    )(aux_map, b_three)
    rings = ring_gather(masked)
    send, goes = plan(domains, own, pairs_dev, blocks_dev, n_pair)

    block_shape = (width, aux_dev)
    in_vmem = pl.BlockSpec(memory_space=pltpu.VMEM)
    orders = tuple(range(n_aux))
    ordered = pl.pallas_call(
        functools.partial(metric_kernel, orders),
        grid_spec=pltpu.PrefetchScalarGridSpec(
            num_scalar_prefetch=1,
            grid=(),
            in_specs=[anywhere],
            out_specs=in_vmem,
            scratch_shapes=[pltpu.SemaphoreType.DMA((n_aux,))],
        ),
        out_shape=jax.ShapeDtypeStruct((n_aux, aux_dev, aux_dev), jnp.bfloat16),
        compiler_params=params,
        name="order_metric",
    )(place, metric)
    sources = {}
    for index, (blocks, ring) in enumerate(zip(CHUNKS, rings)):
        fitted = pl.pallas_call(
            fit_kernel,
            in_specs=[in_vmem] * (n_aux + 1),
            out_specs=in_vmem,
            scratch_shapes=[pltpu.VMEM((blocks * width, aux_dev), jnp.float32)],
            out_shape=jax.ShapeDtypeStruct((blocks, *block_shape), jnp.bfloat16),
            compiler_params=params,
            name="fit",
        )(*[ring[hop] for hop in orders], ordered)
        sources[0, index] = fitted
        for hop in (1, 3, 2):
            sources[hop, index] = lax.ppermute(fitted, "pair", gather_perm(hop))

    messages, slots = 2 * SIDE, SIDE * CAP
    picked = pl.pallas_call(
        pick_kernel,
        grid_spec=pltpu.PrefetchScalarGridSpec(
            num_scalar_prefetch=1,
            grid=(),
            in_specs=[in_vmem] * (SIDE * len(CHUNKS)),
            out_specs=[in_vmem] * messages,
        ),
        out_shape=[jax.ShapeDtypeStruct((slots, *block_shape), jnp.bfloat16)] * messages,
        compiler_params=params,
        name="pick",
    )(send, *[sources[hop, index] for hop in range(SIDE) for index in range(len(CHUNKS))])

    arrived = {0: picked[0]}
    for hop, flip in ((1, 0), (3, 0), (1, 1), (3, 1), (2, 0), (2, 1), (0, 1)):
        message = hop * 2 + flip
        arrived[message] = lax.ppermute(picked[message], "pair", spread_perm(hop, flip))

    size = domain_max * width
    share = size // n_aux
    half = pairs_dev // 2
    partial_values = [
        pl.pallas_call(
            functools.partial(gram_kernel, first_pair, domain_max),
            grid_spec=pltpu.PrefetchScalarGridSpec(
                num_scalar_prefetch=3,
                grid=(),
                in_specs=[in_vmem] * messages,
                out_specs=in_vmem,
                scratch_shapes=[pltpu.VMEM((half * domain_max, *block_shape), jnp.bfloat16)],
            ),
            out_shape=jax.ShapeDtypeStruct((n_aux, half, share, size), jnp.float32),
            compiler_params=params,
            name="gram",
        )(goes, counts, place, *[arrived[message] for message in range(messages)])
        for first_pair in (0, half)
    ]
    return jnp.concatenate(ring_sum(partial_values), axis=0)


def solution(mesh):
    return jax.shard_map(
        per_device,
        mesh=mesh,
        in_specs=(P("pair", "aux"), P(None, "aux"), P("pair", "aux"), P(), P("pair")),
        out_specs=P("pair", "aux", None),
        check_vma=False,
    )
```

time: 161 us -> 146 us (0.907)
  waiting for transfers between devices: 63.4 us -> 52.9 us
  Pallas kernels: 21.2 us -> 11.5 us
  local copies, waits for them, and re-layouts: 6.16 us -> 8.72 us
    ppermute x28, waiting for transfers between devices: 35.6 us -> 26 us  [shift(): lax.ppermute(value, 'aux', [(index, (index + by) % n_aux) for index in ra...]
    pallas_call x3 -> x5, Pallas kernels: 14.6 us -> 7.75 us  [the longest x2 3.7 us: per_device(): pl.pallas_call(fit_kernel, in_specs=[in_vmem] * (n_aux + 1), out_specs=in...]
    unnamed x11 -> x27, local copies, waits for them, and re-layouts: 4.75 us -> 8.32 us
    pallas_call x1, Pallas kernels: 6.49 us -> 3.55 us  [per_device(): pl.pallas_call(pick_kernel, grid_spec=pltpu.PrefetchScalarGridSpec(num_sc...]
    ppermute x7, starting transfers between devices: 12.6 us -> 9.67 us  [per_device(): lax.ppermute(picked[message], 'pair', spread_perm(hop, flip))]
    ppermute x28, starting transfers between devices: 45.7 us -> 48.3 us  [shift(): lax.ppermute(value, 'aux', [(index, (index + by) % n_aux) for index in ra...]
    ppermute x6, waiting for transfers between devices: 9.93 us -> 7.46 us  [per_device(): sources[hop, index] = lax.ppermute(fitted, 'pair', gather_perm(hop))]
    ppermute x7, waiting for transfers between devices: 17.9 us -> 19.5 us  [per_device(): lax.ppermute(picked[message], 'pair', spread_perm(hop, flip))]
  transfers between devices with their start and end apart: 41 -> 41, of which waited for: 18 -> 21; matrix products, arithmetic and copies ran while one was open for 3% -> 3% of each run, Pallas kernels for 5% -> 4%
where the time goes in v4:
time: 146 us; the launch traced here: 144 us
  starting transfers between devices  66.3 us (45%)
  waiting for transfers between devices  52.9 us (36%)
  Pallas kernels  11.5 us (8%)
  local copies, waits for them, and re-layouts  8.72 us (6%)
  other arithmetic  4.07 us (3%)
    ppermute x28, starting transfers between devices, shift(): lax.ppermute(value, 'aux', [(index, (index + by) % n_aux) for index in ra...  48.3 us
    ppermute x28, waiting for transfers between devices, shift(): lax.ppermute(value, 'aux', [(index, (index + by) % n_aux) for index in ra...  26 us
    ppermute x7, waiting for transfers between devices, per_device(): lax.ppermute(picked[message], 'pair', spread_perm(hop, flip))  19.5 us
    ppermute x7, starting transfers between devices, per_device(): lax.ppermute(picked[message], 'pair', spread_perm(hop, flip))  9.67 us
    ppermute x6, starting transfers between devices, per_device(): sources[hop, index] = lax.ppermute(fitted, 'pair', gather_perm(hop))  8.41 us
    unnamed x27, local copies, waits for them, and re-layouts  8.32 us
    ppermute x6, waiting for transfers between devices, per_device(): sources[hop, index] = lax.ppermute(fitted, 'pair', gather_perm(hop))  7.46 us
    pallas_call x2, Pallas kernels, per_device(): pl.pallas_call(fit_kernel, in_specs=[in_vmem] * (n_aux + 1), out_specs=in...  3.7 us
  transfers between devices with their start and end apart: 41, of which 21 were waited for; matrix products, arithmetic and copies ran while one was open for 3% of the time, Pallas kernels for 4%

profile of v4, /device:TPU:2, one launch (start us, length us, event | category | flops | bytes accessed | tf_op | source)
XLA Modules:
  0.0 144.0 jit_solution(9457432240870365715)
XLA Ops:
  3.9 4.0 %collective-permute-start.4 = (bf16[320,512]{1,0:T(8,128)(2,1)S(1)}, bf16[320,512]{1,0:T(8,128)(2,1)S(1)}, u32[]{:S(2)}, u32[]{:S(2)}) collective-permute-start(bf16[320,512]{1,0:T(8,128)(2,1)S(1)} %get-tuple-element.15.refs_0_), channel_id=1, source_target_pairs={{0,224},{32,0},{64,32},{96,64},{128,96},{160,128},{192,160},{224,1... | collective-permute-start | bytes 983048 | tf_op jit(solution)/shard_map/ppermute | solution.py:141
  7.9 3.2 %collective-permute-start.10 = (bf16[192,512]{1,0:T(8,128)(2,1)S(1)}, bf16[192,512]{1,0:T(8,128)(2,1)S(1)}, u32[]{:S(2)}, u32[]{:S(2)}) collective-permute-start(bf16[192,512]{1,0:T(8,128)(2,1)S(1)} %get-tuple-element.16.refs_0_), channel_id=1, source_target_pairs={{0,224},{32,0},{64,32},{96,64},{128,96},{160,128},{192,160},{224,1... | collective-permute-start | bytes 589832 | tf_op jit(solution)/shard_map/ppermute | solution.py:141
  16.4 2.7 %collective-permute-done.10.refs_7_ = bf16[192,512]{1,0:T(8,128)(2,1)S(1)} collective-permute-done((bf16[192,512]{1,0:T(8,128)(2,1)S(1)}, bf16[192,512]{1,0:T(8,128)(2,1)S(1)}, u32[]{:S(2)}, u32[]{:S(2)}) %collective-permute-start.10) | collective-permute-done | bytes 196640 | tf_op jit(solution)/shard_map/ppermute | solution.py:141
  19.1 3.7 %collective-permute-start.11 = (bf16[192,512]{1,0:T(8,128)(2,1)S(1)}, bf16[192,512]{1,0:T(8,128)(2,1)S(1)}, u32[]{:S(2)}, u32[]{:S(2)}) collective-permute-start(bf16[192,512]{1,0:T(8,128)(2,1)S(1)} %collective-permute-done.10.refs_7_), channel_id=1, source_target_pairs={{0,224},{32,0},{64,32},{96,64},{128,96},{160,128},{192,160},{224,1... | collective-permute-start | bytes 589832 | tf_op jit(solution)/shard_map/ppermute | solution.py:141
  22.9 3.2 %collective-permute-start.5 = (bf16[320,512]{1,0:T(8,128)(2,1)S(1)}, bf16[320,512]{1,0:T(8,128)(2,1)S(1)}, u32[]{:S(2)}, u32[]{:S(2)}) collective-permute-start(bf16[320,512]{1,0:T(8,128)(2,1)S(1)} %collective-permute-done.4.refs_7_), channel_id=1, source_target_pairs={{0,224},{32,0},{64,32},{96,64},{128,96},{160,128},{192,160},{224,1... | collective-permute-start | bytes 983048 | tf_op jit(solution)/shard_map/ppermute | solution.py:141
  27.5 3.7 %collective-permute-start.12 = (bf16[192,512]{1,0:T(8,128)(2,1)S(1)}, bf16[192,512]{1,0:T(8,128)(2,1)}, u32[]{:S(2)}, u32[]{:S(2)}) collective-permute-start(bf16[192,512]{1,0:T(8,128)(2,1)S(1)} %collective-permute-done.11.refs_6_), channel_id=1, source_target_pairs={{0,224},{32,0},{64,32},{96,64},{128,96},{160,128},{192,160},{224,1... | collective-permute-start | bytes 589832 | tf_op jit(solution)/shard_map/ppermute | solution.py:141
  31.5 5.8 %collective-permute-done.12.refs_5_ = bf16[192,512]{1,0:T(8,128)(2,1)} collective-permute-done((bf16[192,512]{1,0:T(8,128)(2,1)S(1)}, bf16[192,512]{1,0:T(8,128)(2,1)}, u32[]{:S(2)}, u32[]{:S(2)}) %collective-permute-start.12) | collective-permute-done | bytes 196640 | tf_op jit(solution)/shard_map/ppermute | solution.py:141
  37.3 3.8 %collective-permute-start.13 = (bf16[192,512]{1,0:T(8,128)(2,1)}, bf16[192,512]{1,0:T(8,128)(2,1)}, u32[]{:S(2)}, u32[]{:S(2)}) collective-permute-start(bf16[192,512]{1,0:T(8,128)(2,1)} %collective-permute-done.12.refs_5_), channel_id=1, source_target_pairs={{0,224},{32,0},{64,32},{96,64},{128,96},{160,128},{192,160},{224,1... | collective-permute-start | bytes 589832 | tf_op jit(solution)/shard_map/ppermute | solution.py:141
  57.0 3.5 %collective-permute-start.16 = (bf16[5,64,512]{2,1,0:T(8,128)(2,1)S(1)}, bf16[5,64,512]{2,1,0:T(8,128)(2,1)S(1)}, u32[]{:S(2)}, u32[]{:S(2)}) collective-permute-start(bf16[5,64,512]{2,1,0:T(8,128)(2,1)S(1)} %fit.2.refs_0_), channel_id=1, source_target_pairs={{0,16},{1,5},{2,18},{3,7},{4,20},{5,1},{6,22},{7,3},{8,24},{9,13},... | collective-permute-start | bytes 983048 | tf_op jit(solution)/shard_map/ppermute | solution.py:259
  65.7 3.4 %collective-permute-done.18.refs_6_ = bf16[5,64,512]{2,1,0:T(8,128)(2,1)S(1)} collective-permute-done((bf16[5,64,512]{2,1,0:T(8,128)(2,1)S(1)}, bf16[5,64,512]{2,1,0:T(8,128)(2,1)S(1)}, u32[]{:S(2)}, u32[]{:S(2)}) %collective-permute-start.18) | collective-permute-done | bytes 327712 | tf_op jit(solution)/shard_map/ppermute | solution.py:259
  70.1 3.5 %pick.1 = (bf16[8,64,512]{2,1,0:T(8,128)(2,1)S(1)}, bf16[8,64,512]{2,1,0:T(8,128)(2,1)}, bf16[8,64,512]{2,1,0:T(8,128)(2,1)}, bf16[8,64,512]{2,1,0:T(8,128)(2,1)...) custom-call(s32[64]{0:T(128)S(1)} %reshape.316.send_ref, ...), custom_call_target="tpu_custom_call" | custom-call | tf_op jit(solution)/shard_map/pick/pallas_call | solution.py:262
  76.4 2.9 %collective-permute-start.23 = (bf16[8,64,512]{2,1,0:T(8,128)(2,1)}, bf16[8,64,512]{2,1,0:T(8,128)(2,1)S(1)}, u32[]{:S(2)}, u32[]{:S(2)}) collective-permute-start(bf16[8,64,512]{2,1,0:T(8,128)(2,1)} %copy-done.9), channel_id=1, source_target_pairs={{0,4},{1,17},{2,6},{3,19},{4,0},{5,21},{6,2},{7,23},{8,12},{9,25},... | collective-permute-start | bytes 1572872 | tf_op jit(solution)/shard_map/ppermute | solution.py:278
  79.3 3.4 %collective-permute-start.24 = (bf16[8,64,512]{2,1,0:T(8,128)(2,1)}, bf16[8,64,512]{2,1,0:T(8,128)(2,1)S(1)}, u32[]{:S(2)}, u32[]{:S(2)}) collective-permute-start(bf16[8,64,512]{2,1,0:T(8,128)(2,1)} %copy-done.8), channel_id=1, source_target_pairs={{0,5},{1,16},{2,7},{3,18},{4,1},{5,20},{6,3},{7,22},{8,13},{9,24},... | collective-permute-start | bytes 1572872 | tf_op jit(solution)/shard_map/ppermute | solution.py:278
  85.8 3.2 %collective-permute-done.22.refs_3_ = bf16[8,64,512]{2,1,0:T(8,128)(2,1)S(1)} collective-permute-done((bf16[8,64,512]{2,1,0:T(8,128)(2,1)}, bf16[8,64,512]{2,1,0:T(8,128)(2,1)S(1)}, u32[]{:S(2)}, u32[]{:S(2)}) %collective-permute-start.22) | collective-permute-done | bytes 524320 | tf_op jit(solution)/shard_map/ppermute | solution.py:278
  89.0 8.9 %collective-permute-done.23.refs_4_ = bf16[8,64,512]{2,1,0:T(8,128)(2,1)S(1)} collective-permute-done((bf16[8,64,512]{2,1,0:T(8,128)(2,1)}, bf16[8,64,512]{2,1,0:T(8,128)(2,1)S(1)}, u32[]{:S(2)}, u32[]{:S(2)}) %collective-permute-start.23) | collective-permute-done | bytes 524320 | tf_op jit(solution)/shard_map/ppermute | solution.py:278
  100.3 3.7 %collective-permute-done.26.refs_7_ = bf16[8,64,512]{2,1,0:T(8,128)(2,1)S(1)} collective-permute-done((bf16[8,64,512]{2,1,0:T(8,128)(2,1)S(1)}, bf16[8,64,512]{2,1,0:T(8,128)(2,1)S(1)}, u32[]{:S(2)}, u32[]{:S(2)}) %collective-permute-start.26) | collective-permute-done | bytes 524320 | tf_op jit(solution)/shard_map/ppermute | solution.py:278
  106.1 3.8 %collective-permute-start.37 = (f32[5,32,256]{2,1,0:T(8,128)S(1)}, f32[5,32,256]{2,1,0:T(8,128)S(1)}, u32[]{:S(2)}, u32[]{:S(2)}) collective-permute-start(f32[5,32,256]{2,1,0:T(8,128)S(1)} %get-tuple-element.36), channel_id=1, source_target_pairs={{0,224},{32,0},{64,32},{96,64},{128,96},{160,128},{192,160},{224,1... | collective-permute-start | bytes 491528 | tf_op jit(solution)/shard_map/ppermute | solution.py:141
  111.7 3.2 %collective-permute-start.31 = (f32[5,32,256]{2,1,0:T(8,128)S(1)}, f32[5,32,256]{2,1,0:T(8,128)S(1)}, u32[]{:S(2)}, u32[]{:S(2)}) collective-permute-start(f32[5,32,256]{2,1,0:T(8,128)S(1)} %get-tuple-element.30), channel_id=1, source_target_pairs={{0,224},{32,0},{64,32},{96,64},{128,96},{160,128},{192,160},{224,1... | collective-permute-start | bytes 491528 | tf_op jit(solution)/shard_map/ppermute | solution.py:141
  118.4 2.6 %collective-permute-done.38 = f32[5,32,256]{2,1,0:T(8,128)S(1)} collective-permute-done((f32[5,32,256]{2,1,0:T(8,128)S(1)}, f32[5,32,256]{2,1,0:T(8,128)S(1)}, u32[]{:S(2)}, u32[]{:S(2)}) %collective-permute-start.38) | collective-permute-done | bytes 163872 | tf_op jit(solution)/shard_map/ppermute | solution.py:141
  126.2 3.2 %collective-permute-start.32 = (f32[5,32,256]{2,1,0:T(8,128)S(1)}, f32[5,32,256]{2,1,0:T(8,128)S(1)}, u32[]{:S(2)}, u32[]{:S(2)}) collective-permute-start(f32[5,32,256]{2,1,0:T(8,128)S(1)} %get-tuple-element.28), channel_id=1, source_target_pairs={{0,224},{32,0},{64,32},{96,64},{128,96},{160,128},{192,160},{224,1... | collective-permute-start | bytes 491528 | tf_op jit(solution)/shard_map/ppermute | solution.py:141
  129.9 3.3 %collective-permute-start.40 = (f32[5,32,256]{2,1,0:T(8,128)S(1)}, f32[5,32,256]{2,1,0:T(8,128)S(1)}, u32[]{:S(2)}, u32[]{:S(2)}) collective-permute-start(f32[5,32,256]{2,1,0:T(8,128)S(1)} %get-tuple-element.32), channel_id=1, source_target_pairs={{0,224},{32,0},{64,32},{96,64},{128,96},{160,128},{192,160},{224,1... | collective-permute-start | bytes 491528 | tf_op jit(solution)/shard_map/ppermute | solution.py:141
  133.7 3.0 %collective-permute-start.33 = (f32[5,32,256]{2,1,0:T(8,128)S(1)}, f32[5,32,256]{2,1,0:T(8,128)S(1)}, u32[]{:S(2)}, u32[]{:S(2)}) collective-permute-start(f32[5,32,256]{2,1,0:T(8,128)S(1)} %get-tuple-element.26), channel_id=1, source_target_pairs={{0,224},{32,0},{64,32},{96,64},{128,96},{160,128},{192,160},{224,1... | collective-permute-start | bytes 491528 | tf_op jit(solution)/shard_map/ppermute | solution.py:141
  136.7 3.4 %collective-permute-done.36 = f32[5,32,256]{2,1,0:T(8,128)S(1)} collective-permute-done((f32[5,32,256]{2,1,0:T(8,128)S(1)}, f32[5,32,256]{2,1,0:T(8,128)S(1)}, u32[]{:S(2)}, u32[]{:S(2)}) %collective-permute-start.36) | collective-permute-done | bytes 163872 | tf_op jit(solution)/shard_map/ppermute | solution.py:141
  140.2 3.0 %collective-permute-done.30 = f32[5,32,256]{2,1,0:T(8,128)S(1)} collective-permute-done((f32[5,32,256]{2,1,0:T(8,128)S(1)}, f32[5,32,256]{2,1,0:T(8,128)S(1)}, u32[]{:S(2)}, u32[]{:S(2)}) %collective-permute-start.30) | collective-permute-done | bytes 163872 | tf_op jit(solution)/shard_map/ppermute | solution.py:141
  (128 shorter events, 55.4 us)
Async XLA Ops:
  1.9 14.5 %collective-permute-start = (bf16[320,512]{1,0:T(8,128)(2,1)S(1)}, bf16[320,512]{1,0:T(8,128)(2,1)S(1)}, u32[]{:S(2)}, u32[]{:S(2)}) collective-permute-start(bf16[320,512]{1,0:T(8,128)(2,1)S(1)} %get-tuple-element.15.refs_0_), channel_id=1, source_target_pairs={{0,32},{32,64},{64,96},{96,128},{128,160},{160,192},{192,224},{224... | collective-permute-start | bytes 983048 | tf_op jit(solution)/shard_map/ppermute | solution.py:141
  3.9 19.0 %collective-permute-start.4 = (bf16[320,512]{1,0:T(8,128)(2,1)S(1)}, bf16[320,512]{1,0:T(8,128)(2,1)S(1)}, u32[]{:S(2)}, u32[]{:S(2)}) collective-permute-start(bf16[320,512]{1,0:T(8,128)(2,1)S(1)} %get-tuple-element.15.refs_0_), channel_id=1, source_target_pairs={{0,224},{32,0},{64,32},{96,64},{128,96},{160,128},{192,160},{224,1... | collective-permute-start | bytes 983048 | tf_op jit(solution)/shard_map/ppermute | solution.py:141
  7.9 14.9 %collective-permute-start.7 = (bf16[192,512]{1,0:T(8,128)(2,1)S(1)}, bf16[192,512]{1,0:T(8,128)(2,1)S(1)}, u32[]{:S(2)}, u32[]{:S(2)}) collective-permute-start(bf16[192,512]{1,0:T(8,128)(2,1)S(1)} %get-tuple-element.16.refs_0_), channel_id=1, source_target_pairs={{0,32},{32,64},{64,96},{96,128},{128,160},{160,192},{192,224},{224... | collective-permute-start | bytes 589832 | tf_op jit(solution)/shard_map/ppermute | solution.py:141
  7.9 11.2 %collective-permute-start.10 = (bf16[192,512]{1,0:T(8,128)(2,1)S(1)}, bf16[192,512]{1,0:T(8,128)(2,1)S(1)}, u32[]{:S(2)}, u32[]{:S(2)}) collective-permute-start(bf16[192,512]{1,0:T(8,128)(2,1)S(1)} %get-tuple-element.16.refs_0_), channel_id=1, source_target_pairs={{0,224},{32,0},{64,32},{96,64},{128,96},{160,128},{192,160},{224,1... | collective-permute-start | bytes 589832 | tf_op jit(solution)/shard_map/ppermute | solution.py:141
  16.4 14.9 %collective-permute-start.1 = (bf16[320,512]{1,0:T(8,128)(2,1)S(1)}, bf16[320,512]{1,0:T(8,128)(2,1)S(1)}, u32[]{:S(2)}, u32[]{:S(2)}) collective-permute-start(bf16[320,512]{1,0:T(8,128)(2,1)S(1)} %collective-permute-done.refs_1_), channel_id=1, source_target_pairs={{0,32},{32,64},{64,96},{96,128},{128,160},{160,192},{192,224},{224... | collective-permute-start | bytes 983048 | tf_op jit(solution)/shard_map/ppermute | solution.py:141
  22.9 18.2 %collective-permute-start.5 = (bf16[320,512]{1,0:T(8,128)(2,1)S(1)}, bf16[320,512]{1,0:T(8,128)(2,1)S(1)}, u32[]{:S(2)}, u32[]{:S(2)}) collective-permute-start(bf16[320,512]{1,0:T(8,128)(2,1)S(1)} %collective-permute-done.4.refs_7_), channel_id=1, source_target_pairs={{0,224},{32,0},{64,32},{96,64},{128,96},{160,128},{192,160},{224,1... | collective-permute-start | bytes 983048 | tf_op jit(solution)/shard_map/ppermute | solution.py:141
  27.5 9.8 %collective-permute-start.12 = (bf16[192,512]{1,0:T(8,128)(2,1)S(1)}, bf16[192,512]{1,0:T(8,128)(2,1)}, u32[]{:S(2)}, u32[]{:S(2)}) collective-permute-start(bf16[192,512]{1,0:T(8,128)(2,1)S(1)} %collective-permute-done.11.refs_6_), channel_id=1, source_target_pairs={{0,224},{32,0},{64,32},{96,64},{128,96},{160,128},{192,160},{224,1... | collective-permute-start | bytes 589832 | tf_op jit(solution)/shard_map/ppermute | solution.py:141
  31.2 9.9 %collective-permute-start.2 = (bf16[320,512]{1,0:T(8,128)(2,1)S(1)}, bf16[320,512]{1,0:T(8,128)(2,1)S(1)}, u32[]{:S(2)}, u32[]{:S(2)}) collective-permute-start(bf16[320,512]{1,0:T(8,128)(2,1)S(1)} %collective-permute-done.1.refs_2_), channel_id=1, source_target_pairs={{0,32},{32,64},{64,96},{96,128},{128,160},{160,192},{192,224},{224... | collective-permute-start | bytes 983048 | tf_op jit(solution)/shard_map/ppermute | solution.py:141
  31.4 14.3 %collective-permute-start.9 = (bf16[192,512]{1,0:T(8,128)(2,1)}, bf16[192,512]{1,0:T(8,128)(2,1)}, u32[]{:S(2)}, u32[]{:S(2)}) collective-permute-start(bf16[192,512]{1,0:T(8,128)(2,1)} %collective-permute-done.8.refs_2_), channel_id=1, source_target_pairs={{0,32},{32,64},{64,96},{96,128},{128,160},{160,192},{192,224},{224... | collective-permute-start | bytes 589832 | tf_op jit(solution)/shard_map/ppermute | solution.py:141
  37.3 9.5 %collective-permute-start.13 = (bf16[192,512]{1,0:T(8,128)(2,1)}, bf16[192,512]{1,0:T(8,128)(2,1)}, u32[]{:S(2)}, u32[]{:S(2)}) collective-permute-start(bf16[192,512]{1,0:T(8,128)(2,1)} %collective-permute-done.12.refs_5_), channel_id=1, source_target_pairs={{0,224},{32,0},{64,32},{96,64},{128,96},{160,128},{192,160},{224,1... | collective-permute-start | bytes 589832 | tf_op jit(solution)/shard_map/ppermute | solution.py:141
  41.1 14.2 %collective-permute-start.6 = (bf16[320,512]{1,0:T(8,128)(2,1)S(1)}, bf16[320,512]{1,0:T(8,128)(2,1)S(1)}, u32[]{:S(2)}, u32[]{:S(2)}) collective-permute-start(bf16[320,512]{1,0:T(8,128)(2,1)S(1)} %collective-permute-done.5.refs_6_), channel_id=1, source_target_pairs={{0,224},{32,0},{64,32},{96,64},{128,96},{160,128},{192,160},{224,1... | collective-permute-start | bytes 983048 | tf_op jit(solution)/shard_map/ppermute | solution.py:141
  41.2 14.2 %collective-permute-start.3 = (bf16[320,512]{1,0:T(8,128)(2,1)S(1)}, bf16[320,512]{1,0:T(8,128)(2,1)S(1)}, u32[]{:S(2)}, u32[]{:S(2)}) collective-permute-start(bf16[320,512]{1,0:T(8,128)(2,1)S(1)} %collective-permute-done.2.refs_3_), channel_id=1, source_target_pairs={{0,32},{32,64},{64,96},{96,128},{128,160},{160,192},{192,224},{224... | collective-permute-start | bytes 983048 | tf_op jit(solution)/shard_map/ppermute | solution.py:141
  49.9 10.6 %collective-permute-start.15 = (bf16[3,64,512]{2,1,0:T(8,128)(2,1)S(1)}, bf16[3,64,512]{2,1,0:T(8,128)(2,1)S(1)}, u32[]{:S(2)}, u32[]{:S(2)}) collective-permute-start(bf16[3,64,512]{2,1,0:T(8,128)(2,1)S(1)} %fit.3.refs_1_), channel_id=1, source_target_pairs={{0,8},{1,3},{2,10},{3,5},{4,12},{5,7},{6,14},{7,1},{8,16},{9,11},{... | collective-permute-start | bytes 589832 | tf_op jit(solution)/shard_map/ppermute | solution.py:259
  52.1 8.9 %collective-permute-start.17 = (bf16[3,64,512]{2,1,0:T(8,128)(2,1)S(1)}, bf16[3,64,512]{2,1,0:T(8,128)(2,1)S(1)}, u32[]{:S(2)}, u32[]{:S(2)}) collective-permute-start(bf16[3,64,512]{2,1,0:T(8,128)(2,1)S(1)} %fit.3.refs_1_), channel_id=1, source_target_pairs={{0,16},{1,5},{2,18},{3,7},{4,20},{5,1},{6,22},{7,3},{8,24},{9,13},... | collective-permute-start | bytes 589832 | tf_op jit(solution)/shard_map/ppermute | solution.py:259
  73.6 9.1 %collective-permute-start.20 = (bf16[8,64,512]{2,1,0:T(8,128)(2,1)}, bf16[8,64,512]{2,1,0:T(8,128)(2,1)S(1)}, u32[]{:S(2)}, u32[]{:S(2)}) collective-permute-start(bf16[8,64,512]{2,1,0:T(8,128)(2,1)} %get-tuple-element.18), channel_id=1, source_target_pairs={{0,1},{1,0},{2,3},{3,2},{4,5},{5,4},{6,7},{7,6},{8,9},{9,8},{10,11... | collective-permute-start | bytes 1572872 | tf_op jit(solution)/shard_map/ppermute | solution.py:278
  74.8 10.6 %collective-permute-start.21 = (bf16[8,64,512]{2,1,0:T(8,128)(2,1)}, bf16[8,64,512]{2,1,0:T(8,128)(2,1)S(1)}, u32[]{:S(2)}, u32[]{:S(2)}) collective-permute-start(bf16[8,64,512]{2,1,0:T(8,128)(2,1)} %get-tuple-element.19), channel_id=1, source_target_pairs={{0,2},{1,9},{2,4},{3,11},{4,6},{5,13},{6,0},{7,15},{8,10},{9,17},{... | collective-permute-start | bytes 1572872 | tf_op jit(solution)/shard_map/ppermute | solution.py:278
  76.4 12.6 %collective-permute-start.22 = (bf16[8,64,512]{2,1,0:T(8,128)(2,1)}, bf16[8,64,512]{2,1,0:T(8,128)(2,1)S(1)}, u32[]{:S(2)}, u32[]{:S(2)}) collective-permute-start(bf16[8,64,512]{2,1,0:T(8,128)(2,1)} %copy-done.10), channel_id=1, source_target_pairs={{0,3},{1,8},{2,5},{3,10},{4,7},{5,12},{6,1},{7,14},{8,11},{9,16},{... | collective-permute-start | bytes 1572872 | tf_op jit(solution)/shard_map/ppermute | solution.py:278
  76.4 21.5 %collective-permute-start.23 = (bf16[8,64,512]{2,1,0:T(8,128)(2,1)}, bf16[8,64,512]{2,1,0:T(8,128)(2,1)S(1)}, u32[]{:S(2)}, u32[]{:S(2)}) collective-permute-start(bf16[8,64,512]{2,1,0:T(8,128)(2,1)} %copy-done.9), channel_id=1, source_target_pairs={{0,4},{1,17},{2,6},{3,19},{4,0},{5,21},{6,2},{7,23},{8,12},{9,25},... | collective-permute-start | bytes 1572872 | tf_op jit(solution)/shard_map/ppermute | solution.py:278
  79.3 21.0 %collective-permute-start.24 = (bf16[8,64,512]{2,1,0:T(8,128)(2,1)}, bf16[8,64,512]{2,1,0:T(8,128)(2,1)S(1)}, u32[]{:S(2)}, u32[]{:S(2)}) collective-permute-start(bf16[8,64,512]{2,1,0:T(8,128)(2,1)} %copy-done.8), channel_id=1, source_target_pairs={{0,5},{1,16},{2,7},{3,18},{4,1},{5,20},{6,3},{7,22},{8,13},{9,24},... | collective-permute-start | bytes 1572872 | tf_op jit(solution)/shard_map/ppermute | solution.py:278
  82.7 17.6 %collective-permute-start.25 = (bf16[8,64,512]{2,1,0:T(8,128)(2,1)S(1)}, bf16[8,64,512]{2,1,0:T(8,128)(2,1)S(1)}, u32[]{:S(2)}, u32[]{:S(2)}) collective-permute-start(bf16[8,64,512]{2,1,0:T(8,128)(2,1)S(1)} %get-tuple-element.23), channel_id=1, source_target_pairs={{0,6},{1,25},{2,0},{3,27},{4,2},{5,29},{6,4},{7,31},{8,14},{9,1},{... | collective-permute-start | bytes 1572872 | tf_op jit(solution)/shard_map/ppermute | solution.py:278
  85.4 18.6 %collective-permute-start.26 = (bf16[8,64,512]{2,1,0:T(8,128)(2,1)S(1)}, bf16[8,64,512]{2,1,0:T(8,128)(2,1)S(1)}, u32[]{:S(2)}, u32[]{:S(2)}) collective-permute-start(bf16[8,64,512]{2,1,0:T(8,128)(2,1)S(1)} %get-tuple-element.24), channel_id=1, source_target_pairs={{0,7},{1,24},{2,1},{3,26},{4,3},{5,28},{6,5},{7,30},{8,15},{9,0},{... | collective-permute-start | bytes 1572872 | tf_op jit(solution)/shard_map/ppermute | solution.py:278
  106.0 12.3 %collective-permute-start.34 = (f32[5,32,256]{2,1,0:T(8,128)S(1)}, f32[5,32,256]{2,1,0:T(8,128)S(1)}, u32[]{:S(2)}, u32[]{:S(2)}) collective-permute-start(f32[5,32,256]{2,1,0:T(8,128)S(1)} %get-tuple-element.35), channel_id=1, source_target_pairs={{0,32},{32,64},{64,96},{96,128},{128,160},{160,192},{192,224},{224... | collective-permute-start | bytes 491528 | tf_op jit(solution)/shard_map/ppermute | solution.py:141
  111.7 13.1 %collective-permute-start.31 = (f32[5,32,256]{2,1,0:T(8,128)S(1)}, f32[5,32,256]{2,1,0:T(8,128)S(1)}, u32[]{:S(2)}, u32[]{:S(2)}) collective-permute-start(f32[5,32,256]{2,1,0:T(8,128)S(1)} %get-tuple-element.30), channel_id=1, source_target_pairs={{0,224},{32,0},{64,32},{96,64},{128,96},{160,128},{192,160},{224,1... | collective-permute-start | bytes 491528 | tf_op jit(solution)/shard_map/ppermute | solution.py:141
  121.0 8.8 %collective-permute-start.35 = (f32[5,32,256]{2,1,0:T(8,128)S(1)}, f32[5,32,256]{2,1,0:T(8,128)S(1)}, u32[]{:S(2)}, u32[]{:S(2)}) collective-permute-start(f32[5,32,256]{2,1,0:T(8,128)S(1)} %get-tuple-element.33), channel_id=1, source_target_pairs={{0,32},{32,64},{64,96},{96,128},{128,160},{160,192},{192,224},{224... | collective-permute-start | bytes 491528 | tf_op jit(solution)/shard_map/ppermute | solution.py:141
  (30 other events, 219.6 us)

commit v5 on v4

--- a/solution.py
+++ b/solution.py
@@ -7,13 +7,22 @@
 from jax.experimental.pallas import tpu as pltpu
 from jax.sharding import PartitionSpec as P
 
-VMEM_LIMIT = 16 * 1024 * 1024
+VMEM_LIMIT = 12 * 1024 * 1024
 CHUNKS = (5, 3)
 SIDE = 4
+GATHER_HOPS = (1, 3, 2, 0)
+SPREAD_ORDER = ((1, 0), (3, 0), (2, 0), (1, 1), (3, 1), (2, 1), (0, 1), (0, 0))
+PICK_GROUP = 2
 CAP = 2
 
 
-def mask_kernel(map_ref, b_ref, *out_refs):
+def mask_kernel(map_hbm, b_hbm, *refs):
+    out_refs, map_ref, b_ref, sems = refs[:-3], refs[-3], refs[-2], refs[-1]
+    load_map = pltpu.make_async_copy(map_hbm, map_ref, sems.at[0])
+    load_b = pltpu.make_async_copy(b_hbm, b_ref, sems.at[1])
+    load_map.start()
+    load_b.start()
+    load_map.wait()
     blocks_dev, aux_blocks = map_ref.shape
     rows_dev, aux_dev = b_ref.shape
     width = rows_dev // blocks_dev
@@ -24,6 +33,7 @@
     ).astype(jnp.float32)
     keep = jnp.dot(map_ref[...].astype(jnp.float32), spread, preferred_element_type=jnp.float32)
     keep = keep.astype(jnp.bfloat16)
+    load_b.wait()
     block = 0
     for out_ref in out_refs:
         for start in range(0, out_ref.shape[0], width):
@@ -46,42 +56,55 @@
         load.wait()
 
 
-def fit_kernel(*refs):
-    pieces, w_ref, out_ref, total = refs[:-3], refs[-3], refs[-2], refs[-1]
-    for step, piece in enumerate(pieces):
-        part = jnp.dot(piece[...], w_ref[step], preferred_element_type=jnp.float32)
-        if step == 0:
-            total[...] = part
-        elif step < len(pieces) - 1:
-            total[...] += part
+def fit_kernel(hops, begun, *refs):
+    out_ref, total = refs[-2:]
+    start_ref = refs[0] if begun else None
+    pieces, w_ref = refs[int(begun) : -3], refs[-3]
+    row = 0
+    for chunk in range(len(pieces) // len(hops)):
+        rows = pieces[chunk * len(hops)].shape[0]
+        part = start_ref[row : row + rows, :] if begun else None
+        for step, hop in enumerate(hops):
+            term = jnp.dot(
+                pieces[chunk * len(hops) + step][...], w_ref[hop], preferred_element_type=jnp.float32
+            )
+            if part is None:
+                part = term
+            elif step == 0:
+                part = part + term
+            else:
+                part = total[:rows, :] + term
+            if step < len(hops) - 1:
+                total[:rows, :] = part
+        if begun:
+            width = out_ref.shape[1]
+            out_ref[row // width : (row + rows) // width] = part.astype(jnp.bfloat16).reshape(
+                rows // width, width, part.shape[1]
+            )
         else:
-            out_ref[...] = (total[...] + part).astype(jnp.bfloat16).reshape(out_ref.shape)
-
-
-def pick_kernel(send_ref, *refs):
-    count = SIDE * len(CHUNKS)
-    sources, outs = refs[:count], refs[count:]
-    slots = outs[0].shape[0]
-    for message, out in enumerate(outs):
+            out_ref[row : row + rows, :] = part
+        row += rows
+
+
+def pick_kernel(messages, send_ref, *refs):
+    sources, outs = refs[:SIDE], refs[SIDE:]
+    hop_of = {hop: index for index, hop in enumerate(GATHER_HOPS)}
+    for message, out in zip(messages, outs):
+        slots = out.shape[0]
         for slot in range(slots):
-            block = send_ref[message * slots + slot]
-            start = 0
-            for chunk, blocks in enumerate(CHUNKS):
-                source = sources[(slot // CAP) * len(CHUNKS) + chunk]
-
-                @pl.when((block >= start) & (block < start + blocks))
-                def _(out=out, slot=slot, source=source, index=block - start):
-                    out[slot] = source[index]
-
-                start += blocks
-
-
-def gram_kernel(first_pair, domain_max, goes_ref, counts_ref, own_ref, *refs):
+            out[slot] = sources[hop_of[slot // CAP]][send_ref[message * slots + slot]]
+
+
+def add_kernel(index, a_ref, part_ref, out_ref):
+    out_ref[...] = a_ref[...] + part_ref[index]
+
+
+def gram_kernel(first_pair, domain_max, order, goes_ref, counts_ref, own_ref, *refs):
     arrived, out_ref, stacks = refs[:-2], refs[-2], refs[-1]
     slots = arrived[0].shape[0]
     n_aux, pairs, share, size = out_ref.shape
     places, width, depth = stacks.shape
-    for message, source in enumerate(arrived):
+    for message, source in zip(order, arrived):
         for slot in range(slots):
             goes = goes_ref[message * slots + slot] - first_pair * domain_max
 
@@ -130,10 +153,22 @@
         for ring in rings:
             part, far_right, far_left, right, left = ring
             if step <= far_right:
-                ring[3] = shift(part[step] if right is None else right + part[step], 1)
+                ring[3] = shift(part[step] if right is None else add_term(right, part, step), 1)
             if step <= far_left:
-                ring[4] = shift(part[n_aux - step] if left is None else left + part[n_aux - step], -1)
+                ring[4] = shift(part[n_aux - step] if left is None else add_term(left, part, n_aux - step), -1)
     return [part[0] + right + left for part, _, _, right, left in rings]
+
+
+def add_term(moving, part, index):
+    in_vmem = pl.BlockSpec(memory_space=pltpu.VMEM)
+    return pl.pallas_call(
+        functools.partial(add_kernel, index),
+        in_specs=[in_vmem] * 2,
+        out_specs=in_vmem,
+        out_shape=jax.ShapeDtypeStruct(moving.shape, moving.dtype),
+        compiler_params=pltpu.CompilerParams(vmem_limit_bytes=VMEM_LIMIT),
+        name="add_term",
+    )(moving, part)
 
 
 def shift(value, by):
@@ -214,28 +249,34 @@
     pairs_dev = counts.shape[0]
     domain_max = domains.shape[1]
     params = pltpu.CompilerParams(vmem_limit_bytes=VMEM_LIMIT)
-    anywhere = pl.BlockSpec(memory_space=pl.ANY)
+    in_hbm = pl.BlockSpec(memory_space=pltpu.HBM)
+    in_vmem = pl.BlockSpec(memory_space=pltpu.VMEM)
 
     place = lax.axis_index("aux").astype(jnp.int32).reshape(1)
 
     masked = pl.pallas_call(
         mask_kernel,
+        in_specs=[in_hbm] * 2,
+        out_specs=[in_vmem] * len(CHUNKS),
+        scratch_shapes=[
+            pltpu.VMEM(aux_map.shape, jnp.int32),
+            pltpu.VMEM(b_three.shape, jnp.bfloat16),
+            pltpu.SemaphoreType.DMA((2,)),
+        ],
         out_shape=[jax.ShapeDtypeStruct((blocks * width, aux_dev), jnp.bfloat16) for blocks in CHUNKS],
         compiler_params=params,
         name="mask",
     )(aux_map, b_three)
-    rings = ring_gather(masked)
     send, goes = plan(domains, own, pairs_dev, blocks_dev, n_pair)
 
     block_shape = (width, aux_dev)
-    in_vmem = pl.BlockSpec(memory_space=pltpu.VMEM)
     orders = tuple(range(n_aux))
     ordered = pl.pallas_call(
         functools.partial(metric_kernel, orders),
         grid_spec=pltpu.PrefetchScalarGridSpec(
             num_scalar_prefetch=1,
             grid=(),
-            in_specs=[anywhere],
+            in_specs=[in_hbm],
             out_specs=in_vmem,
             scratch_shapes=[pltpu.SemaphoreType.DMA((n_aux,))],
         ),
@@ -243,46 +284,58 @@
         compiler_params=params,
         name="order_metric",
     )(place, metric)
-    sources = {}
-    for index, (blocks, ring) in enumerate(zip(CHUNKS, rings)):
-        fitted = pl.pallas_call(
-            fit_kernel,
-            in_specs=[in_vmem] * (n_aux + 1),
-            out_specs=in_vmem,
-            scratch_shapes=[pltpu.VMEM((blocks * width, aux_dev), jnp.float32)],
-            out_shape=jax.ShapeDtypeStruct((blocks, *block_shape), jnp.bfloat16),
+    rings = ring_gather(masked)
+    near = tuple(hop for hop in orders if min(hop, n_aux - hop) <= n_aux // 4)
+    far = tuple(hop for hop in orders if hop not in near)
+    begun = pl.pallas_call(
+        functools.partial(fit_kernel, near, False),
+        in_specs=[in_vmem] * (len(near) * len(CHUNKS) + 1),
+        out_specs=in_vmem,
+        scratch_shapes=[pltpu.VMEM((max(CHUNKS) * width, aux_dev), jnp.float32)],
+        out_shape=jax.ShapeDtypeStruct((rows_dev, aux_dev), jnp.float32),
+        compiler_params=params,
+        name="fit_near",
+    )(*[ring[hop] for ring in rings for hop in near], ordered)
+    fitted = pl.pallas_call(
+        functools.partial(fit_kernel, far, True),
+        in_specs=[in_vmem] * (len(far) * len(CHUNKS) + 2),
+        out_specs=in_vmem,
+        scratch_shapes=[pltpu.VMEM((max(CHUNKS) * width, aux_dev), jnp.float32)],
+        out_shape=jax.ShapeDtypeStruct((blocks_dev, *block_shape), jnp.bfloat16),
+        compiler_params=params,
+        name="fit_far",
+    )(begun, *[ring[hop] for ring in rings for hop in far], ordered)
+    sources = {hop: lax.ppermute(fitted, "pair", gather_perm(hop)) for hop in GATHER_HOPS if hop > 0}
+    sources[0] = fitted
+
+    messages, slots = 2 * SIDE, SIDE * CAP
+    order = tuple(hop * 2 + flip for hop, flip in SPREAD_ORDER)
+    picked = []
+    for start in range(0, messages, PICK_GROUP):
+        group = order[start : start + PICK_GROUP]
+        picked += pl.pallas_call(
+            functools.partial(pick_kernel, group),
+            grid_spec=pltpu.PrefetchScalarGridSpec(
+                num_scalar_prefetch=1,
+                grid=(),
+                in_specs=[in_vmem] * SIDE,
+                out_specs=[in_vmem] * len(group),
+            ),
+            out_shape=[jax.ShapeDtypeStruct((slots, *block_shape), jnp.bfloat16)] * len(group),
             compiler_params=params,
-            name="fit",
-        )(*[ring[hop] for hop in orders], ordered)
-        sources[0, index] = fitted
-        for hop in (1, 3, 2):
-            sources[hop, index] = lax.ppermute(fitted, "pair", gather_perm(hop))
-
-    messages, slots = 2 * SIDE, SIDE * CAP
-    picked = pl.pallas_call(
-        pick_kernel,
-        grid_spec=pltpu.PrefetchScalarGridSpec(
-            num_scalar_prefetch=1,
-            grid=(),
-            in_specs=[in_vmem] * (SIDE * len(CHUNKS)),
-            out_specs=[in_vmem] * messages,
-        ),
-        out_shape=[jax.ShapeDtypeStruct((slots, *block_shape), jnp.bfloat16)] * messages,
-        compiler_params=params,
-        name="pick",
-    )(send, *[sources[hop, index] for hop in range(SIDE) for index in range(len(CHUNKS))])
-
-    arrived = {0: picked[0]}
-    for hop, flip in ((1, 0), (3, 0), (1, 1), (3, 1), (2, 0), (2, 1), (0, 1)):
-        message = hop * 2 + flip
-        arrived[message] = lax.ppermute(picked[message], "pair", spread_perm(hop, flip))
+            name="pick",
+        )(send, *[sources[hop] for hop in GATHER_HOPS])
+    arrived = [
+        lax.ppermute(message, "pair", spread_perm(hop, flip)) if (hop, flip) != (0, 0) else message
+        for (hop, flip), message in zip(SPREAD_ORDER, picked)
+    ]
 
     size = domain_max * width
     share = size // n_aux
     half = pairs_dev // 2
     partial_values = [
         pl.pallas_call(
-            functools.partial(gram_kernel, first_pair, domain_max),
+            functools.partial(gram_kernel, first_pair, domain_max, order),
             grid_spec=pltpu.PrefetchScalarGridSpec(
                 num_scalar_prefetch=3,
                 grid=(),
@@ -293,7 +346,7 @@
             out_shape=jax.ShapeDtypeStruct((n_aux, half, share, size), jnp.float32),
             compiler_params=params,
             name="gram",
-        )(goes, counts, place, *[arrived[message] for message in range(messages)])
+        )(goes, counts, place, *arrived)
         for first_pair in (0, half)
     ]
     return jnp.concatenate(ring_sum(partial_values), axis=0)

time: 146 us -> 136 us (0.932)
  starting transfers between devices: 66.3 us -> 52.2 us
  waiting for transfers between devices: 52.9 us -> 64 us
  local copies, waits for them, and re-layouts: 8.72 us -> 5.16 us
    ppermute x28, waiting for transfers between devices: 26 us -> 35.3 us  [shift(): lax.ppermute(value, 'aux', [(index, (index + by) % n_aux) for index in ra...]
    ppermute x28, starting transfers between devices: 48.3 us -> 41 us  [shift(): lax.ppermute(value, 'aux', [(index, (index + by) % n_aux) for index in ra...]
    ppermute x13 -> x10, starting transfers between devices: 18.1 us -> 11.2 us  [the longest x7 6.97 us: per_device(): lax.ppermute(message, 'pair', spread_perm(hop, flip))]
    unnamed x27 -> x13, local copies, waits for them, and re-layouts: 8.32 us -> 4.75 us
    ppermute x13 -> x10, waiting for transfers between devices: 27 us -> 28.7 us  [the longest x7 16.4 us: per_device(): lax.ppermute(message, 'pair', spread_perm(hop, flip))]
    pallas_call x6 -> x19, Pallas kernels: 11.1 us -> 9.79 us  [the longest x2 3.46 us: per_device(): pl.pallas_call(functools.partial(gram_kernel, first_pair, domain_max, ord...]
  transfers between devices with their start and end apart: 41 -> 38, of which waited for: 21 -> 23; matrix products, arithmetic and copies ran while one was open for 3% -> 2% of each run, Pallas kernels for 4% -> 4%
where the time goes in v5:
time: 136 us; the launch traced here: 134 us
  waiting for transfers between devices  64 us (47%)
  starting transfers between devices  52.2 us (38%)
  Pallas kernels  10.2 us (7%)
  local copies, waits for them, and re-layouts  5.16 us (4%)
  other arithmetic  2.64 us (2%)
    ppermute x28, starting transfers between devices, shift(): lax.ppermute(value, 'aux', [(index, (index + by) % n_aux) for index in ra...  41 us
    ppermute x28, waiting for transfers between devices, shift(): lax.ppermute(value, 'aux', [(index, (index + by) % n_aux) for index in ra...  35.3 us
    ppermute x7, waiting for transfers between devices, per_device(): lax.ppermute(message, 'pair', spread_perm(hop, flip))  16.4 us
    ppermute x3, waiting for transfers between devices, per_device(): lax.ppermute(fitted, 'pair', gather_perm(hop))  12.2 us
    ppermute x7, starting transfers between devices, per_device(): lax.ppermute(message, 'pair', spread_perm(hop, flip))  6.97 us
    unnamed x13, local copies, waits for them, and re-layouts  4.75 us
    ppermute x3, starting transfers between devices, per_device(): lax.ppermute(fitted, 'pair', gather_perm(hop))  4.23 us
    pallas_call x2, Pallas kernels, per_device(): pl.pallas_call(functools.partial(gram_kernel, first_pair, domain_max, ord...  3.46 us
  transfers between devices with their start and end apart: 38, of which 23 were waited for; matrix products, arithmetic and copies ran while one was open for 2% of the time, Pallas kernels for 4%

profile of v5, /device:TPU:2, one launch (start us, length us, event | category | flops | bytes accessed | tf_op | source)
XLA Modules:
  0.0 134.5 jit_solution(2865665413083272792)
XLA Ops:
  3.9 4.0 %collective-permute-start.2 = (bf16[320,512]{1,0:T(8,128)(2,1)S(1)}, bf16[320,512]{1,0:T(8,128)(2,1)S(1)}, u32[]{:S(2)}, u32[]{:S(2)}) collective-permute-start(bf16[320,512]{1,0:T(8,128)(2,1)S(1)} %get-tuple-element.15.refs_0_), channel_id=1, source_target_pairs={{0,224},{32,0},{64,32},{96,64},{128,96},{160,128},{192,160},{224,1... | collective-permute-start | bytes 983048 | tf_op jit(solution)/shard_map/ppermute | solution.py:176
  8.0 3.2 %collective-permute-start.6 = (bf16[192,512]{1,0:T(8,128)(2,1)S(1)}, bf16[192,512]{1,0:T(8,128)(2,1)S(1)}, u32[]{:S(2)}, u32[]{:S(2)}) collective-permute-start(bf16[192,512]{1,0:T(8,128)(2,1)S(1)} %get-tuple-element.16.refs_5_), channel_id=1, source_target_pairs={{0,224},{32,0},{64,32},{96,64},{128,96},{160,128},{192,160},{224,1... | collective-permute-start | bytes 589832 | tf_op jit(solution)/shard_map/ppermute | solution.py:176
  13.2 3.2 %collective-permute-done.refs_1_ = bf16[320,512]{1,0:T(8,128)(2,1)S(1)} collective-permute-done((bf16[320,512]{1,0:T(8,128)(2,1)S(1)}, bf16[320,512]{1,0:T(8,128)(2,1)S(1)}, u32[]{:S(2)}, u32[]{:S(2)}) %collective-permute-start) | collective-permute-done | bytes 327712 | tf_op jit(solution)/shard_map/ppermute | solution.py:176
  16.4 2.7 %collective-permute-done.6.refs_9_ = bf16[192,512]{1,0:T(8,128)(2,1)S(1)} collective-permute-done((bf16[192,512]{1,0:T(8,128)(2,1)S(1)}, bf16[192,512]{1,0:T(8,128)(2,1)S(1)}, u32[]{:S(2)}, u32[]{:S(2)}) %collective-permute-start.6) | collective-permute-done | bytes 196640 | tf_op jit(solution)/shard_map/ppermute | solution.py:176
  19.2 3.7 %collective-permute-start.7 = (bf16[192,512]{1,0:T(8,128)(2,1)S(1)}, bf16[192,512]{1,0:T(8,128)(2,1)S(1)}, u32[]{:S(2)}, u32[]{:S(2)}) collective-permute-start(bf16[192,512]{1,0:T(8,128)(2,1)S(1)} %collective-permute-done.6.refs_9_), channel_id=1, source_target_pairs={{0,224},{32,0},{64,32},{96,64},{128,96},{160,128},{192,160},{224,1... | collective-permute-start | bytes 589832 | tf_op jit(solution)/shard_map/ppermute | solution.py:176
  23.5 3.4 %collective-permute-done.1.refs_2_ = bf16[320,512]{1,0:T(8,128)(2,1)S(1)} collective-permute-done((bf16[320,512]{1,0:T(8,128)(2,1)S(1)}, bf16[320,512]{1,0:T(8,128)(2,1)S(1)}, u32[]{:S(2)}, u32[]{:S(2)}) %collective-permute-start.1) | collective-permute-done | bytes 327712 | tf_op jit(solution)/shard_map/ppermute | solution.py:176
  28.2 3.7 %collective-permute-start.12 = (bf16[192,512]{1,0:T(8,128)(2,1)S(1)}, bf16[192,512]{1,0:T(8,128)(2,1)S(1)}, u32[]{:S(2)}, u32[]{:S(2)}) collective-permute-start(bf16[192,512]{1,0:T(8,128)(2,1)S(1)} %collective-permute-done.7.refs_8_), channel_id=1, source_target_pairs={{0,224},{32,0},{64,32},{96,64},{128,96},{160,128},{192,160},{224,1... | collective-permute-start | bytes 589832 | tf_op jit(solution)/shard_map/ppermute | solution.py:176
  32.0 3.3 %collective-permute-done.3.refs_3_ = bf16[320,512]{1,0:T(8,128)(2,1)S(1)} collective-permute-done((bf16[320,512]{1,0:T(8,128)(2,1)S(1)}, bf16[320,512]{1,0:T(8,128)(2,1)S(1)}, u32[]{:S(2)}, u32[]{:S(2)}) %collective-permute-start.3) | collective-permute-done | bytes 327712 | tf_op jit(solution)/shard_map/ppermute | solution.py:176
  35.2 3.7 %collective-permute-start.10 = (bf16[320,512]{1,0:T(8,128)(2,1)S(1)}, bf16[320,512]{1,0:T(8,128)(2,1)S(1)}, u32[]{:S(2)}, u32[]{:S(2)}) collective-permute-start(bf16[320,512]{1,0:T(8,128)(2,1)S(1)} %collective-permute-done.3.refs_3_), channel_id=1, source_target_pairs={{0,224},{32,0},{64,32},{96,64},{128,96},{160,128},{192,160},{224,1... | collective-permute-start | bytes 983048 | tf_op jit(solution)/shard_map/ppermute | solution.py:176
  39.1 3.5 %collective-permute-done.5.refs_7_ = bf16[192,512]{1,0:T(8,128)(2,1)S(1)} collective-permute-done((bf16[192,512]{1,0:T(8,128)(2,1)S(1)}, bf16[192,512]{1,0:T(8,128)(2,1)S(1)}, u32[]{:S(2)}, u32[]{:S(2)}) %collective-permute-start.5) | collective-permute-done | bytes 196640 | tf_op jit(solution)/shard_map/ppermute | solution.py:176
  42.6 3.2 %collective-permute-start.13 = (bf16[192,512]{1,0:T(8,128)(2,1)S(1)}, bf16[192,512]{1,0:T(8,128)(2,1)S(1)}, u32[]{:S(2)}, u32[]{:S(2)}) collective-permute-start(bf16[192,512]{1,0:T(8,128)(2,1)S(1)} %collective-permute-done.12.refs_6_), channel_id=1, source_target_pairs={{0,224},{32,0},{64,32},{96,64},{128,96},{160,128},{192,160},{224,1... | collective-permute-start | bytes 589832 | tf_op jit(solution)/shard_map/ppermute | solution.py:176
  57.5 4.5 %collective-permute-done.14.refs_0_ = bf16[8,64,512]{2,1,0:T(8,128)(2,1)S(1)} collective-permute-done((bf16[8,64,512]{2,1,0:T(8,128)(2,1)S(1)}, bf16[8,64,512]{2,1,0:T(8,128)(2,1)S(1)}, u32[]{:S(2)}, u32[]{:S(2)}) %collective-permute-start.14) | collective-permute-done | bytes 524320 | tf_op jit(solution)/shard_map/ppermute | solution.py:308
  63.5 6.3 %collective-permute-done.16.refs_2_ = bf16[8,64,512]{2,1,0:T(8,128)(2,1)S(1)} collective-permute-done((bf16[8,64,512]{2,1,0:T(8,128)(2,1)S(1)}, bf16[8,64,512]{2,1,0:T(8,128)(2,1)S(1)}, u32[]{:S(2)}, u32[]{:S(2)}) %collective-permute-start.16) | collective-permute-done | bytes 524320 | tf_op jit(solution)/shard_map/ppermute | solution.py:308
  78.8 3.2 %collective-permute-done.17.refs_0_ = bf16[8,64,512]{2,1,0:T(8,128)(2,1)S(1)} collective-permute-done((bf16[8,64,512]{2,1,0:T(8,128)(2,1)}, bf16[8,64,512]{2,1,0:T(8,128)(2,1)S(1)}, u32[]{:S(2)}, u32[]{:S(2)}) %collective-permute-start.17) | collective-permute-done | bytes 524320 | tf_op jit(solution)/shard_map/ppermute | solution.py:329
  83.9 5.0 %collective-permute-done.19.refs_2_ = bf16[8,64,512]{2,1,0:T(8,128)(2,1)S(1)} collective-permute-done((bf16[8,64,512]{2,1,0:T(8,128)(2,1)S(1)}, bf16[8,64,512]{2,1,0:T(8,128)(2,1)S(1)}, u32[]{:S(2)}, u32[]{:S(2)}) %collective-permute-start.19) | collective-permute-done | bytes 524320 | tf_op jit(solution)/shard_map/ppermute | solution.py:329
  92.8 4.0 %collective-permute-done.22.refs_5_ = bf16[8,64,512]{2,1,0:T(8,128)(2,1)S(1)} collective-permute-done((bf16[8,64,512]{2,1,0:T(8,128)(2,1)S(1)}, bf16[8,64,512]{2,1,0:T(8,128)(2,1)S(1)}, u32[]{:S(2)}, u32[]{:S(2)}) %collective-permute-start.22) | collective-permute-done | bytes 524320 | tf_op jit(solution)/shard_map/ppermute | solution.py:329
  108.3 3.1 %collective-permute-done.31.a_ref = f32[5,32,256]{2,1,0:T(8,128)S(1)} collective-permute-done((f32[5,32,256]{2,1,0:T(8,128)S(1)}, f32[5,32,256]{2,1,0:T(8,128)S(1)}, u32[]{:S(2)}, u32[]{:S(2)}) %collective-permute-start.31) | collective-permute-done | bytes 163872 | tf_op jit(solution)/shard_map/ppermute | solution.py:176
  111.6 3.3 %collective-permute-start.36 = (f32[5,32,256]{2,1,0:T(8,128)S(1)}, f32[5,32,256]{2,1,0:T(8,128)S(1)}, u32[]{:S(2)}, u32[]{:S(2)}) collective-permute-start(f32[5,32,256]{2,1,0:T(8,128)S(1)} %add_term.18), channel_id=1, source_target_pairs={{0,224},{32,0},{64,32},{96,64},{128,96},{160,128},{192,160},{224,1... | collective-permute-start | bytes 491528 | tf_op jit(solution)/shard_map/ppermute | solution.py:176
  117.1 2.7 %collective-permute-done.32.a_ref = f32[5,32,256]{2,1,0:T(8,128)S(1)} collective-permute-done((f32[5,32,256]{2,1,0:T(8,128)S(1)}, f32[5,32,256]{2,1,0:T(8,128)S(1)}, u32[]{:S(2)}, u32[]{:S(2)}) %collective-permute-start.32) | collective-permute-done | bytes 163872 | tf_op jit(solution)/shard_map/ppermute | solution.py:176
  119.9 3.3 %collective-permute-start.37 = (f32[5,32,256]{2,1,0:T(8,128)S(1)}, f32[5,32,256]{2,1,0:T(8,128)S(1)}, u32[]{:S(2)}, u32[]{:S(2)}) collective-permute-start(f32[5,32,256]{2,1,0:T(8,128)S(1)} %add_term.19), channel_id=1, source_target_pairs={{0,224},{32,0},{64,32},{96,64},{128,96},{160,128},{192,160},{224,1... | collective-permute-start | bytes 491528 | tf_op jit(solution)/shard_map/ppermute | solution.py:176
  123.2 2.3 %collective-permute-start.30 = (f32[5,32,256]{2,1,0:T(8,128)S(1)}, f32[5,32,256]{2,1,0:T(8,128)S(1)}, u32[]{:S(2)}, u32[]{:S(2)}) collective-permute-start(f32[5,32,256]{2,1,0:T(8,128)S(1)} %add_term.14), channel_id=1, source_target_pairs={{0,224},{32,0},{64,32},{96,64},{128,96},{160,128},{192,160},{224,1... | collective-permute-start | bytes 491528 | tf_op jit(solution)/shard_map/ppermute | solution.py:176
  125.6 2.7 %collective-permute-done.33 = f32[5,32,256]{2,1,0:T(8,128)S(1)} collective-permute-done((f32[5,32,256]{2,1,0:T(8,128)S(1)}, f32[5,32,256]{2,1,0:T(8,128)S(1)}, u32[]{:S(2)}, u32[]{:S(2)}) %collective-permute-start.33) | collective-permute-done | bytes 163872 | tf_op jit(solution)/shard_map/ppermute | solution.py:176
  128.4 2.6 %collective-permute-done.30 = f32[5,32,256]{2,1,0:T(8,128)S(1)} collective-permute-done((f32[5,32,256]{2,1,0:T(8,128)S(1)}, f32[5,32,256]{2,1,0:T(8,128)S(1)}, u32[]{:S(2)}, u32[]{:S(2)}) %collective-permute-start.30) | collective-permute-done | bytes 163872 | tf_op jit(solution)/shard_map/ppermute | solution.py:176
  131.0 2.7 %collective-permute-done.27 = f32[5,32,256]{2,1,0:T(8,128)S(1)} collective-permute-done((f32[5,32,256]{2,1,0:T(8,128)S(1)}, f32[5,32,256]{2,1,0:T(8,128)S(1)}, u32[]{:S(2)}, u32[]{:S(2)}) %collective-permute-start.27) | collective-permute-done | bytes 163872 | tf_op jit(solution)/shard_map/ppermute | solution.py:176
  (116 shorter events, 50.8 us)
Async XLA Ops:
  2.0 14.5 %collective-permute-start = (bf16[320,512]{1,0:T(8,128)(2,1)S(1)}, bf16[320,512]{1,0:T(8,128)(2,1)S(1)}, u32[]{:S(2)}, u32[]{:S(2)}) collective-permute-start(bf16[320,512]{1,0:T(8,128)(2,1)S(1)} %get-tuple-element.15.refs_0_), channel_id=1, source_target_pairs={{0,32},{32,64},{64,96},{96,128},{128,160},{160,192},{192,224},{224... | collective-permute-start | bytes 983048 | tf_op jit(solution)/shard_map/ppermute | solution.py:176
  3.9 19.1 %collective-permute-start.2 = (bf16[320,512]{1,0:T(8,128)(2,1)S(1)}, bf16[320,512]{1,0:T(8,128)(2,1)S(1)}, u32[]{:S(2)}, u32[]{:S(2)}) collective-permute-start(bf16[320,512]{1,0:T(8,128)(2,1)S(1)} %get-tuple-element.15.refs_0_), channel_id=1, source_target_pairs={{0,224},{32,0},{64,32},{96,64},{128,96},{160,128},{192,160},{224,1... | collective-permute-start | bytes 983048 | tf_op jit(solution)/shard_map/ppermute | solution.py:176
  8.0 18.9 %collective-permute-start.4 = (bf16[192,512]{1,0:T(8,128)(2,1)S(1)}, bf16[192,512]{1,0:T(8,128)(2,1)S(1)}, u32[]{:S(2)}, u32[]{:S(2)}) collective-permute-start(bf16[192,512]{1,0:T(8,128)(2,1)S(1)} %get-tuple-element.16.refs_5_), channel_id=1, source_target_pairs={{0,32},{32,64},{64,96},{96,128},{128,160},{160,192},{192,224},{224... | collective-permute-start | bytes 589832 | tf_op jit(solution)/shard_map/ppermute | solution.py:176
  8.0 11.2 %collective-permute-start.6 = (bf16[192,512]{1,0:T(8,128)(2,1)S(1)}, bf16[192,512]{1,0:T(8,128)(2,1)S(1)}, u32[]{:S(2)}, u32[]{:S(2)}) collective-permute-start(bf16[192,512]{1,0:T(8,128)(2,1)S(1)} %get-tuple-element.16.refs_5_), channel_id=1, source_target_pairs={{0,224},{32,0},{64,32},{96,64},{128,96},{160,128},{192,160},{224,1... | collective-permute-start | bytes 589832 | tf_op jit(solution)/shard_map/ppermute | solution.py:176
  16.4 10.4 %collective-permute-start.1 = (bf16[320,512]{1,0:T(8,128)(2,1)S(1)}, bf16[320,512]{1,0:T(8,128)(2,1)S(1)}, u32[]{:S(2)}, u32[]{:S(2)}) collective-permute-start(bf16[320,512]{1,0:T(8,128)(2,1)S(1)} %collective-permute-done.refs_1_), channel_id=1, source_target_pairs={{0,32},{32,64},{64,96},{96,128},{128,160},{160,192},{192,224},{224... | collective-permute-start | bytes 983048 | tf_op jit(solution)/shard_map/ppermute | solution.py:176
  19.2 9.0 %collective-permute-start.7 = (bf16[192,512]{1,0:T(8,128)(2,1)S(1)}, bf16[192,512]{1,0:T(8,128)(2,1)S(1)}, u32[]{:S(2)}, u32[]{:S(2)}) collective-permute-start(bf16[192,512]{1,0:T(8,128)(2,1)S(1)} %collective-permute-done.6.refs_9_), channel_id=1, source_target_pairs={{0,224},{32,0},{64,32},{96,64},{128,96},{160,128},{192,160},{224,1... | collective-permute-start | bytes 589832 | tf_op jit(solution)/shard_map/ppermute | solution.py:176
  23.0 12.2 %collective-permute-start.3 = (bf16[320,512]{1,0:T(8,128)(2,1)S(1)}, bf16[320,512]{1,0:T(8,128)(2,1)S(1)}, u32[]{:S(2)}, u32[]{:S(2)}) collective-permute-start(bf16[320,512]{1,0:T(8,128)(2,1)S(1)} %collective-permute-done.2.refs_4_), channel_id=1, source_target_pairs={{0,224},{32,0},{64,32},{96,64},{128,96},{160,128},{192,160},{224,1... | collective-permute-start | bytes 983048 | tf_op jit(solution)/shard_map/ppermute | solution.py:176
  26.8 12.1 %collective-permute-start.8 = (bf16[320,512]{1,0:T(8,128)(2,1)S(1)}, bf16[320,512]{1,0:T(8,128)(2,1)S(1)}, u32[]{:S(2)}, u32[]{:S(2)}) collective-permute-start(bf16[320,512]{1,0:T(8,128)(2,1)S(1)} %collective-permute-done.1.refs_2_), channel_id=1, source_target_pairs={{0,32},{32,64},{64,96},{96,128},{128,160},{160,192},{192,224},{224... | collective-permute-start | bytes 983048 | tf_op jit(solution)/shard_map/ppermute | solution.py:176
  26.9 15.6 %collective-permute-start.5 = (bf16[192,512]{1,0:T(8,128)(2,1)S(1)}, bf16[192,512]{1,0:T(8,128)(2,1)S(1)}, u32[]{:S(2)}, u32[]{:S(2)}) collective-permute-start(bf16[192,512]{1,0:T(8,128)(2,1)S(1)} %collective-permute-done.4.refs_6_), channel_id=1, source_target_pairs={{0,32},{32,64},{64,96},{96,128},{128,160},{160,192},{192,224},{224... | collective-permute-start | bytes 589832 | tf_op jit(solution)/shard_map/ppermute | solution.py:176
  28.2 14.4 %collective-permute-start.12 = (bf16[192,512]{1,0:T(8,128)(2,1)S(1)}, bf16[192,512]{1,0:T(8,128)(2,1)S(1)}, u32[]{:S(2)}, u32[]{:S(2)}) collective-permute-start(bf16[192,512]{1,0:T(8,128)(2,1)S(1)} %collective-permute-done.7.refs_8_), channel_id=1, source_target_pairs={{0,224},{32,0},{64,32},{96,64},{128,96},{160,128},{192,160},{224,1... | collective-permute-start | bytes 589832 | tf_op jit(solution)/shard_map/ppermute | solution.py:176
  35.2 16.5 %collective-permute-start.10 = (bf16[320,512]{1,0:T(8,128)(2,1)S(1)}, bf16[320,512]{1,0:T(8,128)(2,1)S(1)}, u32[]{:S(2)}, u32[]{:S(2)}) collective-permute-start(bf16[320,512]{1,0:T(8,128)(2,1)S(1)} %collective-permute-done.3.refs_3_), channel_id=1, source_target_pairs={{0,224},{32,0},{64,32},{96,64},{128,96},{160,128},{192,160},{224,1... | collective-permute-start | bytes 983048 | tf_op jit(solution)/shard_map/ppermute | solution.py:176
  38.9 12.8 %collective-permute-start.9 = (bf16[320,512]{1,0:T(8,128)(2,1)S(1)}, bf16[320,512]{1,0:T(8,128)(2,1)S(1)}, u32[]{:S(2)}, u32[]{:S(2)}) collective-permute-start(bf16[320,512]{1,0:T(8,128)(2,1)S(1)} %collective-permute-done.8.refs_1_), channel_id=1, source_target_pairs={{0,32},{32,64},{64,96},{96,128},{128,160},{160,192},{192,224},{224... | collective-permute-start | bytes 983048 | tf_op jit(solution)/shard_map/ppermute | solution.py:176
  42.6 9.2 %collective-permute-start.11 = (bf16[192,512]{1,0:T(8,128)(2,1)S(1)}, bf16[192,512]{1,0:T(8,128)(2,1)S(1)}, u32[]{:S(2)}, u32[]{:S(2)}) collective-permute-start(bf16[192,512]{1,0:T(8,128)(2,1)S(1)} %collective-permute-done.5.refs_7_), channel_id=1, source_target_pairs={{0,32},{32,64},{64,96},{96,128},{128,160},{160,192},{192,224},{224... | collective-permute-start | bytes 589832 | tf_op jit(solution)/shard_map/ppermute | solution.py:176
  42.6 9.2 %collective-permute-start.13 = (bf16[192,512]{1,0:T(8,128)(2,1)S(1)}, bf16[192,512]{1,0:T(8,128)(2,1)S(1)}, u32[]{:S(2)}, u32[]{:S(2)}) collective-permute-start(bf16[192,512]{1,0:T(8,128)(2,1)S(1)} %collective-permute-done.12.refs_6_), channel_id=1, source_target_pairs={{0,224},{32,0},{64,32},{96,64},{128,96},{160,128},{192,160},{224,1... | collective-permute-start | bytes 589832 | tf_op jit(solution)/shard_map/ppermute | solution.py:176
  52.8 9.3 %collective-permute-start.14 = (bf16[8,64,512]{2,1,0:T(8,128)(2,1)S(1)}, bf16[8,64,512]{2,1,0:T(8,128)(2,1)S(1)}, u32[]{:S(2)}, u32[]{:S(2)}) collective-permute-start(bf16[8,64,512]{2,1,0:T(8,128)(2,1)S(1)} %fit_far.1.refs_3_), channel_id=1, source_target_pairs={{0,8},{1,3},{2,10},{3,5},{4,12},{5,7},{6,14},{7,1},{8,16},{9,11},{... | collective-permute-start | bytes 1572872 | tf_op jit(solution)/shard_map/ppermute | solution.py:308
  54.3 9.2 %collective-permute-start.15 = (bf16[8,64,512]{2,1,0:T(8,128)(2,1)S(1)}, bf16[8,64,512]{2,1,0:T(8,128)(2,1)S(1)}, u32[]{:S(2)}, u32[]{:S(2)}) collective-permute-start(bf16[8,64,512]{2,1,0:T(8,128)(2,1)S(1)} %fit_far.1.refs_3_), channel_id=1, source_target_pairs={{0,24},{1,7},{2,26},{3,1},{4,28},{5,3},{6,30},{7,5},{8,0},{9,15},{... | collective-permute-start | bytes 1572872 | tf_op jit(solution)/shard_map/ppermute | solution.py:308
  54.9 14.9 %collective-permute-start.16 = (bf16[8,64,512]{2,1,0:T(8,128)(2,1)S(1)}, bf16[8,64,512]{2,1,0:T(8,128)(2,1)S(1)}, u32[]{:S(2)}, u32[]{:S(2)}) collective-permute-start(bf16[8,64,512]{2,1,0:T(8,128)(2,1)S(1)} %fit_far.1.refs_3_), channel_id=1, source_target_pairs={{0,16},{1,5},{2,18},{3,7},{4,20},{5,1},{6,22},{7,3},{8,24},{9,13},... | collective-permute-start | bytes 1572872 | tf_op jit(solution)/shard_map/ppermute | solution.py:308
  71.4 10.6 %collective-permute-start.17 = (bf16[8,64,512]{2,1,0:T(8,128)(2,1)}, bf16[8,64,512]{2,1,0:T(8,128)(2,1)S(1)}, u32[]{:S(2)}, u32[]{:S(2)}) collective-permute-start(bf16[8,64,512]{2,1,0:T(8,128)(2,1)} %get-tuple-element.17), channel_id=1, source_target_pairs={{0,2},{1,9},{2,4},{3,11},{4,6},{5,13},{6,0},{7,15},{8,10},{9,17},{... | collective-permute-start | bytes 1572872 | tf_op jit(solution)/shard_map/ppermute | solution.py:329
  72.9 9.4 %collective-permute-start.18 = (bf16[8,64,512]{2,1,0:T(8,128)(2,1)}, bf16[8,64,512]{2,1,0:T(8,128)(2,1)S(1)}, u32[]{:S(2)}, u32[]{:S(2)}) collective-permute-start(bf16[8,64,512]{2,1,0:T(8,128)(2,1)} %get-tuple-element.18), channel_id=1, source_target_pairs={{0,6},{1,25},{2,0},{3,27},{4,2},{5,29},{6,4},{7,31},{8,14},{9,1},{... | collective-permute-start | bytes 1572872 | tf_op jit(solution)/shard_map/ppermute | solution.py:329
  75.2 13.7 %collective-permute-start.19 = (bf16[8,64,512]{2,1,0:T(8,128)(2,1)S(1)}, bf16[8,64,512]{2,1,0:T(8,128)(2,1)S(1)}, u32[]{:S(2)}, u32[]{:S(2)}) collective-permute-start(bf16[8,64,512]{2,1,0:T(8,128)(2,1)S(1)} %get-tuple-element.19), channel_id=1, source_target_pairs={{0,4},{1,17},{2,6},{3,19},{4,0},{5,21},{6,2},{7,23},{8,12},{9,25},... | collective-permute-start | bytes 1572872 | tf_op jit(solution)/shard_map/ppermute | solution.py:329
  77.3 13.8 %collective-permute-start.20 = (bf16[8,64,512]{2,1,0:T(8,128)(2,1)S(1)}, bf16[8,64,512]{2,1,0:T(8,128)(2,1)S(1)}, u32[]{:S(2)}, u32[]{:S(2)}) collective-permute-start(bf16[8,64,512]{2,1,0:T(8,128)(2,1)S(1)} %get-tuple-element.20), channel_id=1, source_target_pairs={{0,3},{1,8},{2,5},{3,10},{4,7},{5,12},{6,1},{7,14},{8,11},{9,16},{... | collective-permute-start | bytes 1572872 | tf_op jit(solution)/shard_map/ppermute | solution.py:329
  78.0 14.8 %collective-permute-start.21 = (bf16[8,64,512]{2,1,0:T(8,128)(2,1)S(1)}, bf16[8,64,512]{2,1,0:T(8,128)(2,1)S(1)}, u32[]{:S(2)}, u32[]{:S(2)}) collective-permute-start(bf16[8,64,512]{2,1,0:T(8,128)(2,1)S(1)} %get-tuple-element.21), channel_id=1, source_target_pairs={{0,7},{1,24},{2,1},{3,26},{4,3},{5,28},{6,5},{7,30},{8,15},{9,0},{... | collective-permute-start | bytes 1572872 | tf_op jit(solution)/shard_map/ppermute | solution.py:329
  82.0 14.8 %collective-permute-start.22 = (bf16[8,64,512]{2,1,0:T(8,128)(2,1)S(1)}, bf16[8,64,512]{2,1,0:T(8,128)(2,1)S(1)}, u32[]{:S(2)}, u32[]{:S(2)}) collective-permute-start(bf16[8,64,512]{2,1,0:T(8,128)(2,1)S(1)} %get-tuple-element.22), channel_id=1, source_target_pairs={{0,5},{1,16},{2,7},{3,18},{4,1},{5,20},{6,3},{7,22},{8,13},{9,24},... | collective-permute-start | bytes 1572872 | tf_op jit(solution)/shard_map/ppermute | solution.py:329
  82.3 14.5 %collective-permute-start.23 = (bf16[8,64,512]{2,1,0:T(8,128)(2,1)S(1)}, bf16[8,64,512]{2,1,0:T(8,128)(2,1)S(1)}, u32[]{:S(2)}, u32[]{:S(2)}) collective-permute-start(bf16[8,64,512]{2,1,0:T(8,128)(2,1)S(1)} %get-tuple-element.23), channel_id=1, source_target_pairs={{0,1},{1,0},{2,3},{3,2},{4,5},{5,4},{6,7},{7,6},{8,9},{9,8},{10,11... | collective-permute-start | bytes 1572872 | tf_op jit(solution)/shard_map/ppermute | solution.py:329
  (21 other events, 150.8 us)

commit v6 on v4

v6 whole, which is shorter than its diff:
```python
import functools

import jax
import jax.numpy as jnp
from jax import lax
from jax.experimental import pallas as pl
from jax.experimental.pallas import tpu as pltpu
from jax.sharding import PartitionSpec as P

VMEM_LIMIT = 12 * 1024 * 1024
CHUNKS = (5, 3)
PAIR_CHUNKS = (5, 5)
SIDE = 4
GATHER_HOPS = (1, 3, 2, 0)
SPREAD_ORDER = ((1, 0), (3, 0), (2, 0), (1, 1), (3, 1), (2, 1), (0, 1), (0, 0))
PICK_GROUP = 2
CAP = 2


def mask_kernel(keep_ref, b_ref, *out_refs):
    width = b_ref.shape[0] // keep_ref.shape[0]
    block = 0
    for out_ref in out_refs:
        for start in range(0, out_ref.shape[0], width):
            out_ref[start : start + width, :] = b_ref[
                block * width : (block + 1) * width, :
            ] * keep_ref[block : block + 1, :].astype(jnp.bfloat16)
            block += 1


def metric_kernel(hops, own_ref, w_ref, out_ref, sems):
    steps = len(hops)
    depth = out_ref.shape[1]
    loads = []
    for step, hop in enumerate(hops):
        row = pl.multiple_of(((own_ref[0] + steps - hop) % steps) * depth, depth)
        loads.append(pltpu.make_async_copy(w_ref.at[pl.ds(row, depth)], out_ref.at[step], sems.at[step]))
    for load in loads:
        load.start()
    for load in loads:
        load.wait()


def fit_kernel(*refs):
    pieces, w_ref, out_ref, total = refs[:-3], refs[-3], refs[-2], refs[-1]
    for step, piece in enumerate(pieces):
        part = jnp.dot(piece[...], w_ref[step], preferred_element_type=jnp.float32)
        if step == 0:
            total[...] = part
        elif step < len(pieces) - 1:
            total[...] += part
        else:
            out_ref[...] = (total[...] + part).astype(jnp.bfloat16).reshape(out_ref.shape)


def pick_kernel(messages, send_ref, *refs):
    count = SIDE * len(CHUNKS)
    sources, outs = refs[:count], refs[count:]
    hop_of = {hop: index for index, hop in enumerate(GATHER_HOPS)}
    for message, out in zip(messages, outs):
        slots = out.shape[0]
        for slot in range(slots):
            block = send_ref[message * slots + slot]
            first = 0
            for chunk, blocks in enumerate(CHUNKS):
                source = sources[hop_of[slot // CAP] * len(CHUNKS) + chunk]

                @pl.when((block >= first) & (block < first + blocks))
                def _(out=out, slot=slot, source=source, index=block - first):
                    out[slot] = source[index]

                first += blocks


def add_kernel(index, a_ref, part_ref, out_ref):
    out_ref[...] = a_ref[...] + part_ref[index]


def last_kernel(*refs):
    refs, out_ref = refs[:-1], refs[-1]
    row = 0
    for index in range(0, len(refs), 3):
        part, right, left = refs[index : index + 3]
        pairs = part.shape[1]
        out_ref[row : row + pairs] = part[0] + right[...] + left[...]
        row += pairs


def gram_kernel(first_pair, domain_max, order, goes_ref, counts_ref, own_ref, *refs):
    arrived, out_ref, stacks = refs[:-2], refs[-2], refs[-1]
    slots = arrived[0].shape[0]
    n_aux, pairs, share, size = out_ref.shape
    places, width, depth = stacks.shape
    for message, source in zip(order, arrived):
        for slot in range(slots):
            goes = goes_ref[message * slots + slot] - first_pair * domain_max

            @pl.when((goes >= 0) & (goes < places))
            def _(source=source, slot=slot, goes=goes):
                stacks[goes] = source[slot]

    row = lax.broadcasted_iota(jnp.int32, (size, size), 0)
    column = lax.broadcasted_iota(jnp.int32, (size, size), 1)
    furthest = jnp.maximum(row, column)
    for pair in range(pairs):
        stack = stacks[pair * domain_max : (pair + 1) * domain_max].reshape(size, depth)
        value = lax.dot_general(
            stack, stack, (((1,), (1,)), ((), ())), preferred_element_type=jnp.float32
        )
        value = jnp.where(furthest < counts_ref[first_pair + pair] * width, value, 0.0)
        value = value.reshape(n_aux, share, size)
        for index in range(n_aux):
            out_ref[(index + n_aux - own_ref[0]) % n_aux, pair] = value[index]


def ring_gather(chunks, early):
    n_aux = lax.axis_size("aux")
    rings = []
    for index, chunk in enumerate(chunks):
        far = n_aux // 2 if index % 2 == 0 else n_aux // 2 - 1
        rings.append((far, n_aux - 1 - far, {0: chunk}, [chunk, chunk]))
    for step in range(1, n_aux // 2 + 1):
        before = None
        for far_right, far_left, found, moving in rings:
            arrived = list(moving)
            for side, (by, far) in enumerate(((1, far_right), (-1, far_left))):
                if step <= far:
                    if before is not None and step > 1:
                        moving[side], _ = lax.optimization_barrier((moving[side], before[side]))
                    moving[side] = shift(moving[side], by)
                    found[step * by % n_aux] = moving[side]
            before = arrived
        if step == 1:
            moving[0], early = lax.optimization_barrier((moving[0], early))
    return [found for _, _, found, _ in rings], early


def ring_sum(parts):
    n_aux = lax.axis_size("aux")
    rings = []
    for index, part in enumerate(parts):
        far = n_aux // 2 if index % 2 == 0 else n_aux // 2 - 1
        rings.append([part, far, n_aux - 1 - far, None, None])
    for step in range(n_aux // 2, 0, -1):
        for ring in rings:
            part, far_right, far_left, right, left = ring
            if step <= far_right:
                ring[3] = shift(part[step] if right is None else add_term(right, part, step), 1)
            if step <= far_left:
                ring[4] = shift(part[n_aux - step] if left is None else add_term(left, part, n_aux - step), -1)
    parts_moved = [value for part, _, _, right, left in rings for value in (part, right, left)]
    pairs = [part.shape[1] for part in parts]
    in_vmem = pl.BlockSpec(memory_space=pltpu.VMEM)
    return pl.pallas_call(
        last_kernel,
        in_specs=[in_vmem] * len(parts_moved),
        out_specs=in_vmem,
        out_shape=jax.ShapeDtypeStruct((sum(pairs), *parts[0].shape[2:]), parts[0].dtype),
        compiler_params=pltpu.CompilerParams(vmem_limit_bytes=VMEM_LIMIT),
        name="last_terms",
    )(*parts_moved)


def add_term(moving, part, index):
    in_vmem = pl.BlockSpec(memory_space=pltpu.VMEM)
    return pl.pallas_call(
        functools.partial(add_kernel, index),
        in_specs=[in_vmem] * 2,
        out_specs=in_vmem,
        out_shape=jax.ShapeDtypeStruct(moving.shape, moving.dtype),
        compiler_params=pltpu.CompilerParams(vmem_limit_bytes=VMEM_LIMIT),
        name="add_term",
    )(moving, part)


def shift(value, by):
    n_aux = lax.axis_size("aux")
    return lax.ppermute(value, "aux", [(index, (index + by) % n_aux) for index in range(n_aux)])


def device_of(x, y, core):
    return (x % SIDE) * 2 * SIDE + (y % SIDE) * 2 + core % 2


def gather_perm(hop):
    return [
        (device_of(x, y, core), device_of(x + hop, y, 0) if core == 0 else device_of(x, y + hop, 1))
        for x in range(SIDE)
        for y in range(SIDE)
        for core in range(2)
    ]


def spread_perm(hop, flip):
    return [
        (
            device_of(x, y, core),
            device_of(x, y + hop, flip) if core == 0 else device_of(x + hop, y, 1 - flip),
        )
        for x in range(SIDE)
        for y in range(SIDE)
        for core in range(2)
    ]


def plan(domains, own, pairs_dev, blocks_dev, n_pair):
    table = domains.reshape(n_pair, pairs_dev * domains.shape[1])
    slots_dev = table.shape[1]
    x, y, core = own // (2 * SIDE), (own // 2) % SIDE, own % 2
    first = core == 0
    hops = jnp.arange(SIDE, dtype=jnp.int32)
    flips = jnp.arange(2, dtype=jnp.int32)
    source = jnp.where(first, device_of(x - hops, y, 0), device_of(x, y - hops, 1))
    target = jnp.where(
        first,
        device_of(x, y + hops[:, None], flips[None, :]),
        device_of(x + hops[:, None], y, 1 - flips[None, :]),
    ).reshape(2 * SIDE)

    chosen = jnp.concatenate([target, own[None]])[:, None] == jnp.arange(n_pair, dtype=jnp.int32)[None, :]
    rows = jnp.sum(jnp.where(chosen[:, :, None], table[None], 0), axis=1)
    owner, local = rows // blocks_dev, rows % blocks_dev
    earlier = jnp.tril(jnp.ones((slots_dev, slots_dev), jnp.bool_), -1)
    rank = jnp.sum(((owner[:, :, None] == owner[:, None, :]) & earlier[None]).astype(jnp.int32), axis=2)
    key = owner * CAP + rank
    wanted = (source[:, None] * CAP + jnp.arange(CAP, dtype=jnp.int32)[None, :]).reshape(SIDE * CAP)
    hit = key[:-1, None, :] == wanted[None, :, None]
    send = jnp.sum(jnp.where(hit, local[:-1, None, :], 0), axis=2)

    named, place = owner[-1], rank[-1]
    back_x, back_y = (x - named // (2 * SIDE)) % SIDE, (y - (named // 2) % SIDE) % SIDE
    sent_first = named % 2 == 0
    gathered = jnp.where(sent_first, back_x, back_y)
    spread = jnp.where(sent_first, back_y, back_x)
    flip = jnp.where(sent_first, core, 1 - core)
    where = ((spread * 2 + flip) * SIDE + gathered) * CAP + place
    arrives = where[None, :] == jnp.arange(2 * SIDE * SIDE * CAP, dtype=jnp.int32)[:, None]
    goes = jnp.sum(jnp.where(arrives, 1 + jnp.arange(slots_dev, dtype=jnp.int32)[None, :], 0), axis=1) - 1
    return send.reshape(-1), goes


def per_device(b_three, metric, aux_map, domains, counts):
    rows_dev, aux_dev = b_three.shape
    blocks_dev, _ = aux_map.shape
    width = rows_dev // blocks_dev
    n_pair = lax.axis_size("pair")
    n_aux = lax.axis_size("aux")
    own = lax.axis_index("pair")
    pairs_dev = counts.shape[0]
    domain_max = domains.shape[1]
    params = pltpu.CompilerParams(vmem_limit_bytes=VMEM_LIMIT)
    in_hbm = pl.BlockSpec(memory_space=pltpu.HBM)
    in_vmem = pl.BlockSpec(memory_space=pltpu.VMEM)

    place = lax.axis_index("aux").astype(jnp.int32).reshape(1)

    aux_block = jnp.arange(aux_dev, dtype=jnp.int32) // (aux_dev // aux_map.shape[1])
    inside = jnp.arange(aux_map.shape[1], dtype=jnp.int32)[:, None] == aux_block[None, :]
    keep = jnp.sum(jnp.where(inside[None], aux_map[:, :, None], 0), axis=1).astype(jnp.float32)
    masked = pl.pallas_call(
        mask_kernel,
        in_specs=[in_vmem] * 2,
        out_specs=[in_vmem] * len(CHUNKS),
        out_shape=[jax.ShapeDtypeStruct((blocks * width, aux_dev), jnp.bfloat16) for blocks in CHUNKS],
        compiler_params=params,
        name="mask",
    )(keep, b_three)
    send, goes = plan(domains, own, pairs_dev, blocks_dev, n_pair)

    block_shape = (width, aux_dev)
    orders = tuple(range(n_aux))
    ordered = pl.pallas_call(
        functools.partial(metric_kernel, orders),
        grid_spec=pltpu.PrefetchScalarGridSpec(
            num_scalar_prefetch=1,
            grid=(),
            in_specs=[in_hbm],
            out_specs=in_vmem,
            scratch_shapes=[pltpu.SemaphoreType.DMA((n_aux,))],
        ),
        out_shape=jax.ShapeDtypeStruct((n_aux, aux_dev, aux_dev), jnp.bfloat16),
        compiler_params=params,
        name="order_metric",
    )(place, metric)
    rings, ordered = ring_gather(masked, ordered)
    sources = {}
    for index, (blocks, ring) in enumerate(zip(CHUNKS, rings)):
        fitted = pl.pallas_call(
            fit_kernel,
            in_specs=[in_vmem] * (n_aux + 1),
            out_specs=in_vmem,
            scratch_shapes=[pltpu.VMEM((blocks * width, aux_dev), jnp.float32)],
            out_shape=jax.ShapeDtypeStruct((blocks, *block_shape), jnp.bfloat16),
            compiler_params=params,
            name="fit",
        )(*[ring[hop] for hop in orders], ordered)
        for hop in GATHER_HOPS:
            sources[hop, index] = lax.ppermute(fitted, "pair", gather_perm(hop)) if hop > 0 else fitted

    messages, slots = 2 * SIDE, SIDE * CAP
    order = tuple(hop * 2 + flip for hop, flip in SPREAD_ORDER)
    picked = []
    for start in range(0, messages, PICK_GROUP):
        group = order[start : start + PICK_GROUP]
        picked += pl.pallas_call(
            functools.partial(pick_kernel, group),
            grid_spec=pltpu.PrefetchScalarGridSpec(
                num_scalar_prefetch=1,
                grid=(),
                in_specs=[in_vmem] * (SIDE * len(CHUNKS)),
                out_specs=[in_vmem] * len(group),
            ),
            out_shape=[jax.ShapeDtypeStruct((slots, *block_shape), jnp.bfloat16)] * len(group),
            compiler_params=params,
            name="pick",
        )(send, *[sources[hop, index] for hop in GATHER_HOPS for index in range(len(CHUNKS))])
    arrived = [
        lax.ppermute(message, "pair", spread_perm(hop, flip)) if (hop, flip) != (0, 0) else message
        for (hop, flip), message in zip(SPREAD_ORDER, picked)
    ]

    size = domain_max * width
    share = size // n_aux
    partial_values = []
    first_pair = 0
    for pairs in PAIR_CHUNKS:
        partial_values.append(
            pl.pallas_call(
                functools.partial(gram_kernel, first_pair, domain_max, order),
                grid_spec=pltpu.PrefetchScalarGridSpec(
                    num_scalar_prefetch=3,
                    grid=(),
                    in_specs=[in_vmem] * messages,
                    out_specs=in_vmem,
                    scratch_shapes=[pltpu.VMEM((pairs * domain_max, *block_shape), jnp.bfloat16)],
                ),
                out_shape=jax.ShapeDtypeStruct((n_aux, pairs, share, size), jnp.float32),
                compiler_params=params,
                name="gram",
            )(goes, counts, place, *arrived)
        )
        first_pair += pairs
    return ring_sum(partial_values)


def solution(mesh):
    return jax.shard_map(
        per_device,
        mesh=mesh,
        in_specs=(P("pair", "aux"), P(None, "aux"), P("pair", "aux"), P(), P("pair")),
        out_specs=P("pair", "aux", None),
        check_vma=False,
    )
```

time: 146 us -> 135 us (0.925)
  local copies, waits for them, and re-layouts: 8.72 us -> 4.46 us
  waiting for transfers between devices: 52.9 us -> 49.4 us
  other arithmetic: 4.07 us -> 2.13 us
    unnamed x27 -> x7, local copies, waits for them, and re-layouts: 8.32 us -> 4.05 us
    ppermute x13, waiting for transfers between devices: 27 us -> 23.6 us  [the longest x7 15.6 us: per_device(): lax.ppermute(message, 'pair', spread_perm(hop, flip))]
    ppermute x13, starting transfers between devices: 18.1 us -> 15.7 us  [the longest x6 8.45 us: per_device(): lax.ppermute(fitted, 'pair', gather_perm(hop))]
    ppermute x28, starting transfers between devices: 48.3 us -> 49.9 us  [shift(): lax.ppermute(value, 'aux', [(index, (index + by) % n_aux) for index in ra...]
    pallas_call x4 -> x18, Pallas kernels: 7.39 us -> 8.92 us  [the longest x4 4.22 us: per_device(): pl.pallas_call(functools.partial(pick_kernel, group), grid_spec=pltpu.Pre...]
  transfers between devices with their start and end apart: 41 -> 41, of which waited for: 21 -> 25; matrix products, arithmetic and copies ran while one was open for 3% -> 2% of each run, Pallas kernels for 4% -> 5%
where the time goes in v6:
time: 135 us; the launch traced here: 134 us
  starting transfers between devices  65.5 us (49%)
  waiting for transfers between devices  49.4 us (37%)
  Pallas kernels  11.8 us (9%)
  local copies, waits for them, and re-layouts  4.46 us (3%)
  other arithmetic  2.13 us (2%)
    ppermute x28, starting transfers between devices, shift(): lax.ppermute(value, 'aux', [(index, (index + by) % n_aux) for index in ra...  49.9 us
    ppermute x28, waiting for transfers between devices, shift(): lax.ppermute(value, 'aux', [(index, (index + by) % n_aux) for index in ra...  25.8 us
    ppermute x7, waiting for transfers between devices, per_device(): lax.ppermute(message, 'pair', spread_perm(hop, flip))  15.6 us
    ppermute x6, starting transfers between devices, per_device(): lax.ppermute(fitted, 'pair', gather_perm(hop))  8.45 us
    ppermute x6, waiting for transfers between devices, per_device(): lax.ppermute(fitted, 'pair', gather_perm(hop))  8.02 us
    ppermute x7, starting transfers between devices, per_device(): lax.ppermute(message, 'pair', spread_perm(hop, flip))  7.2 us
    pallas_call x4, Pallas kernels, per_device(): pl.pallas_call(functools.partial(pick_kernel, group), grid_spec=pltpu.Pre...  4.22 us
    unnamed x7, local copies, waits for them, and re-layouts  4.05 us
  transfers between devices with their start and end apart: 41, of which 25 were waited for; matrix products, arithmetic and copies ran while one was open for 2% of the time, Pallas kernels for 5%

profile of v6, /device:TPU:2, one launch (start us, length us, event | category | flops | bytes accessed | tf_op | source)
XLA Modules:
  0.0 133.7 jit_solution(10438250697353870213)
XLA Ops:
  3.9 4.0 %collective-permute-start.4 = (bf16[320,512]{1,0:T(8,128)(2,1)S(1)}, bf16[320,512]{1,0:T(8,128)(2,1)S(1)}, u32[]{:S(2)}, u32[]{:S(2)}) collective-permute-start(bf16[320,512]{1,0:T(8,128)(2,1)S(1)} %get-tuple-element.22.refs_0_), channel_id=1, source_target_pairs={{0,224},{32,0},{64,32},{96,64},{128,96},{160,128},{192,160},{224,1... | collective-permute-start | bytes 983048 | tf_op jit(solution)/shard_map/ppermute | solution.py:178
  7.9 3.2 %collective-permute-start.11 = (bf16[192,512]{1,0:T(8,128)(2,1)S(1)}, bf16[192,512]{1,0:T(8,128)(2,1)S(1)}, u32[]{:S(2)}, u32[]{:S(2)}) collective-permute-start(bf16[192,512]{1,0:T(8,128)(2,1)S(1)} %get-tuple-element.23.refs_0_), channel_id=1, source_target_pairs={{0,224},{32,0},{64,32},{96,64},{128,96},{160,128},{192,160},{224,1... | collective-permute-start | bytes 589832 | tf_op jit(solution)/shard_map/ppermute | solution.py:178
  12.7 3.7 %collective-permute-done.refs_1_ = bf16[320,512]{1,0:T(8,128)(2,1)S(1)} collective-permute-done((bf16[320,512]{1,0:T(8,128)(2,1)S(1)}, bf16[320,512]{1,0:T(8,128)(2,1)S(1)}, u32[]{:S(2)}, u32[]{:S(2)}) %collective-permute-start) | collective-permute-done | bytes 327712 | tf_op jit(solution)/shard_map/ppermute | solution.py:178
  16.4 3.4 %collective-permute-start.5 = (bf16[320,512]{1,0:T(8,128)(2,1)S(1)}, bf16[320,512]{1,0:T(8,128)(2,1)S(1)}, u32[]{:S(2)}, u32[]{:S(2)}) collective-permute-start(bf16[320,512]{1,0:T(8,128)(2,1)S(1)} %collective-permute-done.4.refs_7_), channel_id=1, source_target_pairs={{0,224},{32,0},{64,32},{96,64},{128,96},{160,128},{192,160},{224,1... | collective-permute-start | bytes 983048 | tf_op jit(solution)/shard_map/ppermute | solution.py:178
  20.3 3.7 %collective-permute-start.12 = (bf16[192,512]{1,0:T(8,128)(2,1)S(1)}, bf16[192,512]{1,0:T(8,128)(2,1)S(1)}, u32[]{:S(2)}, u32[]{:S(2)}) collective-permute-start(bf16[192,512]{1,0:T(8,128)(2,1)S(1)} %collective-permute-done.11.refs_7_), channel_id=1, source_target_pairs={{0,224},{32,0},{64,32},{96,64},{128,96},{160,128},{192,160},{224,1... | collective-permute-start | bytes 589832 | tf_op jit(solution)/shard_map/ppermute | solution.py:178
  27.9 3.7 %collective-permute-start.6 = (bf16[320,512]{1,0:T(8,128)(2,1)S(1)}, bf16[320,512]{1,0:T(8,128)(2,1)S(1)}, u32[]{:S(2)}, u32[]{:S(2)}) collective-permute-start(bf16[320,512]{1,0:T(8,128)(2,1)S(1)} %collective-permute-done.5.refs_6_), channel_id=1, source_target_pairs={{0,224},{32,0},{64,32},{96,64},{128,96},{160,128},{192,160},{224,1... | collective-permute-start | bytes 983048 | tf_op jit(solution)/shard_map/ppermute | solution.py:178
  32.1 3.7 %collective-permute-start.13 = (bf16[192,512]{1,0:T(8,128)(2,1)S(1)}, bf16[192,512]{1,0:T(8,128)(2,1)S(1)}, u32[]{:S(2)}, u32[]{:S(2)}) collective-permute-start(bf16[192,512]{1,0:T(8,128)(2,1)S(1)} %collective-permute-done.12.refs_6_), channel_id=1, source_target_pairs={{0,224},{32,0},{64,32},{96,64},{128,96},{160,128},{192,160},{224,1... | collective-permute-start | bytes 589832 | tf_op jit(solution)/shard_map/ppermute | solution.py:178
  35.8 4.7 %collective-permute-done.9.refs_2_ = bf16[192,512]{1,0:T(8,128)(2,1)S(1)} collective-permute-done((bf16[192,512]{1,0:T(8,128)(2,1)S(1)}, bf16[192,512]{1,0:T(8,128)(2,1)S(1)}, u32[]{:S(2)}, u32[]{:S(2)}) %collective-permute-start.9) | collective-permute-done | bytes 196640 | tf_op jit(solution)/shard_map/ppermute | solution.py:178
  41.6 3.7 %collective-permute-start.14 = (bf16[192,512]{1,0:T(8,128)(2,1)S(1)}, bf16[192,512]{1,0:T(8,128)(2,1)S(1)}, u32[]{:S(2)}, u32[]{:S(2)}) collective-permute-start(bf16[192,512]{1,0:T(8,128)(2,1)S(1)} %collective-permute-done.13.refs_5_), channel_id=1, source_target_pairs={{0,224},{32,0},{64,32},{96,64},{128,96},{160,128},{192,160},{224,1... | collective-permute-start | bytes 589832 | tf_op jit(solution)/shard_map/ppermute | solution.py:178
  45.3 2.9 %collective-permute-done.10.refs_3_ = bf16[192,512]{1,0:T(8,128)(2,1)S(1)} collective-permute-done((bf16[192,512]{1,0:T(8,128)(2,1)S(1)}, bf16[192,512]{1,0:T(8,128)(2,1)S(1)}, u32[]{:S(2)}, u32[]{:S(2)}) %collective-permute-start.10) | collective-permute-done | bytes 196640 | tf_op jit(solution)/shard_map/ppermute | solution.py:178
  60.7 2.4 %collective-permute-done.8.refs_0_ = bf16[5,64,512]{2,1,0:T(8,128)(2,1)S(1)} collective-permute-done((bf16[5,64,512]{2,1,0:T(8,128)(2,1)S(1)}, bf16[5,64,512]{2,1,0:T(8,128)(2,1)S(1)}, u32[]{:S(2)}, u32[]{:S(2)}) %collective-permute-start.8) | collective-permute-done | bytes 327712 | tf_op jit(solution)/shard_map/ppermute | solution.py:298
  64.6 4.1 %collective-permute-done.18.refs_4_ = bf16[5,64,512]{2,1,0:T(8,128)(2,1)S(1)} collective-permute-done((bf16[5,64,512]{2,1,0:T(8,128)(2,1)S(1)}, bf16[5,64,512]{2,1,0:T(8,128)(2,1)S(1)}, u32[]{:S(2)}, u32[]{:S(2)}) %collective-permute-start.18) | collective-permute-done | bytes 327712 | tf_op jit(solution)/shard_map/ppermute | solution.py:298
  78.5 2.6 %collective-permute-done.20.refs_0_ = bf16[8,64,512]{2,1,0:T(8,128)(2,1)S(1)} collective-permute-done((bf16[8,64,512]{2,1,0:T(8,128)(2,1)}, bf16[8,64,512]{2,1,0:T(8,128)(2,1)S(1)}, u32[]{:S(2)}, u32[]{:S(2)}) %collective-permute-start.20) | collective-permute-done | bytes 524320 | tf_op jit(solution)/shard_map/ppermute | solution.py:318
  83.2 4.8 %collective-permute-done.22.refs_2_ = bf16[8,64,512]{2,1,0:T(8,128)(2,1)S(1)} collective-permute-done((bf16[8,64,512]{2,1,0:T(8,128)(2,1)S(1)}, bf16[8,64,512]{2,1,0:T(8,128)(2,1)S(1)}, u32[]{:S(2)}, u32[]{:S(2)}) %collective-permute-start.22) | collective-permute-done | bytes 524320 | tf_op jit(solution)/shard_map/ppermute | solution.py:318
  91.9 4.0 %collective-permute-done.25.refs_5_ = bf16[8,64,512]{2,1,0:T(8,128)(2,1)S(1)} collective-permute-done((bf16[8,64,512]{2,1,0:T(8,128)(2,1)S(1)}, bf16[8,64,512]{2,1,0:T(8,128)(2,1)S(1)}, u32[]{:S(2)}, u32[]{:S(2)}) %collective-permute-start.25) | collective-permute-done | bytes 524320 | tf_op jit(solution)/shard_map/ppermute | solution.py:318
  99.7 3.3 %collective-permute-start.37 = (f32[5,32,256]{2,1,0:T(8,128)S(1)}, f32[5,32,256]{2,1,0:T(8,128)S(1)}, u32[]{:S(2)}, u32[]{:S(2)}) collective-permute-start(f32[5,32,256]{2,1,0:T(8,128)S(1)} %get-tuple-element.39), channel_id=1, source_target_pairs={{0,224},{32,0},{64,32},{96,64},{128,96},{160,128},{192,160},{224,1... | collective-permute-start | bytes 491528 | tf_op jit(solution)/shard_map/ppermute | solution.py:178
  105.9 3.8 %collective-permute-start.38 = (f32[5,32,256]{2,1,0:T(8,128)S(1)}, f32[5,32,256]{2,1,0:T(8,128)S(1)}, u32[]{:S(2)}, u32[]{:S(2)}) collective-permute-start(f32[5,32,256]{2,1,0:T(8,128)S(1)} %add_term.17), channel_id=1, source_target_pairs={{0,224},{32,0},{64,32},{96,64},{128,96},{160,128},{192,160},{224,1... | collective-permute-start | bytes 491528 | tf_op jit(solution)/shard_map/ppermute | solution.py:178
  109.9 3.0 %collective-permute-start.32 = (f32[5,32,256]{2,1,0:T(8,128)S(1)}, f32[5,32,256]{2,1,0:T(8,128)S(1)}, u32[]{:S(2)}, u32[]{:S(2)}) collective-permute-start(f32[5,32,256]{2,1,0:T(8,128)S(1)} %add_term.13), channel_id=1, source_target_pairs={{0,224},{32,0},{64,32},{96,64},{128,96},{160,128},{192,160},{224,1... | collective-permute-start | bytes 491528 | tf_op jit(solution)/shard_map/ppermute | solution.py:178
  114.8 3.3 %collective-permute-start.39 = (f32[5,32,256]{2,1,0:T(8,128)S(1)}, f32[5,32,256]{2,1,0:T(8,128)S(1)}, u32[]{:S(2)}, u32[]{:S(2)}) collective-permute-start(f32[5,32,256]{2,1,0:T(8,128)S(1)} %add_term.18), channel_id=1, source_target_pairs={{0,224},{32,0},{64,32},{96,64},{128,96},{160,128},{192,160},{224,1... | collective-permute-start | bytes 491528 | tf_op jit(solution)/shard_map/ppermute | solution.py:178
  118.1 3.2 %collective-permute-start.33 = (f32[5,32,256]{2,1,0:T(8,128)S(1)}, f32[5,32,256]{2,1,0:T(8,128)S(1)}, u32[]{:S(2)}, u32[]{:S(2)}) collective-permute-start(f32[5,32,256]{2,1,0:T(8,128)S(1)} %add_term.14), channel_id=1, source_target_pairs={{0,224},{32,0},{64,32},{96,64},{128,96},{160,128},{192,160},{224,1... | collective-permute-start | bytes 491528 | tf_op jit(solution)/shard_map/ppermute | solution.py:178
  121.4 2.2 %collective-permute-done.29.a_ref = f32[5,32,256]{2,1,0:T(8,128)S(1)} collective-permute-done((f32[5,32,256]{2,1,0:T(8,128)S(1)}, f32[5,32,256]{2,1,0:T(8,128)S(1)}, u32[]{:S(2)}, u32[]{:S(2)}) %collective-permute-start.29) | collective-permute-done | bytes 163872 | tf_op jit(solution)/shard_map/ppermute | solution.py:178
  123.8 3.3 %collective-permute-start.40 = (f32[5,32,256]{2,1,0:T(8,128)S(1)}, f32[5,32,256]{2,1,0:T(8,128)S(1)}, u32[]{:S(2)}, u32[]{:S(2)}) collective-permute-start(f32[5,32,256]{2,1,0:T(8,128)S(1)} %add_term.19), channel_id=1, source_target_pairs={{0,224},{32,0},{64,32},{96,64},{128,96},{160,128},{192,160},{224,1... | collective-permute-start | bytes 491528 | tf_op jit(solution)/shard_map/ppermute | solution.py:178
  127.1 2.3 %collective-permute-done.36.refs_4_ = f32[5,32,256]{2,1,0:T(8,128)S(1)} collective-permute-done((f32[5,32,256]{2,1,0:T(8,128)S(1)}, f32[5,32,256]{2,1,0:T(8,128)S(1)}, u32[]{:S(2)}, u32[]{:S(2)}) %collective-permute-start.36) | collective-permute-done | bytes 163872 | tf_op jit(solution)/shard_map/ppermute | solution.py:178
  129.4 3.5 %collective-permute-done.30.refs_1_ = f32[5,32,256]{2,1,0:T(8,128)S(1)} collective-permute-done((f32[5,32,256]{2,1,0:T(8,128)S(1)}, f32[5,32,256]{2,1,0:T(8,128)S(1)}, u32[]{:S(2)}, u32[]{:S(2)}) %collective-permute-start.30) | collective-permute-done | bytes 163872 | tf_op jit(solution)/shard_map/ppermute | solution.py:178
  (116 shorter events, 50.9 us)
Async XLA Ops:
  1.9 14.5 %collective-permute-start = (bf16[320,512]{1,0:T(8,128)(2,1)S(1)}, bf16[320,512]{1,0:T(8,128)(2,1)S(1)}, u32[]{:S(2)}, u32[]{:S(2)}) collective-permute-start(bf16[320,512]{1,0:T(8,128)(2,1)S(1)} %get-tuple-element.22.refs_0_), channel_id=1, source_target_pairs={{0,32},{32,64},{64,96},{96,128},{128,160},{160,192},{192,224},{224... | collective-permute-start | bytes 983048 | tf_op jit(solution)/shard_map/ppermute | solution.py:178
  3.9 12.5 %collective-permute-start.4 = (bf16[320,512]{1,0:T(8,128)(2,1)S(1)}, bf16[320,512]{1,0:T(8,128)(2,1)S(1)}, u32[]{:S(2)}, u32[]{:S(2)}) collective-permute-start(bf16[320,512]{1,0:T(8,128)(2,1)S(1)} %get-tuple-element.22.refs_0_), channel_id=1, source_target_pairs={{0,224},{32,0},{64,32},{96,64},{128,96},{160,128},{192,160},{224,1... | collective-permute-start | bytes 983048 | tf_op jit(solution)/shard_map/ppermute | solution.py:178
  7.9 24.0 %collective-permute-start.7 = (bf16[192,512]{1,0:T(8,128)(2,1)S(1)}, bf16[192,512]{1,0:T(8,128)(2,1)S(1)}, u32[]{:S(2)}, u32[]{:S(2)}) collective-permute-start(bf16[192,512]{1,0:T(8,128)(2,1)S(1)} %get-tuple-element.23.refs_0_), channel_id=1, source_target_pairs={{0,32},{32,64},{64,96},{96,128},{128,160},{160,192},{192,224},{224... | collective-permute-start | bytes 589832 | tf_op jit(solution)/shard_map/ppermute | solution.py:178
  7.9 12.3 %collective-permute-start.11 = (bf16[192,512]{1,0:T(8,128)(2,1)S(1)}, bf16[192,512]{1,0:T(8,128)(2,1)S(1)}, u32[]{:S(2)}, u32[]{:S(2)}) collective-permute-start(bf16[192,512]{1,0:T(8,128)(2,1)S(1)} %get-tuple-element.23.refs_0_), channel_id=1, source_target_pairs={{0,224},{32,0},{64,32},{96,64},{128,96},{160,128},{192,160},{224,1... | collective-permute-start | bytes 589832 | tf_op jit(solution)/shard_map/ppermute | solution.py:178
  16.4 10.4 %collective-permute-start.1 = (bf16[320,512]{1,0:T(8,128)(2,1)S(1)}, bf16[320,512]{1,0:T(8,128)(2,1)S(1)}, u32[]{:S(2)}, u32[]{:S(2)}) collective-permute-start(bf16[320,512]{1,0:T(8,128)(2,1)S(1)} %collective-permute-done.refs_1_), channel_id=1, source_target_pairs={{0,32},{32,64},{64,96},{96,128},{128,160},{160,192},{192,224},{224... | collective-permute-start | bytes 983048 | tf_op jit(solution)/shard_map/ppermute | solution.py:178
  16.4 11.5 %collective-permute-start.5 = (bf16[320,512]{1,0:T(8,128)(2,1)S(1)}, bf16[320,512]{1,0:T(8,128)(2,1)S(1)}, u32[]{:S(2)}, u32[]{:S(2)}) collective-permute-start(bf16[320,512]{1,0:T(8,128)(2,1)S(1)} %collective-permute-done.4.refs_7_), channel_id=1, source_target_pairs={{0,224},{32,0},{64,32},{96,64},{128,96},{160,128},{192,160},{224,1... | collective-permute-start | bytes 983048 | tf_op jit(solution)/shard_map/ppermute | solution.py:178
  20.3 11.9 %collective-permute-start.12 = (bf16[192,512]{1,0:T(8,128)(2,1)S(1)}, bf16[192,512]{1,0:T(8,128)(2,1)S(1)}, u32[]{:S(2)}, u32[]{:S(2)}) collective-permute-start(bf16[192,512]{1,0:T(8,128)(2,1)S(1)} %collective-permute-done.11.refs_7_), channel_id=1, source_target_pairs={{0,224},{32,0},{64,32},{96,64},{128,96},{160,128},{192,160},{224,1... | collective-permute-start | bytes 589832 | tf_op jit(solution)/shard_map/ppermute | solution.py:178
  26.8 18.5 %collective-permute-start.2 = (bf16[320,512]{1,0:T(8,128)(2,1)S(1)}, bf16[320,512]{1,0:T(8,128)(2,1)S(1)}, u32[]{:S(2)}, u32[]{:S(2)}) collective-permute-start(bf16[320,512]{1,0:T(8,128)(2,1)S(1)} %collective-permute-done.1.refs_2_), channel_id=1, source_target_pairs={{0,32},{32,64},{64,96},{96,128},{128,160},{160,192},{192,224},{224... | collective-permute-start | bytes 983048 | tf_op jit(solution)/shard_map/ppermute | solution.py:178
  27.9 13.7 %collective-permute-start.6 = (bf16[320,512]{1,0:T(8,128)(2,1)S(1)}, bf16[320,512]{1,0:T(8,128)(2,1)S(1)}, u32[]{:S(2)}, u32[]{:S(2)}) collective-permute-start(bf16[320,512]{1,0:T(8,128)(2,1)S(1)} %collective-permute-done.5.refs_6_), channel_id=1, source_target_pairs={{0,224},{32,0},{64,32},{96,64},{128,96},{160,128},{192,160},{224,1... | collective-permute-start | bytes 983048 | tf_op jit(solution)/shard_map/ppermute | solution.py:178
  32.1 9.5 %collective-permute-start.13 = (bf16[192,512]{1,0:T(8,128)(2,1)S(1)}, bf16[192,512]{1,0:T(8,128)(2,1)S(1)}, u32[]{:S(2)}, u32[]{:S(2)}) collective-permute-start(bf16[192,512]{1,0:T(8,128)(2,1)S(1)} %collective-permute-done.12.refs_6_), channel_id=1, source_target_pairs={{0,224},{32,0},{64,32},{96,64},{128,96},{160,128},{192,160},{224,1... | collective-permute-start | bytes 589832 | tf_op jit(solution)/shard_map/ppermute | solution.py:178
  45.3 9.1 %collective-permute-start.3 = (bf16[320,512]{1,0:T(8,128)(2,1)S(1)}, bf16[320,512]{1,0:T(8,128)(2,1)S(1)}, u32[]{:S(2)}, u32[]{:S(2)}) collective-permute-start(bf16[320,512]{1,0:T(8,128)(2,1)S(1)} %collective-permute-done.2.refs_3_), channel_id=1, source_target_pairs={{0,32},{32,64},{64,96},{96,128},{128,160},{160,192},{192,224},{224... | collective-permute-start | bytes 983048 | tf_op jit(solution)/shard_map/ppermute | solution.py:178
  51.0 9.6 %collective-permute-start.17 = (bf16[3,64,512]{2,1,0:T(8,128)(2,1)S(1)}, bf16[3,64,512]{2,1,0:T(8,128)(2,1)S(1)}, u32[]{:S(2)}, u32[]{:S(2)}) collective-permute-start(bf16[3,64,512]{2,1,0:T(8,128)(2,1)S(1)} %fit.3.refs_7_), channel_id=1, source_target_pairs={{0,24},{1,7},{2,26},{3,1},{4,28},{5,3},{6,30},{7,5},{8,0},{9,15},{... | collective-permute-start | bytes 589832 | tf_op jit(solution)/shard_map/ppermute | solution.py:298
  51.6 9.1 %collective-permute-start.19 = (bf16[3,64,512]{2,1,0:T(8,128)(2,1)S(1)}, bf16[3,64,512]{2,1,0:T(8,128)(2,1)S(1)}, u32[]{:S(2)}, u32[]{:S(2)}) collective-permute-start(bf16[3,64,512]{2,1,0:T(8,128)(2,1)S(1)} %fit.3.refs_7_), channel_id=1, source_target_pairs={{0,16},{1,5},{2,18},{3,7},{4,20},{5,1},{6,22},{7,3},{8,24},{9,13},... | collective-permute-start | bytes 589832 | tf_op jit(solution)/shard_map/ppermute | solution.py:298
  58.0 10.7 %collective-permute-start.18 = (bf16[5,64,512]{2,1,0:T(8,128)(2,1)S(1)}, bf16[5,64,512]{2,1,0:T(8,128)(2,1)S(1)}, u32[]{:S(2)}, u32[]{:S(2)}) collective-permute-start(bf16[5,64,512]{2,1,0:T(8,128)(2,1)S(1)} %fit.2.refs_6_), channel_id=1, source_target_pairs={{0,16},{1,5},{2,18},{3,7},{4,20},{5,1},{6,22},{7,3},{8,24},{9,13},... | collective-permute-start | bytes 983048 | tf_op jit(solution)/shard_map/ppermute | solution.py:298
  70.5 10.6 %collective-permute-start.20 = (bf16[8,64,512]{2,1,0:T(8,128)(2,1)}, bf16[8,64,512]{2,1,0:T(8,128)(2,1)S(1)}, u32[]{:S(2)}, u32[]{:S(2)}) collective-permute-start(bf16[8,64,512]{2,1,0:T(8,128)(2,1)} %get-tuple-element.31), channel_id=1, source_target_pairs={{0,2},{1,9},{2,4},{3,11},{4,6},{5,13},{6,0},{7,15},{8,10},{9,17},{... | collective-permute-start | bytes 1572872 | tf_op jit(solution)/shard_map/ppermute | solution.py:318
  72.1 9.4 %collective-permute-start.21 = (bf16[8,64,512]{2,1,0:T(8,128)(2,1)}, bf16[8,64,512]{2,1,0:T(8,128)(2,1)S(1)}, u32[]{:S(2)}, u32[]{:S(2)}) collective-permute-start(bf16[8,64,512]{2,1,0:T(8,128)(2,1)} %get-tuple-element.32), channel_id=1, source_target_pairs={{0,6},{1,25},{2,0},{3,27},{4,2},{5,29},{6,4},{7,31},{8,14},{9,1},{... | collective-permute-start | bytes 1572872 | tf_op jit(solution)/shard_map/ppermute | solution.py:318
  74.5 13.5 %collective-permute-start.22 = (bf16[8,64,512]{2,1,0:T(8,128)(2,1)S(1)}, bf16[8,64,512]{2,1,0:T(8,128)(2,1)S(1)}, u32[]{:S(2)}, u32[]{:S(2)}) collective-permute-start(bf16[8,64,512]{2,1,0:T(8,128)(2,1)S(1)} %get-tuple-element.33), channel_id=1, source_target_pairs={{0,4},{1,17},{2,6},{3,19},{4,0},{5,21},{6,2},{7,23},{8,12},{9,25},... | collective-permute-start | bytes 1572872 | tf_op jit(solution)/shard_map/ppermute | solution.py:318
  76.6 13.6 %collective-permute-start.23 = (bf16[8,64,512]{2,1,0:T(8,128)(2,1)S(1)}, bf16[8,64,512]{2,1,0:T(8,128)(2,1)S(1)}, u32[]{:S(2)}, u32[]{:S(2)}) collective-permute-start(bf16[8,64,512]{2,1,0:T(8,128)(2,1)S(1)} %get-tuple-element.34), channel_id=1, source_target_pairs={{0,3},{1,8},{2,5},{3,10},{4,7},{5,12},{6,1},{7,14},{8,11},{9,16},{... | collective-permute-start | bytes 1572872 | tf_op jit(solution)/shard_map/ppermute | solution.py:318
  77.4 14.5 %collective-permute-start.24 = (bf16[8,64,512]{2,1,0:T(8,128)(2,1)S(1)}, bf16[8,64,512]{2,1,0:T(8,128)(2,1)S(1)}, u32[]{:S(2)}, u32[]{:S(2)}) collective-permute-start(bf16[8,64,512]{2,1,0:T(8,128)(2,1)S(1)} %get-tuple-element.35), channel_id=1, source_target_pairs={{0,7},{1,24},{2,1},{3,26},{4,3},{5,28},{6,5},{7,30},{8,15},{9,0},{... | collective-permute-start | bytes 1572872 | tf_op jit(solution)/shard_map/ppermute | solution.py:318
  81.1 14.8 %collective-permute-start.25 = (bf16[8,64,512]{2,1,0:T(8,128)(2,1)S(1)}, bf16[8,64,512]{2,1,0:T(8,128)(2,1)S(1)}, u32[]{:S(2)}, u32[]{:S(2)}) collective-permute-start(bf16[8,64,512]{2,1,0:T(8,128)(2,1)S(1)} %get-tuple-element.36), channel_id=1, source_target_pairs={{0,5},{1,16},{2,7},{3,18},{4,1},{5,20},{6,3},{7,22},{8,13},{9,24},... | collective-permute-start | bytes 1572872 | tf_op jit(solution)/shard_map/ppermute | solution.py:318
  81.5 14.4 %collective-permute-start.26 = (bf16[8,64,512]{2,1,0:T(8,128)(2,1)S(1)}, bf16[8,64,512]{2,1,0:T(8,128)(2,1)S(1)}, u32[]{:S(2)}, u32[]{:S(2)}) collective-permute-start(bf16[8,64,512]{2,1,0:T(8,128)(2,1)S(1)} %get-tuple-element.37), channel_id=1, source_target_pairs={{0,1},{1,0},{2,3},{3,2},{4,5},{5,4},{6,7},{7,6},{8,9},{9,8},{10,11... | collective-permute-start | bytes 1572872 | tf_op jit(solution)/shard_map/ppermute | solution.py:318
  105.1 9.5 %collective-permute-start.28 = (f32[5,32,256]{2,1,0:T(8,128)S(1)}, f32[5,32,256]{2,1,0:T(8,128)S(1)}, u32[]{:S(2)}, u32[]{:S(2)}) collective-permute-start(f32[5,32,256]{2,1,0:T(8,128)S(1)} %add_term.10), channel_id=1, source_target_pairs={{0,32},{32,64},{64,96},{96,128},{128,160},{160,192},{192,224},{224... | collective-permute-start | bytes 491528 | tf_op jit(solution)/shard_map/ppermute | solution.py:178
  123.7 9.3 %collective-permute-start.30 = (f32[5,32,256]{2,1,0:T(8,128)S(1)}, f32[5,32,256]{2,1,0:T(8,128)S(1)}, u32[]{:S(2)}, u32[]{:S(2)}) collective-permute-start(f32[5,32,256]{2,1,0:T(8,128)S(1)} %add_term.12), channel_id=1, source_target_pairs={{0,32},{32,64},{64,96},{96,128},{128,160},{160,192},{192,224},{224... | collective-permute-start | bytes 491528 | tf_op jit(solution)/shard_map/ppermute | solution.py:178
  123.8 9.1 %collective-permute-start.40 = (f32[5,32,256]{2,1,0:T(8,128)S(1)}, f32[5,32,256]{2,1,0:T(8,128)S(1)}, u32[]{:S(2)}, u32[]{:S(2)}) collective-permute-start(f32[5,32,256]{2,1,0:T(8,128)S(1)} %add_term.19), channel_id=1, source_target_pairs={{0,224},{32,0},{64,32},{96,64},{128,96},{160,128},{192,160},{224,1... | collective-permute-start | bytes 491528 | tf_op jit(solution)/shard_map/ppermute | solution.py:178
  (20 other events, 156.8 us)

commit v7 on v6

--- a/solution.py
+++ b/solution.py
@@ -12,7 +12,7 @@
 PAIR_CHUNKS = (5, 5)
 SIDE = 4
 GATHER_HOPS = (1, 3, 2, 0)
-SPREAD_ORDER = ((1, 0), (3, 0), (2, 0), (1, 1), (3, 1), (2, 1), (0, 1), (0, 0))
+SPREAD_ORDER = ((1, 0), (3, 0), (1, 1), (3, 1), (2, 0), (2, 1), (0, 1), (0, 0))
 PICK_GROUP = 2
 CAP = 2
 

time: 135 us -> 136 us (level)
  no operation moved by 1% of the time
where the time goes in v7:
time: 136 us; the launch traced here: 134 us
  starting transfers between devices  65.1 us (48%)
  waiting for transfers between devices  50 us (37%)
  Pallas kernels  11.8 us (9%)
  local copies, waits for them, and re-layouts  4.46 us (3%)
  other arithmetic  2.13 us (2%)
    ppermute x28, starting transfers between devices, shift(): lax.ppermute(value, 'aux', [(index, (index + by) % n_aux) for index in ra...  49.5 us
    ppermute x28, waiting for transfers between devices, shift(): lax.ppermute(value, 'aux', [(index, (index + by) % n_aux) for index in ra...  26.3 us
    ppermute x7, waiting for transfers between devices, per_device(): lax.ppermute(message, 'pair', spread_perm(hop, flip))  15.6 us
    ppermute x6, starting transfers between devices, per_device(): lax.ppermute(fitted, 'pair', gather_perm(hop))  8.45 us
    ppermute x6, waiting for transfers between devices, per_device(): lax.ppermute(fitted, 'pair', gather_perm(hop))  8.02 us
    ppermute x7, starting transfers between devices, per_device(): lax.ppermute(message, 'pair', spread_perm(hop, flip))  7.14 us
    pallas_call x4, Pallas kernels, per_device(): pl.pallas_call(functools.partial(pick_kernel, group), grid_spec=pltpu.Pre...  4.22 us
    unnamed x7, local copies, waits for them, and re-layouts  4.05 us
  transfers between devices with their start and end apart: 41, of which 25 were waited for; matrix products, arithmetic and copies ran while one was open for 2% of the time, Pallas kernels for 5%

profile of v7, /device:TPU:2, one launch (start us, length us, event | category | flops | bytes accessed | tf_op | source)
XLA Modules:
  0.0 133.8 jit_solution(3848030356833296184)
XLA Ops:
  3.9 4.0 %collective-permute-start.4 = (bf16[320,512]{1,0:T(8,128)(2,1)S(1)}, bf16[320,512]{1,0:T(8,128)(2,1)S(1)}, u32[]{:S(2)}, u32[]{:S(2)}) collective-permute-start(bf16[320,512]{1,0:T(8,128)(2,1)S(1)} %get-tuple-element.22.refs_0_), channel_id=1, source_target_pairs={{0,224},{32,0},{64,32},{96,64},{128,96},{160,128},{192,160},{224,1... | collective-permute-start | bytes 983048 | tf_op jit(solution)/shard_map/ppermute | solution.py:178
  7.9 3.2 %collective-permute-start.11 = (bf16[192,512]{1,0:T(8,128)(2,1)S(1)}, bf16[192,512]{1,0:T(8,128)(2,1)S(1)}, u32[]{:S(2)}, u32[]{:S(2)}) collective-permute-start(bf16[192,512]{1,0:T(8,128)(2,1)S(1)} %get-tuple-element.23.refs_0_), channel_id=1, source_target_pairs={{0,224},{32,0},{64,32},{96,64},{128,96},{160,128},{192,160},{224,1... | collective-permute-start | bytes 589832 | tf_op jit(solution)/shard_map/ppermute | solution.py:178
  12.7 3.7 %collective-permute-done.refs_1_ = bf16[320,512]{1,0:T(8,128)(2,1)S(1)} collective-permute-done((bf16[320,512]{1,0:T(8,128)(2,1)S(1)}, bf16[320,512]{1,0:T(8,128)(2,1)S(1)}, u32[]{:S(2)}, u32[]{:S(2)}) %collective-permute-start) | collective-permute-done | bytes 327712 | tf_op jit(solution)/shard_map/ppermute | solution.py:178
  16.4 3.4 %collective-permute-start.5 = (bf16[320,512]{1,0:T(8,128)(2,1)S(1)}, bf16[320,512]{1,0:T(8,128)(2,1)S(1)}, u32[]{:S(2)}, u32[]{:S(2)}) collective-permute-start(bf16[320,512]{1,0:T(8,128)(2,1)S(1)} %collective-permute-done.4.refs_7_), channel_id=1, source_target_pairs={{0,224},{32,0},{64,32},{96,64},{128,96},{160,128},{192,160},{224,1... | collective-permute-start | bytes 983048 | tf_op jit(solution)/shard_map/ppermute | solution.py:178
  20.3 3.7 %collective-permute-start.12 = (bf16[192,512]{1,0:T(8,128)(2,1)S(1)}, bf16[192,512]{1,0:T(8,128)(2,1)S(1)}, u32[]{:S(2)}, u32[]{:S(2)}) collective-permute-start(bf16[192,512]{1,0:T(8,128)(2,1)S(1)} %collective-permute-done.11.refs_7_), channel_id=1, source_target_pairs={{0,224},{32,0},{64,32},{96,64},{128,96},{160,128},{192,160},{224,1... | collective-permute-start | bytes 589832 | tf_op jit(solution)/shard_map/ppermute | solution.py:178
  27.9 3.7 %collective-permute-start.6 = (bf16[320,512]{1,0:T(8,128)(2,1)S(1)}, bf16[320,512]{1,0:T(8,128)(2,1)S(1)}, u32[]{:S(2)}, u32[]{:S(2)}) collective-permute-start(bf16[320,512]{1,0:T(8,128)(2,1)S(1)} %collective-permute-done.5.refs_6_), channel_id=1, source_target_pairs={{0,224},{32,0},{64,32},{96,64},{128,96},{160,128},{192,160},{224,1... | collective-permute-start | bytes 983048 | tf_op jit(solution)/shard_map/ppermute | solution.py:178
  32.1 3.7 %collective-permute-start.13 = (bf16[192,512]{1,0:T(8,128)(2,1)S(1)}, bf16[192,512]{1,0:T(8,128)(2,1)S(1)}, u32[]{:S(2)}, u32[]{:S(2)}) collective-permute-start(bf16[192,512]{1,0:T(8,128)(2,1)S(1)} %collective-permute-done.12.refs_6_), channel_id=1, source_target_pairs={{0,224},{32,0},{64,32},{96,64},{128,96},{160,128},{192,160},{224,1... | collective-permute-start | bytes 589832 | tf_op jit(solution)/shard_map/ppermute | solution.py:178
  35.8 4.7 %collective-permute-done.9.refs_2_ = bf16[192,512]{1,0:T(8,128)(2,1)S(1)} collective-permute-done((bf16[192,512]{1,0:T(8,128)(2,1)S(1)}, bf16[192,512]{1,0:T(8,128)(2,1)S(1)}, u32[]{:S(2)}, u32[]{:S(2)}) %collective-permute-start.9) | collective-permute-done | bytes 196640 | tf_op jit(solution)/shard_map/ppermute | solution.py:178
  41.6 3.7 %collective-permute-start.14 = (bf16[192,512]{1,0:T(8,128)(2,1)S(1)}, bf16[192,512]{1,0:T(8,128)(2,1)S(1)}, u32[]{:S(2)}, u32[]{:S(2)}) collective-permute-start(bf16[192,512]{1,0:T(8,128)(2,1)S(1)} %collective-permute-done.13.refs_5_), channel_id=1, source_target_pairs={{0,224},{32,0},{64,32},{96,64},{128,96},{160,128},{192,160},{224,1... | collective-permute-start | bytes 589832 | tf_op jit(solution)/shard_map/ppermute | solution.py:178
  45.3 2.9 %collective-permute-done.10.refs_3_ = bf16[192,512]{1,0:T(8,128)(2,1)S(1)} collective-permute-done((bf16[192,512]{1,0:T(8,128)(2,1)S(1)}, bf16[192,512]{1,0:T(8,128)(2,1)S(1)}, u32[]{:S(2)}, u32[]{:S(2)}) %collective-permute-start.10) | collective-permute-done | bytes 196640 | tf_op jit(solution)/shard_map/ppermute | solution.py:178
  60.7 2.4 %collective-permute-done.8.refs_0_ = bf16[5,64,512]{2,1,0:T(8,128)(2,1)S(1)} collective-permute-done((bf16[5,64,512]{2,1,0:T(8,128)(2,1)S(1)}, bf16[5,64,512]{2,1,0:T(8,128)(2,1)S(1)}, u32[]{:S(2)}, u32[]{:S(2)}) %collective-permute-start.8) | collective-permute-done | bytes 327712 | tf_op jit(solution)/shard_map/ppermute | solution.py:298
  64.6 4.1 %collective-permute-done.18.refs_4_ = bf16[5,64,512]{2,1,0:T(8,128)(2,1)S(1)} collective-permute-done((bf16[5,64,512]{2,1,0:T(8,128)(2,1)S(1)}, bf16[5,64,512]{2,1,0:T(8,128)(2,1)S(1)}, u32[]{:S(2)}, u32[]{:S(2)}) %collective-permute-start.18) | collective-permute-done | bytes 327712 | tf_op jit(solution)/shard_map/ppermute | solution.py:298
  78.4 2.6 %collective-permute-done.20.refs_0_ = bf16[8,64,512]{2,1,0:T(8,128)(2,1)S(1)} collective-permute-done((bf16[8,64,512]{2,1,0:T(8,128)(2,1)}, bf16[8,64,512]{2,1,0:T(8,128)(2,1)S(1)}, u32[]{:S(2)}, u32[]{:S(2)}) %collective-permute-start.20) | collective-permute-done | bytes 524320 | tf_op jit(solution)/shard_map/ppermute | solution.py:318
  86.3 7.3 %collective-permute-done.24.refs_4_ = bf16[8,64,512]{2,1,0:T(8,128)(2,1)S(1)} collective-permute-done((bf16[8,64,512]{2,1,0:T(8,128)(2,1)S(1)}, bf16[8,64,512]{2,1,0:T(8,128)(2,1)S(1)}, u32[]{:S(2)}, u32[]{:S(2)}) %collective-permute-start.24) | collective-permute-done | bytes 524320 | tf_op jit(solution)/shard_map/ppermute | solution.py:318
  93.6 2.3 %collective-permute-done.25.refs_5_ = bf16[8,64,512]{2,1,0:T(8,128)(2,1)S(1)} collective-permute-done((bf16[8,64,512]{2,1,0:T(8,128)(2,1)S(1)}, bf16[8,64,512]{2,1,0:T(8,128)(2,1)S(1)}, u32[]{:S(2)}, u32[]{:S(2)}) %collective-permute-start.25) | collective-permute-done | bytes 524320 | tf_op jit(solution)/shard_map/ppermute | solution.py:318
  99.7 3.3 %collective-permute-start.37 = (f32[5,32,256]{2,1,0:T(8,128)S(1)}, f32[5,32,256]{2,1,0:T(8,128)S(1)}, u32[]{:S(2)}, u32[]{:S(2)}) collective-permute-start(f32[5,32,256]{2,1,0:T(8,128)S(1)} %get-tuple-element.39), channel_id=1, source_target_pairs={{0,224},{32,0},{64,32},{96,64},{128,96},{160,128},{192,160},{224,1... | collective-permute-start | bytes 491528 | tf_op jit(solution)/shard_map/ppermute | solution.py:178
  105.9 3.8 %collective-permute-start.38 = (f32[5,32,256]{2,1,0:T(8,128)S(1)}, f32[5,32,256]{2,1,0:T(8,128)S(1)}, u32[]{:S(2)}, u32[]{:S(2)}) collective-permute-start(f32[5,32,256]{2,1,0:T(8,128)S(1)} %add_term.17), channel_id=1, source_target_pairs={{0,224},{32,0},{64,32},{96,64},{128,96},{160,128},{192,160},{224,1... | collective-permute-start | bytes 491528 | tf_op jit(solution)/shard_map/ppermute | solution.py:178
  109.9 3.1 %collective-permute-start.32 = (f32[5,32,256]{2,1,0:T(8,128)S(1)}, f32[5,32,256]{2,1,0:T(8,128)S(1)}, u32[]{:S(2)}, u32[]{:S(2)}) collective-permute-start(f32[5,32,256]{2,1,0:T(8,128)S(1)} %add_term.13), channel_id=1, source_target_pairs={{0,224},{32,0},{64,32},{96,64},{128,96},{160,128},{192,160},{224,1... | collective-permute-start | bytes 491528 | tf_op jit(solution)/shard_map/ppermute | solution.py:178
  113.1 2.3 %collective-permute-done.28.a_ref = f32[5,32,256]{2,1,0:T(8,128)S(1)} collective-permute-done((f32[5,32,256]{2,1,0:T(8,128)S(1)}, f32[5,32,256]{2,1,0:T(8,128)S(1)}, u32[]{:S(2)}, u32[]{:S(2)}) %collective-permute-start.28) | collective-permute-done | bytes 163872 | tf_op jit(solution)/shard_map/ppermute | solution.py:178
  115.6 3.3 %collective-permute-start.39 = (f32[5,32,256]{2,1,0:T(8,128)S(1)}, f32[5,32,256]{2,1,0:T(8,128)S(1)}, u32[]{:S(2)}, u32[]{:S(2)}) collective-permute-start(f32[5,32,256]{2,1,0:T(8,128)S(1)} %add_term.18), channel_id=1, source_target_pairs={{0,224},{32,0},{64,32},{96,64},{128,96},{160,128},{192,160},{224,1... | collective-permute-start | bytes 491528 | tf_op jit(solution)/shard_map/ppermute | solution.py:178
  118.9 2.4 %collective-permute-start.33 = (f32[5,32,256]{2,1,0:T(8,128)S(1)}, f32[5,32,256]{2,1,0:T(8,128)S(1)}, u32[]{:S(2)}, u32[]{:S(2)}) collective-permute-start(f32[5,32,256]{2,1,0:T(8,128)S(1)} %add_term.14), channel_id=1, source_target_pairs={{0,224},{32,0},{64,32},{96,64},{128,96},{160,128},{192,160},{224,1... | collective-permute-start | bytes 491528 | tf_op jit(solution)/shard_map/ppermute | solution.py:178
  121.5 2.4 %collective-permute-done.29.a_ref = f32[5,32,256]{2,1,0:T(8,128)S(1)} collective-permute-done((f32[5,32,256]{2,1,0:T(8,128)S(1)}, f32[5,32,256]{2,1,0:T(8,128)S(1)}, u32[]{:S(2)}, u32[]{:S(2)}) %collective-permute-start.29) | collective-permute-done | bytes 163872 | tf_op jit(solution)/shard_map/ppermute | solution.py:178
  124.0 3.3 %collective-permute-start.40 = (f32[5,32,256]{2,1,0:T(8,128)S(1)}, f32[5,32,256]{2,1,0:T(8,128)S(1)}, u32[]{:S(2)}, u32[]{:S(2)}) collective-permute-start(f32[5,32,256]{2,1,0:T(8,128)S(1)} %add_term.19), channel_id=1, source_target_pairs={{0,224},{32,0},{64,32},{96,64},{128,96},{160,128},{192,160},{224,1... | collective-permute-start | bytes 491528 | tf_op jit(solution)/shard_map/ppermute | solution.py:178
  129.5 3.5 %collective-permute-done.30.refs_1_ = f32[5,32,256]{2,1,0:T(8,128)S(1)} collective-permute-done((f32[5,32,256]{2,1,0:T(8,128)S(1)}, f32[5,32,256]{2,1,0:T(8,128)S(1)}, u32[]{:S(2)}, u32[]{:S(2)}) %collective-permute-start.30) | collective-permute-done | bytes 163872 | tf_op jit(solution)/shard_map/ppermute | solution.py:178
  (116 shorter events, 50.7 us)
Async XLA Ops:
  1.9 14.5 %collective-permute-start = (bf16[320,512]{1,0:T(8,128)(2,1)S(1)}, bf16[320,512]{1,0:T(8,128)(2,1)S(1)}, u32[]{:S(2)}, u32[]{:S(2)}) collective-permute-start(bf16[320,512]{1,0:T(8,128)(2,1)S(1)} %get-tuple-element.22.refs_0_), channel_id=1, source_target_pairs={{0,32},{32,64},{64,96},{96,128},{128,160},{160,192},{192,224},{224... | collective-permute-start | bytes 983048 | tf_op jit(solution)/shard_map/ppermute | solution.py:178
  3.9 12.5 %collective-permute-start.4 = (bf16[320,512]{1,0:T(8,128)(2,1)S(1)}, bf16[320,512]{1,0:T(8,128)(2,1)S(1)}, u32[]{:S(2)}, u32[]{:S(2)}) collective-permute-start(bf16[320,512]{1,0:T(8,128)(2,1)S(1)} %get-tuple-element.22.refs_0_), channel_id=1, source_target_pairs={{0,224},{32,0},{64,32},{96,64},{128,96},{160,128},{192,160},{224,1... | collective-permute-start | bytes 983048 | tf_op jit(solution)/shard_map/ppermute | solution.py:178
  7.9 24.0 %collective-permute-start.7 = (bf16[192,512]{1,0:T(8,128)(2,1)S(1)}, bf16[192,512]{1,0:T(8,128)(2,1)S(1)}, u32[]{:S(2)}, u32[]{:S(2)}) collective-permute-start(bf16[192,512]{1,0:T(8,128)(2,1)S(1)} %get-tuple-element.23.refs_0_), channel_id=1, source_target_pairs={{0,32},{32,64},{64,96},{96,128},{128,160},{160,192},{192,224},{224... | collective-permute-start | bytes 589832 | tf_op jit(solution)/shard_map/ppermute | solution.py:178
  7.9 12.3 %collective-permute-start.11 = (bf16[192,512]{1,0:T(8,128)(2,1)S(1)}, bf16[192,512]{1,0:T(8,128)(2,1)S(1)}, u32[]{:S(2)}, u32[]{:S(2)}) collective-permute-start(bf16[192,512]{1,0:T(8,128)(2,1)S(1)} %get-tuple-element.23.refs_0_), channel_id=1, source_target_pairs={{0,224},{32,0},{64,32},{96,64},{128,96},{160,128},{192,160},{224,1... | collective-permute-start | bytes 589832 | tf_op jit(solution)/shard_map/ppermute | solution.py:178
  16.4 10.4 %collective-permute-start.1 = (bf16[320,512]{1,0:T(8,128)(2,1)S(1)}, bf16[320,512]{1,0:T(8,128)(2,1)S(1)}, u32[]{:S(2)}, u32[]{:S(2)}) collective-permute-start(bf16[320,512]{1,0:T(8,128)(2,1)S(1)} %collective-permute-done.refs_1_), channel_id=1, source_target_pairs={{0,32},{32,64},{64,96},{96,128},{128,160},{160,192},{192,224},{224... | collective-permute-start | bytes 983048 | tf_op jit(solution)/shard_map/ppermute | solution.py:178
  16.4 11.5 %collective-permute-start.5 = (bf16[320,512]{1,0:T(8,128)(2,1)S(1)}, bf16[320,512]{1,0:T(8,128)(2,1)S(1)}, u32[]{:S(2)}, u32[]{:S(2)}) collective-permute-start(bf16[320,512]{1,0:T(8,128)(2,1)S(1)} %collective-permute-done.4.refs_7_), channel_id=1, source_target_pairs={{0,224},{32,0},{64,32},{96,64},{128,96},{160,128},{192,160},{224,1... | collective-permute-start | bytes 983048 | tf_op jit(solution)/shard_map/ppermute | solution.py:178
  20.3 11.9 %collective-permute-start.12 = (bf16[192,512]{1,0:T(8,128)(2,1)S(1)}, bf16[192,512]{1,0:T(8,128)(2,1)S(1)}, u32[]{:S(2)}, u32[]{:S(2)}) collective-permute-start(bf16[192,512]{1,0:T(8,128)(2,1)S(1)} %collective-permute-done.11.refs_7_), channel_id=1, source_target_pairs={{0,224},{32,0},{64,32},{96,64},{128,96},{160,128},{192,160},{224,1... | collective-permute-start | bytes 589832 | tf_op jit(solution)/shard_map/ppermute | solution.py:178
  26.8 18.5 %collective-permute-start.2 = (bf16[320,512]{1,0:T(8,128)(2,1)S(1)}, bf16[320,512]{1,0:T(8,128)(2,1)S(1)}, u32[]{:S(2)}, u32[]{:S(2)}) collective-permute-start(bf16[320,512]{1,0:T(8,128)(2,1)S(1)} %collective-permute-done.1.refs_2_), channel_id=1, source_target_pairs={{0,32},{32,64},{64,96},{96,128},{128,160},{160,192},{192,224},{224... | collective-permute-start | bytes 983048 | tf_op jit(solution)/shard_map/ppermute | solution.py:178
  27.9 13.7 %collective-permute-start.6 = (bf16[320,512]{1,0:T(8,128)(2,1)S(1)}, bf16[320,512]{1,0:T(8,128)(2,1)S(1)}, u32[]{:S(2)}, u32[]{:S(2)}) collective-permute-start(bf16[320,512]{1,0:T(8,128)(2,1)S(1)} %collective-permute-done.5.refs_6_), channel_id=1, source_target_pairs={{0,224},{32,0},{64,32},{96,64},{128,96},{160,128},{192,160},{224,1... | collective-permute-start | bytes 983048 | tf_op jit(solution)/shard_map/ppermute | solution.py:178
  32.1 9.5 %collective-permute-start.13 = (bf16[192,512]{1,0:T(8,128)(2,1)S(1)}, bf16[192,512]{1,0:T(8,128)(2,1)S(1)}, u32[]{:S(2)}, u32[]{:S(2)}) collective-permute-start(bf16[192,512]{1,0:T(8,128)(2,1)S(1)} %collective-permute-done.12.refs_6_), channel_id=1, source_target_pairs={{0,224},{32,0},{64,32},{96,64},{128,96},{160,128},{192,160},{224,1... | collective-permute-start | bytes 589832 | tf_op jit(solution)/shard_map/ppermute | solution.py:178
  45.3 9.1 %collective-permute-start.3 = (bf16[320,512]{1,0:T(8,128)(2,1)S(1)}, bf16[320,512]{1,0:T(8,128)(2,1)S(1)}, u32[]{:S(2)}, u32[]{:S(2)}) collective-permute-start(bf16[320,512]{1,0:T(8,128)(2,1)S(1)} %collective-permute-done.2.refs_3_), channel_id=1, source_target_pairs={{0,32},{32,64},{64,96},{96,128},{128,160},{160,192},{192,224},{224... | collective-permute-start | bytes 983048 | tf_op jit(solution)/shard_map/ppermute | solution.py:178
  51.0 9.6 %collective-permute-start.17 = (bf16[3,64,512]{2,1,0:T(8,128)(2,1)S(1)}, bf16[3,64,512]{2,1,0:T(8,128)(2,1)S(1)}, u32[]{:S(2)}, u32[]{:S(2)}) collective-permute-start(bf16[3,64,512]{2,1,0:T(8,128)(2,1)S(1)} %fit.3.refs_7_), channel_id=1, source_target_pairs={{0,24},{1,7},{2,26},{3,1},{4,28},{5,3},{6,30},{7,5},{8,0},{9,15},{... | collective-permute-start | bytes 589832 | tf_op jit(solution)/shard_map/ppermute | solution.py:298
  51.6 9.1 %collective-permute-start.19 = (bf16[3,64,512]{2,1,0:T(8,128)(2,1)S(1)}, bf16[3,64,512]{2,1,0:T(8,128)(2,1)S(1)}, u32[]{:S(2)}, u32[]{:S(2)}) collective-permute-start(bf16[3,64,512]{2,1,0:T(8,128)(2,1)S(1)} %fit.3.refs_7_), channel_id=1, source_target_pairs={{0,16},{1,5},{2,18},{3,7},{4,20},{5,1},{6,22},{7,3},{8,24},{9,13},... | collective-permute-start | bytes 589832 | tf_op jit(solution)/shard_map/ppermute | solution.py:298
  58.0 10.7 %collective-permute-start.18 = (bf16[5,64,512]{2,1,0:T(8,128)(2,1)S(1)}, bf16[5,64,512]{2,1,0:T(8,128)(2,1)S(1)}, u32[]{:S(2)}, u32[]{:S(2)}) collective-permute-start(bf16[5,64,512]{2,1,0:T(8,128)(2,1)S(1)} %fit.2.refs_6_), channel_id=1, source_target_pairs={{0,16},{1,5},{2,18},{3,7},{4,20},{5,1},{6,22},{7,3},{8,24},{9,13},... | collective-permute-start | bytes 983048 | tf_op jit(solution)/shard_map/ppermute | solution.py:298
  70.5 10.6 %collective-permute-start.20 = (bf16[8,64,512]{2,1,0:T(8,128)(2,1)}, bf16[8,64,512]{2,1,0:T(8,128)(2,1)S(1)}, u32[]{:S(2)}, u32[]{:S(2)}) collective-permute-start(bf16[8,64,512]{2,1,0:T(8,128)(2,1)} %get-tuple-element.31), channel_id=1, source_target_pairs={{0,2},{1,9},{2,4},{3,11},{4,6},{5,13},{6,0},{7,15},{8,10},{9,17},{... | collective-permute-start | bytes 1572872 | tf_op jit(solution)/shard_map/ppermute | solution.py:318
  72.1 9.4 %collective-permute-start.21 = (bf16[8,64,512]{2,1,0:T(8,128)(2,1)}, bf16[8,64,512]{2,1,0:T(8,128)(2,1)S(1)}, u32[]{:S(2)}, u32[]{:S(2)}) collective-permute-start(bf16[8,64,512]{2,1,0:T(8,128)(2,1)} %get-tuple-element.32), channel_id=1, source_target_pairs={{0,6},{1,25},{2,0},{3,27},{4,2},{5,29},{6,4},{7,31},{8,14},{9,1},{... | collective-permute-start | bytes 1572872 | tf_op jit(solution)/shard_map/ppermute | solution.py:318
  74.5 10.0 %collective-permute-start.22 = (bf16[8,64,512]{2,1,0:T(8,128)(2,1)S(1)}, bf16[8,64,512]{2,1,0:T(8,128)(2,1)S(1)}, u32[]{:S(2)}, u32[]{:S(2)}) collective-permute-start(bf16[8,64,512]{2,1,0:T(8,128)(2,1)S(1)} %get-tuple-element.33), channel_id=1, source_target_pairs={{0,3},{1,8},{2,5},{3,10},{4,7},{5,12},{6,1},{7,14},{8,11},{9,16},{... | collective-permute-start | bytes 1572872 | tf_op jit(solution)/shard_map/ppermute | solution.py:318
  74.6 11.7 %collective-permute-start.23 = (bf16[8,64,512]{2,1,0:T(8,128)(2,1)S(1)}, bf16[8,64,512]{2,1,0:T(8,128)(2,1)S(1)}, u32[]{:S(2)}, u32[]{:S(2)}) collective-permute-start(bf16[8,64,512]{2,1,0:T(8,128)(2,1)S(1)} %get-tuple-element.34), channel_id=1, source_target_pairs={{0,7},{1,24},{2,1},{3,26},{4,3},{5,28},{6,5},{7,30},{8,15},{9,0},{... | collective-permute-start | bytes 1572872 | tf_op jit(solution)/shard_map/ppermute | solution.py:318
  76.4 17.2 %collective-permute-start.24 = (bf16[8,64,512]{2,1,0:T(8,128)(2,1)S(1)}, bf16[8,64,512]{2,1,0:T(8,128)(2,1)S(1)}, u32[]{:S(2)}, u32[]{:S(2)}) collective-permute-start(bf16[8,64,512]{2,1,0:T(8,128)(2,1)S(1)} %get-tuple-element.35), channel_id=1, source_target_pairs={{0,4},{1,17},{2,6},{3,19},{4,0},{5,21},{6,2},{7,23},{8,12},{9,25},... | collective-permute-start | bytes 1572872 | tf_op jit(solution)/shard_map/ppermute | solution.py:318
  81.1 14.8 %collective-permute-start.25 = (bf16[8,64,512]{2,1,0:T(8,128)(2,1)S(1)}, bf16[8,64,512]{2,1,0:T(8,128)(2,1)S(1)}, u32[]{:S(2)}, u32[]{:S(2)}) collective-permute-start(bf16[8,64,512]{2,1,0:T(8,128)(2,1)S(1)} %get-tuple-element.36), channel_id=1, source_target_pairs={{0,5},{1,16},{2,7},{3,18},{4,1},{5,20},{6,3},{7,22},{8,13},{9,24},... | collective-permute-start | bytes 1572872 | tf_op jit(solution)/shard_map/ppermute | solution.py:318
  81.5 14.4 %collective-permute-start.26 = (bf16[8,64,512]{2,1,0:T(8,128)(2,1)S(1)}, bf16[8,64,512]{2,1,0:T(8,128)(2,1)S(1)}, u32[]{:S(2)}, u32[]{:S(2)}) collective-permute-start(bf16[8,64,512]{2,1,0:T(8,128)(2,1)S(1)} %get-tuple-element.37), channel_id=1, source_target_pairs={{0,1},{1,0},{2,3},{3,2},{4,5},{5,4},{6,7},{7,6},{8,9},{9,8},{10,11... | collective-permute-start | bytes 1572872 | tf_op jit(solution)/shard_map/ppermute | solution.py:318
  105.1 10.3 %collective-permute-start.28 = (f32[5,32,256]{2,1,0:T(8,128)S(1)}, f32[5,32,256]{2,1,0:T(8,128)S(1)}, u32[]{:S(2)}, u32[]{:S(2)}) collective-permute-start(f32[5,32,256]{2,1,0:T(8,128)S(1)} %add_term.10), channel_id=1, source_target_pairs={{0,32},{32,64},{64,96},{96,128},{128,160},{160,192},{192,224},{224... | collective-permute-start | bytes 491528 | tf_op jit(solution)/shard_map/ppermute | solution.py:178
  105.9 9.7 %collective-permute-start.38 = (f32[5,32,256]{2,1,0:T(8,128)S(1)}, f32[5,32,256]{2,1,0:T(8,128)S(1)}, u32[]{:S(2)}, u32[]{:S(2)}) collective-permute-start(f32[5,32,256]{2,1,0:T(8,128)S(1)} %add_term.17), channel_id=1, source_target_pairs={{0,224},{32,0},{64,32},{96,64},{128,96},{160,128},{192,160},{224,1... | collective-permute-start | bytes 491528 | tf_op jit(solution)/shard_map/ppermute | solution.py:178
  123.9 9.2 %collective-permute-start.30 = (f32[5,32,256]{2,1,0:T(8,128)S(1)}, f32[5,32,256]{2,1,0:T(8,128)S(1)}, u32[]{:S(2)}, u32[]{:S(2)}) collective-permute-start(f32[5,32,256]{2,1,0:T(8,128)S(1)} %add_term.12), channel_id=1, source_target_pairs={{0,32},{32,64},{64,96},{96,128},{128,160},{160,192},{192,224},{224... | collective-permute-start | bytes 491528 | tf_op jit(solution)/shard_map/ppermute | solution.py:178
  (20 other events, 156.9 us)
